TPU v7x, 128 devices: a whole 4x4x4 slice. The times are simulated.
128 devices in a mesh: row: 8 (over z, x_lo), col: 16 (over y, x_hi, core).
Axes of the slice: x: 4 (x_hi: 2, x_lo: 2; x = x_hi * 2 + x_lo), y: 4, z: 4, core: 2. Of those that a mesh axis runs over, the one named last changes fastest.
Arguments:
- edge_left: bfloat16 [8, 2048, 4096], P(None, 'row', 'col'), may hold values from -6 to 6
- site_left: bfloat16 [8, 4096, 2048], P(None, 'col'), may hold values from -0.09375 to 0.09375
- edge_right: bfloat16 [8, 2048, 4096], P(None, None, 'row'), may hold values from -6 to 6
- site_right: bfloat16 [8, 4096, 2048], P(None, 'row', 'col'), may hold values from -0.09375 to 0.09375
- sector_sizes: int32 [8], replicated, may hold values from 1 to 2048, 9216 in all
Outputs:
- half_system: bfloat16 [8, 2048, 2048], P(None, 'row', 'col')
Inputs may be any that keep to these rules, and one draw needn't show every extreme that they name: `sector_sizes`: every sector size is at least 1, one sector has exactly 2048, and the sizes sum to 9216.
All inputs are finite; a program needn't handle non-finite values.
Results may differ from a plain program's by a relative error of at most 0.025.
Values may be sent and summed in bfloat16 or wider, within the bound.
No kernel may reach another device: no remote copies, remote signals or barrier semaphores. Data moves between devices by JAX's collectives and lax.ppermute only.
A program may use at most 128 MiB of HBM per device.

v0:
```python
import jax
import jax.numpy as jnp
from jax import lax
from jax.sharding import PartitionSpec as P


def sector_live(sector_sizes, row_first, row_count, col_first, col_count):
    row_index = row_first + jnp.arange(row_count, dtype=jnp.int32)
    col_index = col_first + jnp.arange(col_count, dtype=jnp.int32)
    limits = sector_sizes[:, None, None]
    return (row_index[None, :, None] < limits) & (col_index[None, None, :] < limits)


def on_device(edge_left, site_left, edge_right, site_right, sector_sizes):
    row_devices = lax.axis_size("row")
    col_devices = lax.axis_size("col")
    order = site_left.shape[2]
    row_block = order // row_devices
    col_block = order // col_devices
    row_first = lax.axis_index("row") * row_block
    col_first = lax.axis_index("col") * col_block
    scale = order ** (-0.5)
    left_terms = jnp.einsum(
        "sik,skj->sij", edge_left, site_left, preferred_element_type=jnp.float32
    ).astype(jnp.bfloat16)
    right_terms = jnp.einsum(
        "sik,skj->sij", edge_right, site_right, preferred_element_type=jnp.float32
    ).astype(jnp.bfloat16)
    left_tile = lax.psum_scatter(left_terms, "col", scatter_dimension=2, tiled=True).astype(
        jnp.float32
    )
    left_live = sector_live(sector_sizes, row_first, row_block, col_first, col_block)
    left_tile = jnp.where(left_live, left_tile, jnp.float32(0.0)).astype(jnp.bfloat16)
    left_whole = lax.all_gather(left_tile, "col", axis=2, tiled=True)
    right_tile = lax.psum_scatter(right_terms, "row", scatter_dimension=1, tiled=True).astype(
        jnp.float32
    )
    right_live = sector_live(sector_sizes, row_first, row_block, col_first, col_block)
    right_tile = jnp.where(right_live, right_tile, jnp.float32(0.0)).astype(jnp.bfloat16)
    product = jnp.einsum(
        "sik,skj->sij",
        left_whole,
        lax.all_gather(right_tile, "row", axis=1, tiled=True),
        preferred_element_type=jnp.float32,
    )
    return (product * jnp.float32(scale)).astype(jnp.bfloat16)


def solution(mesh):
    placed = (
        P(None, "row", "col"),
        P(None, "col", None),
        P(None, None, "row"),
        P(None, "row", "col"),
        P(),
    )
    return jax.shard_map(
        on_device, mesh=mesh, in_specs=placed, out_specs=P(None, "row", "col"), check_vma=False
    )
```

profile of v0, /device:TPU:1, one launch (start us, length us, event | category | flops | bytes accessed | tf_op | source)
XLA Modules:
  0.0 424.9 jit_solution(12987263522181841127)
XLA Ops:
  6.5 0.0 copy-start
  6.5 0.0 reduce-scatter.7.cloned.1.call-start
  6.5 1.2 copy-done
  7.8 9.0 %convolution_convert_fusion = bf16[8,256,2048]{2,1,0:T(8,128)(2,1)} fusion(bf16[8,256,256]{2,1,0:T(8,128)(2,1)S(1)} %copy-done, bf16[8,256,2048]{2,1,0:T(8,128)(2,1)} %param.6), kind=kOutput, calls=%fused_computation | convolution fusion | flops 2151677952 | bytes 17825792 | tf_op jit(solution)/shard_map/sik,skj->sij/dot_general | solution.py:23
  16.7 12.7 %copy.6 = bf16[8,256,2048]{1,0,2:T(8,128)(2,1)} copy(bf16[8,256,2048]{2,1,0:T(8,128)(2,1)} %convolution_convert_fusion) | data formatting | bytes 16777216
  29.4 10.3 %copy.8 = bf16[256,8,8,256]{3,1,2,0:T(8,128)(2,1)} copy(bf16[256,8,8,256]{3,2,1,0:T(8,128)(2,1)} %bitcast.14) | data formatting | bytes 16777216
  39.6 0.0 copy-start.3
  39.7 0.0 reduce-scatter.7.cloned.1.call-update
  39.7 0.0 copy-start.2
  39.7 0.0 reduce-scatter.5.cloned.1.call-start
  39.7 1.1 copy-done.3
  40.9 12.3 %convolution_convert_fusion.1 = bf16[8,2048,128]{2,1,0:T(8,128)(2,1)} fusion(bf16[8,2048,512]{2,1,0:T(8,128)(2,1)} %param.7, bf16[8,512,128]{2,1,0:T(8,128)(2,1)S(1)} %copy-done.3), kind=kOutput, calls=%fused_computation.1 | convolution fusion | flops 2149580800 | bytes 22020096 | tf_op jit(solution)/shard_map/sik,skj->sij/dot_general | solution.py:26
  53.1 0.0 reduce-scatter.5.cloned.1.call-update
  53.2 0.0 all-gather.5.cloned.1.call-start
  53.2 0.0 copy-done.2
  53.2 0.1 broadcast_compare_fusion.1
  53.3 0.1 broadcast_compare_fusion
  53.4 90.9 %reduce-scatter.7.cloned.1.call-done = bf16[128,2048]{1,0:T(8,128)(2,1)} async-done(((bf16[2048,2048]{1,0:T(8,128)(2,1)}), bf16[128,2048]{1,0:T(8,128)(2,1)}) %reduce-scatter.7.cloned.1.call-update) | async-done | bytes 524304
  144.3 1.1 copy.9
  145.4 0.4 copy.7
  145.9 92.0 %reduce-scatter.5.cloned.1.call-done = bf16[8,256,128]{2,1,0:T(8,128)(2,1)} async-done(((bf16[8,2048,128]{2,1,0:T(8,128)(2,1)}), bf16[8,256,128]{2,1,0:T(8,128)(2,1)}) %reduce-scatter.5.cloned.1.call-update) | async-done | bytes 524304 | tf_op jit(solution)/shard_map/reduce_scatter | solution.py:35
  237.9 2.2 fusion.2
  240.0 0.0 all-gather.5.cloned.1.call-update
  240.1 0.2 all-gather.3.cloned.1.call-start
  240.3 0.3 all-gather.3.cloned.1.call-update
  240.7 0.0 copy-start.1
  240.7 90.3 %all-gather.5.cloned.1.call-done = bf16[8,2048,128]{2,1,0:T(8,128)(2,1)} async-done(((bf16[8,256,128]{2,1,0:T(8,128)(2,1)}), bf16[8,2048,128]{2,1,0:T(8,128)(2,1)}) %all-gather.5.cloned.1.call-update) | async-done | bytes 4194320 | tf_op jit(solution)/shard_map/all_gather | solution.py:43
  330.9 79.7 %all-gather.3.cloned.1.call-done = bf16[8,256,2048]{2,1,0:T(8,128)(2,1)} async-done(((bf16[8,256,128]{2,1,0:T(8,128)(2,1)}), bf16[8,256,2048]{2,1,0:T(8,128)(2,1)}) %all-gather.3.cloned.1.call-update) | async-done | bytes 8388624 | tf_op jit(solution)/shard_map/all_gather | solution.py:34
  410.6 7.7 %fusion = bf16[8,256,128]{2,1,0:T(8,128)(2,1)} fusion(bf16[8,256,2048]{2,1,0:T(8,128)(2,1)} %all-gather.3.cloned.1.call-done, bf16[8,2048,128]{2,1,0:T(8,128)(2,1)} %all-gather.5.cloned.1.call-done), kind=kOutput, calls=%fused_computation.5 | convolution fusion | flops 1074266112 | bytes 13107200 | tf_op jit(solution)/shard_map/sik,skj->sij/dot_general | solution.py:40
  418.3 0.0 copy-done.1
  (2 shorter events, 0.0 us)
Async XLA Ops:
  6.5 1.2 copy-start
  6.5 137.8 %reduce-scatter.7.cloned.1.call-start = ((), (), s32[]{:S(2)}) async-start(), calls=%async_computation.5 | async-start | bytes 8912896
  39.6 1.2 copy-start.3
  39.7 13.6 %copy-start.2 = (s32[8]{0:T(128)S(1)}, s32[8]{0:T(128)}, u32[]{:S(2)}) copy-start(s32[8]{0:T(128)} %param.9) | copy-start | bytes 100
  39.7 198.2 %reduce-scatter.5.cloned.1.call-start = ((), (), s32[]{:S(2)}) async-start(), calls=%async_computation.3 | async-start | bytes 4718592 | tf_op jit(solution)/shard_map/reduce_scatter | solution.py:35
  53.2 277.8 %all-gather.5.cloned.1.call-start = ((), (), s32[]{:S(2)}) async-start(), calls=%async_computation.4 | async-start | bytes 4718592 | tf_op jit(solution)/shard_map/all_gather | solution.py:43
  240.1 170.6 %all-gather.3.cloned.1.call-start = ((), (), s32[]{:S(2)}) async-start(), calls=%async_computation.2 | async-start | bytes 8912896 | tf_op jit(solution)/shard_map/all_gather | solution.py:34
  240.7 177.7 %copy-start.1 = (bf16[8,256,256]{2,1,0:T(8,128)(2,1)S(1)}, bf16[8,256,256]{2,1,0:T(8,128)(2,1)}, u32[]{:S(2)}) copy-start(bf16[8,256,256]{2,1,0:T(8,128)(2,1)} %param.5) | copy-start | bytes 3145732
Sparse Core Ops, SparseCore 0:
  39.8 104.4 reduce-scatter.6
  146.7 91.1 reduce-scatter.4
  240.2 90.6 all-gather.4
  333.1 77.4 all-gather.2
where the time goes:
time: 426 us; the launch traced here: 425 us
  waiting for transfers between devices  353 us (83%)
  matrix products  28.9 us (7%)
  local copies, waits for them, and re-layouts  26.9 us (6%)
  between operations  13.2 us (3%)
    reduce_scatter x1, waiting for transfers between devices, on_device(): lax.psum_scatter(right_terms, 'row', scatter_dimension=1, tiled=True)  92 us
    unnamed x5, waiting for transfers between devices  91.3 us
    all_gather x1, waiting for transfers between devices, on_device(): lax.all_gather(right_tile, 'row', axis=1, tiled=True)  90.3 us
    all_gather x1, waiting for transfers between devices, on_device(): left_whole = lax.all_gather(left_tile, 'col', axis=2, tiled=True)  79.7 us
    unnamed x12, local copies, waits for them, and re-layouts  26.9 us
    dot_general x1, matrix products, on_device(): jnp.einsum('sik,skj->sij', edge_right, site_right, preferred_element_type...  12.3 us
    dot_general x1, matrix products, on_device(): jnp.einsum('sik,skj->sij', edge_left, site_left, preferred_element_type=j...  8.95 us
  transfers between devices with their start and end apart: 4, of which 4 were waited for; matrix products, arithmetic and copies ran while one was open for 3% of the time, Pallas kernels for 0%

commit v1 on v0

v1 whole, which is shorter than its diff:
```python
import jax
import jax.numpy as jnp
from jax import lax
from jax.experimental import pallas as pl
from jax.experimental.pallas import tpu as pltpu
from jax.sharding import Mesh
from jax.sharding import PartitionSpec as P

WIDTH = 128
SLOTS = 80
HALF = SLOTS // 2
Z, XL, Y, XH, CORE = 4, 2, 4, 2, 2
ONE = HALF // (Y * XH)
TWO = SLOTS // (Z * XL)


def slot_table(sector_sizes):
    sectors = sector_sizes.shape[0]
    blocks = (sector_sizes + (WIDTH - 1)) // WIDTH
    line = jnp.arange(sectors, dtype=jnp.int32)
    ends = jnp.sum(jnp.where(line[None, :] <= line[:, None], blocks[None, :], 0), axis=1)
    firsts = ends - blocks
    slot = jnp.arange(SLOTS, dtype=jnp.int32)
    past = slot[:, None] >= ends[None, :]
    inside = (slot[:, None] >= firsts[None, :]) & ~past
    sector = jnp.minimum(jnp.sum(past.astype(jnp.int32), axis=1), sectors - 1)
    block = jnp.sum(jnp.where(inside, slot[:, None] - firsts[None, :], 0), axis=1)
    limit = jnp.sum(jnp.where(inside, sector_sizes[None, :], 0), axis=1)
    return firsts, ends, sector, block, limit


def masked(values, row_limit, col_limit):
    rows = lax.broadcasted_iota(jnp.int32, values.shape, 0)
    cols = lax.broadcasted_iota(jnp.int32, values.shape, 1)
    return jnp.where((rows < row_limit) & (cols < col_limit), values, jnp.float32(0.0))


def left_kernel(add, where_ref, sector_ref, block_ref, limit_ref, edge_ref, site_ref, *rest):
    if add:
        other_ref, out_ref, site_buf, sems = rest
    else:
        out_ref, site_buf, sems = rest
    first_slot = where_ref[0]
    row_first = where_ref[1]

    def fetch(q):
        p = first_slot + q
        return pltpu.make_async_copy(
            site_ref.at[sector_ref[p], :, pl.ds(pl.multiple_of(block_ref[p] * WIDTH, WIDTH), WIDTH)],
            site_buf.at[q],
            sems.at[q],
        )

    @pl.loop(0, HALF)
    def _(q):
        fetch(q).start()

    @pl.loop(0, HALF // 4)
    def _(group):
        for k in range(4):
            fetch(group * 4 + k).wait()
        for k in range(4):
            q = group * 4 + k
            p = first_slot + q
            limit = limit_ref[p]
            term = jnp.dot(edge_ref[sector_ref[p]], site_buf[q], preferred_element_type=jnp.float32)
            if add:
                term = term + other_ref[q].astype(jnp.float32)
            out_ref[q] = masked(term, limit - row_first, limit - block_ref[p] * WIDTH).astype(jnp.bfloat16)


def left_terms(add, first_slot, row_first, table, edge, site, *other):
    rows, depth = edge.shape[1], edge.shape[2]
    vmem = pl.BlockSpec(memory_space=pltpu.VMEM)
    spec = pltpu.PrefetchScalarGridSpec(
        num_scalar_prefetch=4,
        grid=(1,),
        in_specs=[vmem, pl.BlockSpec(memory_space=pl.ANY)] + [vmem] * len(other),
        out_specs=vmem,
        scratch_shapes=[
            pltpu.VMEM((HALF, depth, WIDTH), jnp.bfloat16),
            pltpu.SemaphoreType.DMA((HALF,)),
        ],
    )
    return pl.pallas_call(
        lambda *refs: left_kernel(add, *refs),
        out_shape=jax.ShapeDtypeStruct((HALF, rows, WIDTH), jnp.bfloat16),
        grid_spec=spec,
        compiler_params=pltpu.CompilerParams(vmem_limit_bytes=32 * 2**20),
        cost_estimate=pl.CostEstimate(
            flops=2 * HALF * rows * depth * WIDTH, bytes_accessed=10 * 2**20, transcendentals=0
        ),
        name="left_add" if add else "left",
    )(jnp.stack([first_slot, row_first]).astype(jnp.int32), *table, edge, site, *other)


def right_kernel(where_ref, sector_ref, block_ref, limit_ref, edge_ref, site_ref, *rest):
    outs, (edge_buf, sems) = rest[:Z], rest[Z:]
    z = where_ref[0]
    x = where_ref[1]
    col_first = where_ref[2]
    per_z = XL * TWO

    def slot(step, q):
        return lax.rem(z + step, Z) * per_z + jnp.where(q < TWO, x * TWO + q, (1 - x) * TWO + q - TWO)

    def fetch(step, q):
        p = slot(step, q)
        at = step * per_z + q
        return pltpu.make_async_copy(
            edge_ref.at[sector_ref[p], pl.ds(pl.multiple_of(block_ref[p] * WIDTH, WIDTH), WIDTH), :],
            edge_buf.at[at],
            sems.at[at],
        )

    order = (2, 1, 3, 0)
    for step in order:

        @pl.loop(0, per_z)
        def _(q):
            fetch(step, q).start()

    for step in order:

        @pl.loop(0, per_z // 4)
        def _(group):
            for k in range(4):
                fetch(step, group * 4 + k).wait()
            for k in range(4):
                q = group * 4 + k
                p = slot(step, q)
                limit = limit_ref[p]
                term = jnp.dot(
                    edge_buf[step * per_z + q], site_ref[sector_ref[p]], preferred_element_type=jnp.float32
                )
                outs[step][q] = masked(term, limit - block_ref[p] * WIDTH, limit - col_first).astype(
                    jnp.bfloat16
                )


def right_terms(z, x, col_first, table, edge, site):
    depth, cols = site.shape[1], site.shape[2]
    vmem = pl.BlockSpec(memory_space=pltpu.VMEM)
    spec = pltpu.PrefetchScalarGridSpec(
        num_scalar_prefetch=4,
        grid=(1,),
        in_specs=[pl.BlockSpec(memory_space=pl.ANY), vmem],
        out_specs=[vmem] * Z,
        scratch_shapes=[
            pltpu.VMEM((SLOTS, WIDTH, depth), jnp.bfloat16),
            pltpu.SemaphoreType.DMA((SLOTS,)),
        ],
    )
    return pl.pallas_call(
        right_kernel,
        out_shape=[jax.ShapeDtypeStruct((XL * TWO, WIDTH, cols), jnp.bfloat16)] * Z,
        grid_spec=spec,
        compiler_params=pltpu.CompilerParams(vmem_limit_bytes=32 * 2**20),
        cost_estimate=pl.CostEstimate(
            flops=2 * SLOTS * WIDTH * depth * cols, bytes_accessed=16 * 2**20, transcendentals=0
        ),
        name="right",
    )(jnp.stack([z, x, col_first]).astype(jnp.int32), *table, edge, site)


def product_kernel(scale, where_ref, first_ref, end_ref, own_ref, other_ref, *rest):
    rights = rest[:Z]
    out_ref, one_buf, two_buf, sems = rest[Z:]
    core, z, x = where_ref[0], where_ref[1], where_ref[2]
    per_z = XL * TWO
    copies = [
        pltpu.make_async_copy(own_ref, one_buf.at[pl.ds(core * HALF, HALF)], sems.at[0]),
        pltpu.make_async_copy(other_ref, one_buf.at[pl.ds((1 - core) * HALF, HALF)], sems.at[1]),
    ]
    for step in range(Z):
        base = lax.rem(z + Z - step, Z) * per_z
        for k in range(XL):
            at = base + (x if k == 0 else 1 - x) * TWO
            copies.append(
                pltpu.make_async_copy(
                    rights[step].at[pl.ds(k * TWO, TWO)], two_buf.at[pl.ds(at, TWO)], sems.at[2 + step * XL + k]
                )
            )
    for copy in copies:
        copy.start()
    for copy in copies:
        copy.wait()

    @pl.loop(0, out_ref.shape[0])
    def _(s):
        def add(p, total):
            return total + jnp.dot(one_buf[p], two_buf[p], preferred_element_type=jnp.float32)

        total = lax.fori_loop(first_ref[s], end_ref[s], add, jnp.zeros(out_ref.shape[1:], jnp.float32))
        out_ref[s] = (total * jnp.float32(scale)).astype(jnp.bfloat16)


def product(scale, where, firsts, ends, own, other, rights):
    rows, cols, sectors = own.shape[1], rights[0].shape[2], firsts.shape[0]
    vmem = pl.BlockSpec(memory_space=pltpu.VMEM)
    anywhere = pl.BlockSpec(memory_space=pl.ANY)
    spec = pltpu.PrefetchScalarGridSpec(
        num_scalar_prefetch=3,
        grid=(1,),
        in_specs=[anywhere] * (2 + Z),
        out_specs=vmem,
        scratch_shapes=[
            pltpu.VMEM((SLOTS, rows, WIDTH), jnp.bfloat16),
            pltpu.VMEM((SLOTS, WIDTH, cols), jnp.bfloat16),
            pltpu.SemaphoreType.DMA((2 + Z * XL,)),
        ],
    )
    return pl.pallas_call(
        lambda *refs: product_kernel(scale, *refs),
        out_shape=jax.ShapeDtypeStruct((sectors, rows, cols), jnp.bfloat16),
        grid_spec=spec,
        compiler_params=pltpu.CompilerParams(vmem_limit_bytes=32 * 2**20),
        cost_estimate=pl.CostEstimate(
            flops=2 * SLOTS * rows * WIDTH * cols, bytes_accessed=9 * 2**20, transcendentals=0
        ),
        name="product",
    )(where, firsts, ends, own, other, *rights)


def shift(array, axis, size, step):
    return lax.ppermute(array, axis, [(i, (i + step) % size) for i in range(size)])


def on_device(edge_left, site_left, edge_right, site_right, sector_sizes):
    order = site_left.shape[2]
    rows, cols = edge_left.shape[1], site_right.shape[2]
    z, xl, y, xh, core = (lax.axis_index(a) for a in ("z", "xl", "y", "xh", "core"))
    row_first = (z * XL + xl) * rows
    col_first = ((y * XH + xh) * CORE + core) * cols
    firsts, ends, *table = slot_table(sector_sizes)
    f32 = lambda a: a.astype(jnp.float32)

    for_other = left_terms(False, (1 - core) * HALF, row_first, table, edge_left, site_left)
    from_other = shift(for_other, "core", CORE, 1)
    to = right_terms(z, xl, col_first, table, edge_right, site_right)
    came = [shift(to[step], "z", Z, step) for step in range(1, Z)]
    chip_sum = left_terms(True, core * HALF, row_first, table, edge_left, site_left, from_other)
    spread = lax.all_to_all(chip_sum, ("y", "xh"), 0, 0, tiled=True)

    right_sum = (f32(to[0]) + f32(came[0]) + f32(came[1]) + f32(came[2])).astype(jnp.bfloat16)
    right_x = shift(right_sum[TWO:], "xl", XL, 1)
    right_own = (f32(right_sum[:TWO]) + f32(right_x)).astype(jnp.bfloat16)
    left_own = jnp.sum(f32(spread.reshape((Y * XH, ONE, rows, WIDTH))), axis=0).astype(jnp.bfloat16)

    right_pair = jnp.concatenate([right_own, shift(right_own, "xl", XL, 1)], axis=0)
    rights = [right_pair] + [shift(right_pair, "z", Z, step) for step in range(1, Z)]
    copies = jnp.broadcast_to(left_own[None], (Y * XH, ONE, rows, WIDTH)).reshape(HALF, rows, WIDTH)
    left_half = lax.all_to_all(copies, ("y", "xh"), 0, 0, tiled=True)
    left_other = shift(left_half, "core", CORE, 1)
    where = jnp.stack([core, z, xl]).astype(jnp.int32)
    return product(order ** (-0.5), where, firsts, ends, left_half, left_other, rights)


def solution(mesh):
    split = Mesh(mesh.devices.reshape(Z, XL, Y, XH, CORE), ("z", "xl", "y", "xh", "core"))
    row, col = ("z", "xl"), ("y", "xh", "core")
    placed = (P(None, row, col), P(None, col, None), P(None, None, row), P(None, row, col), P())
    return jax.shard_map(
        on_device, mesh=split, in_specs=placed, out_specs=P(None, row, col), check_vma=False
    )
```

time: 426 us -> 208 us (0.49)
  waiting for transfers between devices: 353 us -> 73.1 us
  Pallas kernels: 0 us -> 51.4 us
  blocking collectives: 0 us -> 39.7 us
  matrix products: 28.9 us -> 0 us
  starting transfers between devices: 0.31 us -> 21.6 us
  between operations: 13.2 us -> 0.11 us
  local copies, waits for them, and re-layouts: 26.9 us -> 17.1 us
    all_gather x2 -> x0, waiting for transfers between devices: 170 us -> none  [the longest x1 90.3 us: on_device(): lax.all_gather(right_tile, 'row', axis=1, tiled=True)]
    reduce_scatter x1 -> x0, waiting for transfers between devices: 92 us -> none  [on_device(): lax.psum_scatter(right_terms, 'row', scatter_dimension=1, tiled=True)]
    unnamed x5 -> x0, waiting for transfers between devices: 91.3 us -> none
    ppermute x0 -> x10, waiting for transfers between devices: none -> 73.1 us  [shift(): lax.ppermute(array, axis, [(i, (i + step) % size) for i in range(size)])]
    pallas_call x0 -> x4, Pallas kernels: none -> 51.4 us  [the longest x1 23.4 us: right_terms(): pl.pallas_call(right_kernel, out_shape=[jax.ShapeDtypeStruct((XL * TWO, W...]
    all_to_all x0 -> x1, blocking collectives: none -> 39.7 us  [on_device(): spread = lax.all_to_all(chip_sum, ('y', 'xh'), 0, 0, tiled=True)]
    dot_general x3 -> x0, matrix products: 28.9 us -> none  [the longest x1 12.3 us: on_device(): jnp.einsum('sik,skj->sij', edge_right, site_right, preferred_element_type...]
    ppermute x0 -> x10, starting transfers between devices: none -> 18 us  [shift(): lax.ppermute(array, axis, [(i, (i + step) % size) for i in range(size)])]
  transfers between devices with their start and end apart: 4 -> 11, of which waited for: 4 -> 9; matrix products, arithmetic and copies ran while one was open for 3% -> 1% of each run, Pallas kernels for 0% -> 11%
where the time goes in v1:
time: 208 us
  waiting for transfers between devices  73.1 us (35%)
  Pallas kernels  51.4 us (25%)
  blocking collectives  39.7 us (19%)
  starting transfers between devices  21.6 us (10%)
  local copies, waits for them, and re-layouts  17.1 us (8%)
  other arithmetic  4.91 us (2%)
    ppermute x10, waiting for transfers between devices, shift(): lax.ppermute(array, axis, [(i, (i + step) % size) for i in range(size)])  73.1 us
    all_to_all x1, blocking collectives, on_device(): spread = lax.all_to_all(chip_sum, ('y', 'xh'), 0, 0, tiled=True)  39.7 us
    pallas_call x1, Pallas kernels, right_terms(): pl.pallas_call(right_kernel, out_shape=[jax.ShapeDtypeStruct((XL * TWO, W...  23.4 us
    ppermute x10, starting transfers between devices, shift(): lax.ppermute(array, axis, [(i, (i + step) % size) for i in range(size)])  18 us
    unnamed x12, local copies, waits for them, and re-layouts  15 us
    pallas_call x1, Pallas kernels, product(): pl.pallas_call(lambda *refs: product_kernel(scale, *refs), out_shape=jax....  14.5 us
    pallas_call x2, Pallas kernels, left_terms(): pl.pallas_call(lambda *refs: left_kernel(add, *refs), out_shape=jax.Shape...  13.5 us
  transfers between devices with their start and end apart: 11, of which 9 were waited for; matrix products, arithmetic and copies ran while one was open for 1% of the time, Pallas kernels for 11%

profile of v1, /device:TPU:1, one launch (start us, length us, event | category | flops | bytes accessed | tf_op | source)
XLA Modules:
  0.0 208.0 jit_solution(16537716420339217920)
XLA Ops:
  0.0 0.7 and_select_fusion
  0.8 0.7 fusion.2.refs_1_
  1.4 0.7 select_reduce_fusion
  2.3 3.4 %copy-done = bf16[8,256,2048]{2,1,0:T(8,128)(2,1)S(1)} copy-done((bf16[8,256,2048]{2,1,0:T(8,128)(2,1)S(1)}, bf16[8,256,2048]{2,1,0:T(8,128)(2,1)}, u32[]{:S(2)}) %copy-start) | copy-done | bytes 8388632
  5.7 1.2 copy-done.3
  6.9 6.7 %left.1 = bf16[40,256,128]{2,1,0:T(8,128)(2,1)} custom-call(s32[2]{0:T(128)S(1)} %pad_add_fusion.2.refs_0_, s32[80]{0:T(128)S(1)} %broadcast_minimum_fusion.refs_1_.sector_ref, s32[80]{0:T(128)S(1)} %get-tuple-element.14.refs_2_.block_ref, s32[80]{0:T(128)S(1)} %get-tuple-element.13.refs_3_.limit_ref, bf16[8,256,256]{2,1,0:T(8,128)(2,1)S(1)} %copy-done.3, ...), custom_call_target="tpu_custom_call" | custom-call | flops 671088640 | bytes 10485760 | tf_op jit(solution)/shard_map/left/pallas_call | solution.py:85
  13.6 1.5 collective-permute-start
  15.2 4.8 %collective-permute-done.refs_6_ = bf16[40,256,128]{2,1,0:T(8,128)(2,1)} collective-permute-done((bf16[40,256,128]{2,1,0:T(8,128)(2,1)}, bf16[40,256,128]{2,1,0:T(8,128)(2,1)}, u32[]{:S(2)}, u32[]{:S(2)}) %collective-permute-start) | collective-permute-done | bytes 2621472 | tf_op jit(solution)/shard_map/ppermute | solution.py:226
  20.0 3.4 %copy-done.1 = bf16[8,256,2048]{2,1,0:T(8,128)(2,1)S(1)} copy-done((bf16[8,256,2048]{2,1,0:T(8,128)(2,1)S(1)}, bf16[8,256,2048]{2,1,0:T(8,128)(2,1)}, u32[]{:S(2)}) %copy-start.1) | copy-done | bytes 8388632
  23.3 6.8 %left_add.1 = bf16[40,256,128]{2,1,0:T(8,128)(2,1)S(1)} custom-call(s32[2]{0:T(128)S(1)} %pad_add_fusion.1.refs_0_, s32[80]{0:T(128)S(1)} %broadcast_minimum_fusion.refs_1_.sector_ref, s32[80]{0:T(128)S(1)} %get-tuple-element.14.refs_2_.block_ref, s32[80]{0:T(128)S(1)} %get-tuple-element.13.refs_3_.limit_ref, bf16[8,256,256]{2,1,0:T(8,128)(2,1)S(1)} %copy-done.4, ...), custom_call_target="tpu_custom_call" | custom-call | flops 671088640 | bytes 10485760 | tf_op jit(solution)/shard_map/left_add/pallas_call | solution.py:85
  30.2 39.7 %all_to_all.10 = bf16[40,256,128]{2,1,0:T(8,128)(2,1)S(1)} all-to-all(bf16[40,256,128]{2,1,0:T(8,128)(2,1)S(1)} %left_add.1), channel_id=1, replica_groups=mesh['z'=4,'xl'=2,'y'=4,'xh'=2,'core'=2] {'y','xh'}, dimensions={0} | all-to-all | bytes 5242880 | tf_op jit(solution)/shard_map/all_to_all | solution.py:243
  70.3 2.1 %broadcast_in_dim.46 = bf16[8,5,256,128]{3,2,1,0:T(8,128)(2,1)} broadcast(bf16[5,256,128]{2,1,0:T(8,128)(2,1)S(1)} %reduce_sum.52), dimensions={1,2,3} | broadcast | bytes 2949120 | tf_op jit(solution)/shard_map/broadcast_in_dim | solution.py:252
  72.5 3.6 %all-to-all-start.1 = ((bf16[40,256,128]{2,1,0:T(8,128)(2,1)}), bf16[40,256,128]{2,1,0:T(8,128)(2,1)S(1)}, u32[]{:S(2)}, u32[]{:S(2)}) async-start(bf16[40,256,128]{2,1,0:T(8,128)(2,1)} %bitcast.9), calls=%async_computation.1 | async-start | bytes 5242880 | tf_op jit(solution)/shard_map/all_to_all | solution.py:253
  76.2 5.8 %copy-done.2 = bf16[8,2048,512]{2,1,0:T(8,128)(2,1)S(1)} copy-done((bf16[8,2048,512]{2,1,0:T(8,128)(2,1)S(1)}, bf16[8,2048,512]{2,1,0:T(8,128)(2,1)}, u32[]{:S(2)}) %copy-start.2) | copy-done | bytes 16777240
  82.0 1.2 copy-done.5
  83.2 23.4 %right.1 = (bf16[20,128,128]{2,1,0:T(8,128)(2,1)S(1)}, bf16[20,128,128]{2,1,0:T(8,128)(2,1)}, bf16[20,128,128]{2,1,0:T(8,128)(2,1)}, bf16[20,128,128]{2,1,0:T(8,128)(2,1)}) custom-call(s32[3]{0:T(128)S(1)} %pad_add_fusion.3.where_ref, s32[80]{0:T(128)S(1)} %broadcast_minimum_fusion.refs_1_.sector_ref, s32[80]{0:T(128)S(1)} %get-tuple-element.14.refs_2_.block_ref, ...), custom_call_target="tpu_custom_call" | custom-call | flops 1342177280 | bytes 16777216 | tf_op jit(solution)/shard_map/right/pallas_call | solution.py:154
  106.6 1.7 collective-permute-start.2
  108.3 3.3 %collective-permute-start.3 = (bf16[20,128,128]{2,1,0:T(8,128)(2,1)}, bf16[20,128,128]{2,1,0:T(8,128)(2,1)}, u32[]{:S(2)}, u32[]{:S(2)}) collective-permute-start(bf16[20,128,128]{2,1,0:T(8,128)(2,1)} %get-tuple-element.11), channel_id=1, source_target_pairs={{0,64},{32,96},{64,0},{96,32},{1,65},{33,97},{65,1},{97,33},{2,66}... | collective-permute-start | bytes 1966088 | tf_op jit(solution)/shard_map/ppermute | solution.py:226
  111.6 0.7 collective-permute-start.4
  112.3 2.7 %collective-permute-start.1 = (bf16[40,256,128]{2,1,0:T(8,128)(2,1)S(1)}, bf16[40,256,128]{2,1,0:T(8,128)(2,1)S(1)}, u32[]{:S(2)}, u32[]{:S(2)}) collective-permute-start(bf16[40,256,128]{2,1,0:T(8,128)(2,1)S(1)} %all-to-all-done.1.refs_3_), channel_id=1, source_target_pairs={{0,1},{1,0},{2,3},{3,2},{4,5},{5,4},{6,7},{7,6},{8,9},{9,8},{10,11... | collective-permute-start | bytes 7864328 | tf_op jit(solution)/shard_map/ppermute | solution.py:226
  115.0 9.0 %collective-permute-done.2 = bf16[20,128,128]{2,1,0:T(8,128)(2,1)} collective-permute-done((bf16[20,128,128]{2,1,0:T(8,128)(2,1)}, bf16[20,128,128]{2,1,0:T(8,128)(2,1)}, u32[]{:S(2)}, u32[]{:S(2)}) %collective-permute-start.2) | collective-permute-done | bytes 655392 | tf_op jit(solution)/shard_map/ppermute | solution.py:226
  124.0 14.9 %collective-permute-done.3 = bf16[20,128,128]{2,1,0:T(8,128)(2,1)} collective-permute-done((bf16[20,128,128]{2,1,0:T(8,128)(2,1)}, bf16[20,128,128]{2,1,0:T(8,128)(2,1)}, u32[]{:S(2)}, u32[]{:S(2)}) %collective-permute-start.3) | collective-permute-done | bytes 655392 | tf_op jit(solution)/shard_map/ppermute | solution.py:226
  138.9 0.7 collective-permute-done.4
  139.6 1.8 add_convert_fusion
  141.9 6.9 %collective-permute-done.5 = bf16[10,128,128]{2,1,0:T(8,128)(2,1)S(1)} collective-permute-done((bf16[10,128,128]{2,1,0:T(8,128)(2,1)S(1)}, bf16[10,128,128]{2,1,0:T(8,128)(2,1)S(1)}, u32[]{:S(2)}, u32[]{:S(2)}) %collective-permute-start.5) | collective-permute-done | bytes 327712 | tf_op jit(solution)/shard_map/ppermute | solution.py:226
  149.2 6.0 %collective-permute-done.6 = bf16[10,128,128]{2,1,0:T(8,128)(2,1)S(1)} collective-permute-done((bf16[10,128,128]{2,1,0:T(8,128)(2,1)S(1)}, bf16[10,128,128]{2,1,0:T(8,128)(2,1)S(1)}, u32[]{:S(2)}, u32[]{:S(2)}) %collective-permute-start.6) | collective-permute-done | bytes 327712 | tf_op jit(solution)/shard_map/ppermute | solution.py:226
  155.3 6.7 %collective-permute-start.9 = (bf16[20,128,128]{2,1,0:T(8,128)(2,1)S(1)}, bf16[20,128,128]{2,1,0:T(8,128)(2,1)S(1)}, u32[]{:S(2)}, u32[]{:S(2)}) collective-permute-start(bf16[20,128,128]{2,1,0:T(8,128)(2,1)S(1)} %pad_maximum_fusion.refs_5_), channel_id=1, source_target_pairs={{0,96},{32,0},{64,32},{96,64},{1,97},{33,1},{65,33},{97,65},{2,98}... | collective-permute-start | bytes 1966088 | tf_op jit(solution)/shard_map/ppermute | solution.py:226
  162.0 0.7 collective-permute-start.7
  162.7 13.2 %collective-permute-done.9.refs_8_ = bf16[20,128,128]{2,1,0:T(8,128)(2,1)S(1)} collective-permute-done((bf16[20,128,128]{2,1,0:T(8,128)(2,1)S(1)}, bf16[20,128,128]{2,1,0:T(8,128)(2,1)S(1)}, u32[]{:S(2)}, u32[]{:S(2)}) %collective-permute-start.9) | collective-permute-done | bytes 655392 | tf_op jit(solution)/shard_map/ppermute | solution.py:226
  176.0 1.3 collective-permute-done.8.refs_7_
  177.2 16.3 %collective-permute-done.7.refs_6_ = bf16[20,128,128]{2,1,0:T(8,128)(2,1)S(1)} collective-permute-done((bf16[20,128,128]{2,1,0:T(8,128)(2,1)S(1)}, bf16[20,128,128]{2,1,0:T(8,128)(2,1)S(1)}, u32[]{:S(2)}, u32[]{:S(2)}) %collective-permute-start.7) | collective-permute-done | bytes 655392 | tf_op jit(solution)/shard_map/ppermute | solution.py:226
  193.5 14.5 %product.1 = bf16[8,256,128]{2,1,0:T(8,128)(2,1)} custom-call(s32[3]{0:T(128)S(1)} %pad_add_fusion.refs_0_, s32[8]{0:T(128)S(1)} %fusion.2.refs_1_, s32[8]{0:T(128)S(1)} %select_reduce_fusion.2.refs_2_, bf16[40,256,128]{2,1,0:T(8,128)(2,1)S(1)} %all-to-all-done.1.refs_3_, bf16[40,256,128]{2,1,0:T(8,128)(2,1)S(1)} %collective-permute-done.1.refs_4_, ...), custom_call_target="tpu_custom_call" | custom-call | flops 671088640 | bytes 9437184 | tf_op jit(solution)/shard_map/product/pallas_call | solution.py:213
  (22 shorter events, 1.8 us)
Async XLA Ops:
  2.3 3.4 %copy-start = (bf16[8,256,2048]{2,1,0:T(8,128)(2,1)S(1)}, bf16[8,256,2048]{2,1,0:T(8,128)(2,1)}, u32[]{:S(2)}) copy-start(bf16[8,256,2048]{2,1,0:T(8,128)(2,1)} %refs_5_.3) | copy-start | bytes 25165828
  5.7 1.2 copy-start.3
  6.9 13.1 %copy-start.4 = (bf16[8,256,256]{2,1,0:T(8,128)(2,1)S(1)}, bf16[8,256,256]{2,1,0:T(8,128)(2,1)}, u32[]{:S(2)}) copy-start(bf16[8,256,256]{2,1,0:T(8,128)(2,1)} %refs_4_.3) | copy-start | bytes 3145732
  13.6 6.4 %collective-permute-start = (bf16[40,256,128]{2,1,0:T(8,128)(2,1)}, bf16[40,256,128]{2,1,0:T(8,128)(2,1)}, u32[]{:S(2)}, u32[]{:S(2)}) collective-permute-start(bf16[40,256,128]{2,1,0:T(8,128)(2,1)} %left.1), channel_id=1, source_target_pairs={{0,1},{1,0},{2,3},{3,2},{4,5},{5,4},{6,7},{7,6},{8,9},{9,8},{10,11... | collective-permute-start | bytes 7864328 | tf_op jit(solution)/shard_map/ppermute | solution.py:226
  20.0 3.4 %copy-start.1 = (bf16[8,256,2048]{2,1,0:T(8,128)(2,1)S(1)}, bf16[8,256,2048]{2,1,0:T(8,128)(2,1)}, u32[]{:S(2)}) copy-start(bf16[8,256,2048]{2,1,0:T(8,128)(2,1)} %refs_5_.3) | copy-start | bytes 25165828
  72.5 39.9 %all-to-all-start.1 = ((bf16[40,256,128]{2,1,0:T(8,128)(2,1)}), bf16[40,256,128]{2,1,0:T(8,128)(2,1)S(1)}, u32[]{:S(2)}, u32[]{:S(2)}) async-start(bf16[40,256,128]{2,1,0:T(8,128)(2,1)} %bitcast.9), calls=%async_computation.1 | async-start | bytes 5242880 | tf_op jit(solution)/shard_map/all_to_all | solution.py:253
  76.2 5.8 %copy-start.2 = (bf16[8,2048,512]{2,1,0:T(8,128)(2,1)S(1)}, bf16[8,2048,512]{2,1,0:T(8,128)(2,1)}, u32[]{:S(2)}) copy-start(bf16[8,2048,512]{2,1,0:T(8,128)(2,1)} %edge_ref.1) | copy-start | bytes 50331652
  82.0 1.2 copy-start.5
  106.6 17.4 %collective-permute-start.2 = (bf16[20,128,128]{2,1,0:T(8,128)(2,1)}, bf16[20,128,128]{2,1,0:T(8,128)(2,1)}, u32[]{:S(2)}, u32[]{:S(2)}) collective-permute-start(bf16[20,128,128]{2,1,0:T(8,128)(2,1)} %get-tuple-element.10), channel_id=1, source_target_pairs={{0,32},{32,64},{64,96},{96,0},{1,33},{33,65},{65,97},{97,1},{2,34}... | collective-permute-start | bytes 1966088 | tf_op jit(solution)/shard_map/ppermute | solution.py:226
  108.3 30.6 %collective-permute-start.3 = (bf16[20,128,128]{2,1,0:T(8,128)(2,1)}, bf16[20,128,128]{2,1,0:T(8,128)(2,1)}, u32[]{:S(2)}, u32[]{:S(2)}) collective-permute-start(bf16[20,128,128]{2,1,0:T(8,128)(2,1)} %get-tuple-element.11), channel_id=1, source_target_pairs={{0,64},{32,96},{64,0},{96,32},{1,65},{33,97},{65,1},{97,33},{2,66}... | collective-permute-start | bytes 1966088 | tf_op jit(solution)/shard_map/ppermute | solution.py:226
  111.6 28.0 %collective-permute-start.4 = (bf16[20,128,128]{2,1,0:T(8,128)(2,1)}, bf16[20,128,128]{2,1,0:T(8,128)(2,1)}, u32[]{:S(2)}, u32[]{:S(2)}) collective-permute-start(bf16[20,128,128]{2,1,0:T(8,128)(2,1)} %get-tuple-element.12), channel_id=1, source_target_pairs={{0,96},{32,0},{64,32},{96,64},{1,97},{33,1},{65,33},{97,65},{2,98}... | collective-permute-start | bytes 1966088 | tf_op jit(solution)/shard_map/ppermute | solution.py:226
  112.3 81.2 %collective-permute-start.1 = (bf16[40,256,128]{2,1,0:T(8,128)(2,1)S(1)}, bf16[40,256,128]{2,1,0:T(8,128)(2,1)S(1)}, u32[]{:S(2)}, u32[]{:S(2)}) collective-permute-start(bf16[40,256,128]{2,1,0:T(8,128)(2,1)S(1)} %all-to-all-done.1.refs_3_), channel_id=1, source_target_pairs={{0,1},{1,0},{2,3},{3,2},{4,5},{5,4},{6,7},{7,6},{8,9},{9,8},{10,11... | collective-permute-start | bytes 7864328 | tf_op jit(solution)/shard_map/ppermute | solution.py:226
  141.5 7.3 %collective-permute-start.5 = (bf16[10,128,128]{2,1,0:T(8,128)(2,1)S(1)}, bf16[10,128,128]{2,1,0:T(8,128)(2,1)S(1)}, u32[]{:S(2)}, u32[]{:S(2)}) collective-permute-start(bf16[10,128,128]{2,1,0:T(8,128)(2,1)S(1)} %slice.9), channel_id=1, source_target_pairs={{0,16},{16,0},{1,17},{17,1},{2,18},{18,2},{3,19},{19,3},{4,20},{20... | collective-permute-start | bytes 983048 | tf_op jit(solution)/shard_map/ppermute | solution.py:226
  148.9 6.3 %collective-permute-start.6 = (bf16[10,128,128]{2,1,0:T(8,128)(2,1)S(1)}, bf16[10,128,128]{2,1,0:T(8,128)(2,1)S(1)}, u32[]{:S(2)}, u32[]{:S(2)}) collective-permute-start(bf16[10,128,128]{2,1,0:T(8,128)(2,1)S(1)} %add_convert_fusion.1), channel_id=1, source_target_pairs={{0,16},{16,0},{1,17},{17,1},{2,18},{18,2},{3,19},{19,3},{4,20},{20... | collective-permute-start | bytes 983048 | tf_op jit(solution)/shard_map/ppermute | solution.py:226
  155.3 20.7 %collective-permute-start.9 = (bf16[20,128,128]{2,1,0:T(8,128)(2,1)S(1)}, bf16[20,128,128]{2,1,0:T(8,128)(2,1)S(1)}, u32[]{:S(2)}, u32[]{:S(2)}) collective-permute-start(bf16[20,128,128]{2,1,0:T(8,128)(2,1)S(1)} %pad_maximum_fusion.refs_5_), channel_id=1, source_target_pairs={{0,96},{32,0},{64,32},{96,64},{1,97},{33,1},{65,33},{97,65},{2,98}... | collective-permute-start | bytes 1966088 | tf_op jit(solution)/shard_map/ppermute | solution.py:226
  162.0 15.3 %collective-permute-start.8 = (bf16[20,128,128]{2,1,0:T(8,128)(2,1)S(1)}, bf16[20,128,128]{2,1,0:T(8,128)(2,1)S(1)}, u32[]{:S(2)}, u32[]{:S(2)}) collective-permute-start(bf16[20,128,128]{2,1,0:T(8,128)(2,1)S(1)} %pad_maximum_fusion.refs_5_), channel_id=1, source_target_pairs={{0,64},{32,96},{64,0},{96,32},{1,65},{33,97},{65,1},{97,33},{2,66}... | collective-permute-start | bytes 1966088 | tf_op jit(solution)/shard_map/ppermute | solution.py:226
  162.0 31.6 %collective-permute-start.7 = (bf16[20,128,128]{2,1,0:T(8,128)(2,1)S(1)}, bf16[20,128,128]{2,1,0:T(8,128)(2,1)S(1)}, u32[]{:S(2)}, u32[]{:S(2)}) collective-permute-start(bf16[20,128,128]{2,1,0:T(8,128)(2,1)S(1)} %pad_maximum_fusion.refs_5_), channel_id=1, source_target_pairs={{0,32},{32,64},{64,96},{96,0},{1,33},{33,65},{65,97},{97,1},{2,34}... | collective-permute-start | bytes 1966088 | tf_op jit(solution)/shard_map/ppermute | solution.py:226

commit v2 on v0

v2 whole, which is shorter than its diff:
```python
import jax
import jax.numpy as jnp
from jax import lax
from jax.experimental import pallas as pl
from jax.experimental.pallas import tpu as pltpu
from jax.sharding import Mesh
from jax.sharding import PartitionSpec as P

WIDTH = 128
PART = 40
CHUNK = 4
Z, XL, Y, XH, CORE = 4, 2, 4, 2, 2
HALF = PART // CORE
ONE = HALF // Y
TWO = PART // Z
HBM = pl.BlockSpec(memory_space=pltpu.HBM)
VMEM = pl.BlockSpec(memory_space=pltpu.VMEM)
SMEM = pl.BlockSpec(memory_space=pltpu.SMEM)
PARAMS = pltpu.CompilerParams(vmem_limit_bytes=60 * 2**20)


def packed(size_ref, lo, hi):
    first, chunk, plan = 0, 0, []
    for s in range(size_ref.shape[0]):
        blocks = (size_ref[s] + (WIDTH - 1)) // WIDTH
        begin, end = jnp.clip(lo - first, 0, blocks), jnp.clip(hi - first, 0, blocks)
        chunks = (end - begin + (CHUNK - 1)) // CHUNK
        plan.append((first, begin, end, chunk, chunks))
        first, chunk = first + blocks, chunk + chunks
    return plan, first


def most_chunks(slots, sectors):
    return (slots + sectors * (CHUNK - 1)) // CHUNK


def left_kernel(add, at_ref, size_ref, edge_ref, site_ref, *rest):
    if add:
        other_ref, out_ref, edge_buf, site_buf, edge_sem, site_sem, other_buf, other_sem = rest
        other = pltpu.make_async_copy(other_ref, other_buf, other_sem)
    else:
        out_ref, edge_buf, site_buf, edge_sem, site_sem = rest
    lo = at_ref[0]
    plan, used = packed(size_ref, lo, lo + HALF)
    last = site_ref.shape[2] // WIDTH - CHUNK

    def block_of(s, c):
        return jnp.minimum(plan[s][1] + c * CHUNK, last)

    def fetch(s, c):
        at = plan[s][3] + c
        columns = pl.ds(pl.multiple_of(block_of(s, c) * WIDTH, WIDTH), CHUNK * WIDTH)
        return pltpu.make_async_copy(site_ref.at[s, :, columns], site_buf.at[at], site_sem.at[at])

    edges = [pltpu.make_async_copy(edge_ref.at[s], edge_buf.at[s], edge_sem.at[s]) for s in range(len(plan))]
    for s in range(len(plan)):
        edges[s].start()

        @pl.loop(0, plan[s][4])
        def _(c):
            fetch(s, c).start()

    if add:
        other.start()

    @pl.loop(jnp.clip(used - lo, 0, HALF), HALF)
    def _(q):
        out_ref[q] = jnp.zeros(out_ref.shape[1:], out_ref.dtype)

    if add:
        other.wait()
    for s in range(len(plan)):
        first, begin, end, chunk, chunks = plan[s]
        edges[s].wait()

        @pl.loop(0, chunks)
        def _(c):
            fetch(s, c).wait()
            block = block_of(s, c)
            term = jnp.dot(edge_buf[s], site_buf[chunk + c], preferred_element_type=jnp.float32)
            for k in range(CHUNK):

                @pl.when((block + k >= begin) & (block + k < end))
                def _():
                    q = first + block + k - lo
                    part = term[:, k * WIDTH : (k + 1) * WIDTH]
                    if add:
                        part = part + other_buf[q].astype(jnp.float32)
                    out_ref[q] = part.astype(out_ref.dtype)


def left_terms(first_slot, sizes, edge, site, *other):
    sectors, rows, depth = edge.shape
    most = most_chunks(HALF, sectors)
    add = bool(other)
    slots = (HALF, rows, WIDTH)
    return pl.pallas_call(
        lambda *refs: left_kernel(add, *refs),
        out_shape=jax.ShapeDtypeStruct(slots, jnp.bfloat16),
        in_specs=[SMEM, SMEM, HBM, HBM] + [HBM] * add,
        out_specs=VMEM,
        scratch_shapes=[
            pltpu.VMEM((sectors, rows, depth), jnp.bfloat16),
            pltpu.VMEM((most, depth, CHUNK * WIDTH), jnp.bfloat16),
            pltpu.SemaphoreType.DMA((sectors,)),
            pltpu.SemaphoreType.DMA((most,)),
        ]
        + [pltpu.VMEM(slots, jnp.bfloat16), pltpu.SemaphoreType.DMA] * add,
        compiler_params=PARAMS,
        cost_estimate=pl.CostEstimate(
            flops=2 * HALF * rows * depth * WIDTH, bytes_accessed=6 * 2**20, transcendentals=0
        ),
        name="left_add" if add else "left",
    )(first_slot.reshape(1).astype(jnp.int32), sizes, edge, site, *other)


def right_kernel(at_ref, size_ref, edge_ref, site_ref, *rest):
    outs, (site_buf, edge_buf, term_buf, site_sem, edge_sem) = rest[:Z], rest[Z:]
    lo, z = at_ref[0], at_ref[1]
    plan, _ = packed(size_ref, lo, lo + PART)
    last = edge_ref.shape[1] // WIDTH - CHUNK

    def block_of(s, c):
        return jnp.minimum(plan[s][1] + c * CHUNK, last)

    def fetch(s, c):
        at = plan[s][3] + c
        rows = pl.ds(pl.multiple_of(block_of(s, c) * WIDTH, WIDTH), CHUNK * WIDTH)
        return pltpu.make_async_copy(edge_ref.at[s, rows, :], edge_buf.at[at], edge_sem.at[at])

    sites = [pltpu.make_async_copy(site_ref.at[s], site_buf.at[s], site_sem.at[s]) for s in range(len(plan))]
    for s in range(len(plan)):
        sites[s].start()

        @pl.loop(0, plan[s][4])
        def _(c):
            fetch(s, c).start()

    for s in range(len(plan)):
        first, _, _, chunk, chunks = plan[s]
        sites[s].wait()

        @pl.loop(0, chunks)
        def _(c):
            fetch(s, c).wait()
            term = jnp.dot(edge_buf[chunk + c], site_buf[s], preferred_element_type=jnp.float32)
            q = first + block_of(s, c) - lo + CHUNK
            term_buf[pl.ds(q, CHUNK)] = term.astype(jnp.bfloat16).reshape(CHUNK, WIDTH, term.shape[1])

    for step in range(Z):
        base = lax.rem(z + step, Z) * TWO + CHUNK
        for k in range(0, TWO, 2):
            outs[step][k : k + 2] = term_buf[pl.ds(base + k, 2)]


def right_terms(first_slot, z, sizes, edge, site):
    sectors, depth, cols = site.shape
    most = most_chunks(PART, sectors)
    return pl.pallas_call(
        right_kernel,
        out_shape=[jax.ShapeDtypeStruct((TWO, WIDTH, cols), jnp.bfloat16)] * Z,
        in_specs=[SMEM, SMEM, HBM, HBM],
        out_specs=[VMEM] * Z,
        scratch_shapes=[
            pltpu.VMEM((sectors, depth, cols), jnp.bfloat16),
            pltpu.VMEM((most, CHUNK * WIDTH, depth), jnp.bfloat16),
            pltpu.VMEM((PART + 2 * CHUNK, WIDTH, cols), jnp.bfloat16),
            pltpu.SemaphoreType.DMA((sectors,)),
            pltpu.SemaphoreType.DMA((most,)),
        ],
        compiler_params=PARAMS,
        cost_estimate=pl.CostEstimate(
            flops=2 * PART * WIDTH * depth * cols, bytes_accessed=10 * 2**20, transcendentals=0
        ),
        name="right",
    )(jnp.stack([first_slot, z]).astype(jnp.int32), sizes, edge, site)


def product_kernel(scale, at_ref, size_ref, own_ref, other_ref, *rest):
    rights, rest = rest[:Z], rest[Z:]
    if scale is None:
        out_ref, one_buf, two_buf, sems = rest
    else:
        before_ref, out_ref, one_buf, two_buf, sems, before_buf = rest
    lo, core, z, row_first, col_first = (at_ref[k] for k in range(5))
    plan, _ = packed(size_ref, lo, lo + PART)
    copies = [
        pltpu.make_async_copy(own_ref, one_buf.at[pl.ds(core * HALF, HALF)], sems.at[0]),
        pltpu.make_async_copy(other_ref, one_buf.at[pl.ds((1 - core) * HALF, HALF)], sems.at[1]),
    ]
    for step in range(Z):
        base = lax.rem(z + Z - step, Z) * TWO
        copies.append(pltpu.make_async_copy(rights[step], two_buf.at[pl.ds(base, TWO)], sems.at[2 + step]))
    if scale is not None:
        copies.append(pltpu.make_async_copy(before_ref, before_buf, sems.at[2 + Z]))
    for copy in copies:
        copy.start()
    for k in range(CHUNK):
        one_buf[PART + k] = jnp.zeros(one_buf.shape[1:], one_buf.dtype)
    for copy in copies:
        copy.wait()
    rows, cols = out_ref.shape[1:]
    deep = lax.broadcasted_iota(jnp.int32, (CHUNK * WIDTH, cols), 0)
    row = lax.broadcasted_iota(jnp.int32, (rows, cols), 0) + row_first
    col = lax.broadcasted_iota(jnp.int32, (rows, cols), 1) + col_first
    for s in range(len(plan)):
        first, begin, end, _, chunks = plan[s]
        size = size_ref[s]
        deep_end = jnp.minimum(size, end * WIDTH)

        def add(c, total):
            block = begin + c * CHUNK
            q = first + block - lo
            left = jnp.concatenate([one_buf[q + k] for k in range(CHUNK)], axis=1)
            right = two_buf[pl.ds(q, CHUNK)].reshape(CHUNK * WIDTH, cols)
            right = jnp.where(deep < deep_end - block * WIDTH, right, jnp.bfloat16(0.0))
            return total + jnp.dot(left, right, preferred_element_type=jnp.float32)

        start = jnp.zeros((rows, cols), jnp.float32) if scale is None else before_buf[s]
        total = lax.fori_loop(0, chunks, add, start)
        if scale is None:
            out_ref[s] = total
        else:
            live = (row < size) & (col < size)
            out_ref[s] = jnp.where(live, total * jnp.float32(scale), jnp.float32(0.0)).astype(out_ref.dtype)


def product(scale, at, sizes, own, other, rights, *before):
    rows, cols, sectors = own.shape[1], rights[0].shape[2], sizes.shape[0]
    shape = (sectors, rows, cols)
    end = bool(before)
    return pl.pallas_call(
        lambda *refs: product_kernel(scale, *refs),
        out_shape=jax.ShapeDtypeStruct(shape, jnp.bfloat16 if end else jnp.float32),
        in_specs=[SMEM, SMEM] + [HBM] * (2 + Z + end),
        out_specs=VMEM,
        scratch_shapes=[
            pltpu.VMEM((PART + CHUNK, rows, WIDTH), jnp.bfloat16),
            pltpu.VMEM((PART + CHUNK, WIDTH, cols), jnp.bfloat16),
            pltpu.SemaphoreType.DMA((2 + Z + end,)),
        ]
        + [pltpu.VMEM(shape, jnp.float32)] * end,
        compiler_params=PARAMS,
        cost_estimate=pl.CostEstimate(
            flops=2 * PART * rows * WIDTH * cols, bytes_accessed=6 * 2**20, transcendentals=0
        ),
        name="product_end" if end else "product",
    )(at, sizes, own, other, *rights, *before)


def shift(array, axis, size, step):
    return lax.ppermute(array, axis, [(i, (i + step) % size) for i in range(size)])


def total(*terms):
    return sum(term.astype(jnp.float32) for term in terms).astype(jnp.bfloat16)


def over_z(arrays):
    return [shift(arrays[step], "z", Z, step) for step in range(1, Z)]


def over_y(array):
    return lax.all_to_all(array, "y", 0, 0, tiled=True)


def swap(array, axis):
    return shift(array, axis, 2, 1)


def on_device(edge_left, site_left, edge_right, site_right, sizes):
    order = site_left.shape[2]
    rows, cols = edge_left.shape[1], site_right.shape[2]
    z, xl, y, xh, core = (lax.axis_index(a) for a in ("z", "xl", "y", "xh", "core"))
    row_first = (z * XL + xl) * rows
    col_first = ((y * XH + xh) * CORE + core) * cols
    fence = lax.optimization_barrier
    A, B = 0, PART

    def left_sums(spread):
        return total(*spread.reshape((Y, ONE, rows, WIDTH)))

    def left_copies(own):
        return jnp.broadcast_to(own[None], (Y,) + own.shape).reshape(HALF, rows, WIDTH)

    def left_for_other(part, edges):
        return left_terms(part + (1 - core) * HALF, sizes, *edges)

    def left_chip(part, edges, came):
        return left_terms(part + core * HALF, sizes, *edges, came)

    left, right = (edge_left, site_left), (edge_right, site_right)
    goes = left_for_other(A, left)
    came = swap(goes, "core")
    goes, right = fence((goes, right))
    right_a = right_terms(jnp.int32(A), z, sizes, *right)
    right_a, left, came = fence((right_a, left, came))
    left_a = left_chip(A, left, came)

    right_a, left_a, left, right = fence((right_a, left_a, left, right))
    spread_a = over_y(left_a)
    came_a = over_z(right_a)
    goes = left_for_other(B, left)
    came = swap(goes, "core")
    goes, right = fence((goes, right))
    right_b = right_terms(jnp.int32(B), z, sizes, *right)
    right_b, left, came = fence((right_b, left, came))
    left_b = left_chip(B, left, came)
    spread_a, came_a, right_b, left_b = fence((spread_a, came_a, right_b, left_b))

    one_a, two_a = left_sums(spread_a), total(right_a[0], *came_a)
    one_a, two_a, right_b, left_b = fence((one_a, two_a, right_b, left_b))
    spread_b = over_y(left_b)
    came_b = over_z(right_b)
    one_x, two_x = swap(one_a, "xh"), swap(two_a, "xl")
    one_a, two_a = total(one_a, one_x), total(two_a, two_x)
    copies_a = left_copies(one_a)
    spread_b, came_b, copies_a, two_a = fence((spread_b, came_b, copies_a, two_a))

    one_b, two_b = left_sums(spread_b), total(right_b[0], *came_b)
    one_b, two_b, copies_a, two_a = fence((one_b, two_b, copies_a, two_a))
    half_a = over_y(copies_a)
    rights_a = [two_a] + over_z([two_a] * Z)
    one_x, two_x = swap(one_b, "xh"), swap(two_b, "xl")
    one_b, two_b = total(one_b, one_x), total(two_b, two_x)
    copies_b = left_copies(one_b)
    half_a, rights_a, copies_b, two_b = fence((half_a, rights_a, copies_b, two_b))

    at = jnp.stack([jnp.int32(A), core, z, row_first, col_first]).astype(jnp.int32)
    half_b = over_y(copies_b)
    rights_b = [two_b] + over_z([two_b] * Z)
    product_a = product(None, at, sizes, half_a, swap(half_a, "core"), rights_a)
    half_b, rights_b, product_a = fence((half_b, rights_b, product_a))
    at = at + jnp.array([B - A, 0, 0, 0, 0], jnp.int32)
    return product(order ** (-0.5), at, sizes, half_b, swap(half_b, "core"), rights_b, product_a)


def solution(mesh):
    split = Mesh(mesh.devices.reshape(Z, XL, Y, XH, CORE), ("z", "xl", "y", "xh", "core"))
    row, col = ("z", "xl"), ("y", "xh", "core")
    placed = (P(None, row, col), P(None, col, None), P(None, None, row), P(None, row, col), P())
    return jax.shard_map(
        on_device, mesh=split, in_specs=placed, out_specs=P(None, row, col), check_vma=False
    )
```

time: 426 us -> 143 us (0.34)
  waiting for transfers between devices: 353 us -> 36.7 us
  Pallas kernels: 0 us -> 49.9 us
  starting transfers between devices: 0.31 us -> 43.6 us
  matrix products: 28.9 us -> 0 us
  local copies, waits for them, and re-layouts: 26.9 us -> 8.23 us
  between operations: 13.2 us -> 0.42 us
    all_gather x2 -> x0, waiting for transfers between devices: 170 us -> none  [the longest x1 90.3 us: on_device(): lax.all_gather(right_tile, 'row', axis=1, tiled=True)]
    reduce_scatter x1 -> x0, waiting for transfers between devices: 92 us -> none  [on_device(): lax.psum_scatter(right_terms, 'row', scatter_dimension=1, tiled=True)]
    unnamed x5 -> x0, waiting for transfers between devices: 91.3 us -> none
    pallas_call x0 -> x8, Pallas kernels: none -> 49.9 us  [the longest x4 21.8 us: left_terms(): pl.pallas_call(lambda *refs: left_kernel(add, *refs), out_shape=jax.Shape...]
    ppermute x0 -> x20, waiting for transfers between devices: none -> 36.6 us  [shift(): lax.ppermute(array, axis, [(i, (i + step) % size) for i in range(size)])]
    dot_general x3 -> x0, matrix products: 28.9 us -> none  [the longest x1 12.3 us: on_device(): jnp.einsum('sik,skj->sij', edge_right, site_right, preferred_element_type...]
    ppermute x0 -> x20, starting transfers between devices: none -> 26.8 us  [shift(): lax.ppermute(array, axis, [(i, (i + step) % size) for i in range(size)])]
    unnamed x12 -> x28, local copies, waits for them, and re-layouts: 26.9 us -> 4.71 us
  transfers between devices with their start and end apart: 4 -> 24, of which waited for: 4 -> 12; matrix products, arithmetic and copies ran while one was open for 3% -> 2% of each run, Pallas kernels for 0% -> 19%
where the time goes in v2:
time: 143 us
  Pallas kernels  49.9 us (35%)
  starting transfers between devices  43.6 us (30%)
  waiting for transfers between devices  36.7 us (26%)
  local copies, waits for them, and re-layouts  8.23 us (6%)
  other arithmetic  4.18 us (3%)
    ppermute x20, waiting for transfers between devices, shift(): lax.ppermute(array, axis, [(i, (i + step) % size) for i in range(size)])  36.6 us
    ppermute x20, starting transfers between devices, shift(): lax.ppermute(array, axis, [(i, (i + step) % size) for i in range(size)])  26.8 us
    pallas_call x4, Pallas kernels, left_terms(): pl.pallas_call(lambda *refs: left_kernel(add, *refs), out_shape=jax.Shape...  21.8 us
    all_to_all x4, starting transfers between devices, over_y(): return lax.all_to_all(array, 'y', 0, 0, tiled=True)  16.8 us
    pallas_call x2, Pallas kernels, product(): pl.pallas_call(lambda *refs: product_kernel(scale, *refs), out_shape=jax....  14.1 us
    pallas_call x2, Pallas kernels, right_terms(): pl.pallas_call(right_kernel, out_shape=[jax.ShapeDtypeStruct((TWO, WIDTH,...  13.9 us
    unnamed x28, local copies, waits for them, and re-layouts  4.71 us
    convert_element_type x8, other arithmetic, total(): sum((term.astype(jnp.float32) for term in terms)).astype(jnp.bfloat16)  3.03 us
  transfers between devices with their start and end apart: 24, of which 12 were waited for; matrix products, arithmetic and copies ran while one was open for 2% of the time, Pallas kernels for 19%

profile of v2, /device:TPU:1, one launch (start us, length us, event | category | flops | bytes accessed | tf_op | source)
XLA Modules:
  0.0 142.9 jit_solution(8870265987885432750)
XLA Ops:
  0.0 4.7 %left.2 = bf16[20,256,128]{2,1,0:T(8,128)(2,1)} custom-call(s32[1]{0:T(128)} %bitcast.4.refs_0_, s32[8]{0:T(128)} %refs_1_.11, bf16[8,256,256]{2,1,0:T(8,128)(2,1)} %refs_2_.4, bf16[8,256,2048]{2,1,0:T(8,128)(2,1)} %refs_3_.4), custom_call_target="tpu_custom_call" | custom-call | flops 335544320 | bytes 6291456 | tf_op jit(solution)/shard_map/left/pallas_call | solution.py:97
  4.7 1.5 %collective-permute-start = (bf16[20,256,128]{2,1,0:T(8,128)(2,1)}, bf16[20,256,128]{2,1,0:T(8,128)(2,1)S(1)}, u32[]{:S(2)}, u32[]{:S(2)}) collective-permute-start(bf16[20,256,128]{2,1,0:T(8,128)(2,1)} %left.2), channel_id=1, source_target_pairs={{0,1},{1,0},{2,3},{3,2},{4,5},{5,4},{6,7},{7,6},{8,9},{9,8},{10,11... | collective-permute-start | bytes 3932168 | tf_op jit(solution)/shard_map/ppermute | solution.py:252
  6.9 6.9 %right.2 = (bf16[10,128,128]{2,1,0:T(8,128)(2,1)}, bf16[10,128,128]{2,1,0:T(8,128)(2,1)}, bf16[10,128,128]{2,1,0:T(8,128)(2,1)}, bf16[10,128,128]{2,1,0:T(8,128)(2,1)}) custom-call(s32[2]{0:T(128)} %get-tuple-element.153.at_ref, s32[8]{0:T(128)} %refs_1_.11, bf16[8,2048,512]{2,1,0:T(8,128)(2,1)} %edge_ref.1, bf16[8,512,128]{2,1,0:T(8,128)(2,1)} %site_ref.1), custom_call_target="tpu_custom_call" | custom-call | flops 671088640 | bytes 10485760 | tf_op jit(solution)/shard_map/right/pallas_call | solution.py:159
  14.9 6.1 %left_add.2 = bf16[20,256,128]{2,1,0:T(8,128)(2,1)} custom-call(s32[1]{0:T(128)} %bitcast.5.refs_0_, s32[8]{0:T(128)} %refs_1_.11, bf16[8,256,256]{2,1,0:T(8,128)(2,1)} %refs_2_.4, bf16[8,256,2048]{2,1,0:T(8,128)(2,1)} %refs_3_.4, bf16[20,256,128]{2,1,0:T(8,128)(2,1)} %copy-done.4), custom_call_target="tpu_custom_call" | custom-call | flops 335544320 | bytes 6291456 | tf_op jit(solution)/shard_map/left_add/pallas_call | solution.py:97
  21.0 4.9 %left.3 = bf16[20,256,128]{2,1,0:T(8,128)(2,1)} custom-call(s32[1]{0:T(128)} %bitcast.6.refs_0_, s32[8]{0:T(128)} %refs_1_.11, bf16[8,256,256]{2,1,0:T(8,128)(2,1)} %refs_2_.4, bf16[8,256,2048]{2,1,0:T(8,128)(2,1)} %refs_3_.4), custom_call_target="tpu_custom_call" | custom-call | flops 335544320 | bytes 6291456 | tf_op jit(solution)/shard_map/left/pallas_call | solution.py:97
  26.0 4.3 %all-to-all-start = ((bf16[20,256,128]{2,1,0:T(8,128)(2,1)}), bf16[20,256,128]{2,1,0:T(8,128)(2,1)S(1)}, u32[]{:S(2)}, u32[]{:S(2)}) async-start(bf16[20,256,128]{2,1,0:T(8,128)(2,1)} %left_add.2), calls=%async_computation | async-start | bytes 2621440 | tf_op jit(solution)/shard_map/all_to_all | solution.py:264
  30.3 1.6 %collective-permute-start.1 = (bf16[10,128,128]{2,1,0:T(8,128)(2,1)}, bf16[10,128,128]{2,1,0:T(8,128)(2,1)S(1)}, u32[]{:S(2)}, u32[]{:S(2)}) collective-permute-start(bf16[10,128,128]{2,1,0:T(8,128)(2,1)} %get-tuple-element.93), channel_id=1, source_target_pairs={{0,32},{32,64},{64,96},{96,0},{1,33},{33,65},{65,97},{97,1},{2,34}... | collective-permute-start | bytes 983048 | tf_op jit(solution)/shard_map/ppermute | solution.py:252
  31.9 3.3 %collective-permute-start.2 = (bf16[10,128,128]{2,1,0:T(8,128)(2,1)}, bf16[10,128,128]{2,1,0:T(8,128)(2,1)S(1)}, u32[]{:S(2)}, u32[]{:S(2)}) collective-permute-start(bf16[10,128,128]{2,1,0:T(8,128)(2,1)} %get-tuple-element.94), channel_id=1, source_target_pairs={{0,64},{32,96},{64,0},{96,32},{1,65},{33,97},{65,1},{97,33},{2,66}... | collective-permute-start | bytes 983048 | tf_op jit(solution)/shard_map/ppermute | solution.py:252
  36.0 7.0 %right.3 = (bf16[10,128,128]{2,1,0:T(8,128)(2,1)}, bf16[10,128,128]{2,1,0:T(8,128)(2,1)}, bf16[10,128,128]{2,1,0:T(8,128)(2,1)}, bf16[10,128,128]{2,1,0:T(8,128)(2,1)}) custom-call(s32[2]{0:T(128)} %get-tuple-element.154.at_ref, s32[8]{0:T(128)} %refs_1_.11, bf16[8,2048,512]{2,1,0:T(8,128)(2,1)} %edge_ref.1, bf16[8,512,128]{2,1,0:T(8,128)(2,1)} %site_ref.1), custom_call_target="tpu_custom_call" | custom-call | flops 671088640 | bytes 10485760 | tf_op jit(solution)/shard_map/right/pallas_call | solution.py:159
  44.1 6.1 %left_add.3 = bf16[20,256,128]{2,1,0:T(8,128)(2,1)} custom-call(s32[1]{0:T(128)} %bitcast.7.refs_0_, s32[8]{0:T(128)} %refs_1_.11, bf16[8,256,256]{2,1,0:T(8,128)(2,1)} %refs_2_.4, bf16[8,256,2048]{2,1,0:T(8,128)(2,1)} %refs_3_.4, bf16[20,256,128]{2,1,0:T(8,128)(2,1)} %copy-done.3), custom_call_target="tpu_custom_call" | custom-call | flops 335544320 | bytes 6291456 | tf_op jit(solution)/shard_map/left_add/pallas_call | solution.py:97
  52.3 4.4 %all-to-all-start.1 = ((bf16[20,256,128]{2,1,0:T(8,128)(2,1)}), bf16[20,256,128]{2,1,0:T(8,128)(2,1)S(1)}, u32[]{:S(2)}, u32[]{:S(2)}) async-start(bf16[20,256,128]{2,1,0:T(8,128)(2,1)} %left_add.3), calls=%async_computation.1 | async-start | bytes 2621440 | tf_op jit(solution)/shard_map/all_to_all | solution.py:264
  56.7 1.2 collective-permute-start.9
  57.9 2.5 %collective-permute-start.8 = (bf16[5,256,128]{2,1,0:T(8,128)(2,1)S(1)}, bf16[5,256,128]{2,1,0:T(8,128)(2,1)S(1)}, u32[]{:S(2)}, u32[]{:S(2)}) collective-permute-start(bf16[5,256,128]{2,1,0:T(8,128)(2,1)S(1)} %add_convert_fusion.7), channel_id=1, source_target_pairs={{0,2},{2,0},{1,3},{3,1},{4,6},{6,4},{5,7},{7,5},{8,10},{10,8},{9,1... | collective-permute-start | bytes 983048 | tf_op jit(solution)/shard_map/ppermute | solution.py:252
  61.1 2.0 %collective-permute-start.6 = (bf16[10,128,128]{2,1,0:T(8,128)(2,1)}, bf16[10,128,128]{2,1,0:T(8,128)(2,1)S(1)}, u32[]{:S(2)}, u32[]{:S(2)}) collective-permute-start(bf16[10,128,128]{2,1,0:T(8,128)(2,1)} %get-tuple-element.125), channel_id=1, source_target_pairs={{0,64},{32,96},{64,0},{96,32},{1,65},{33,97},{65,1},{97,33},{2,66}... | collective-permute-start | bytes 983048 | tf_op jit(solution)/shard_map/ppermute | solution.py:252
  63.8 9.1 %collective-permute-done.8 = bf16[5,256,128]{2,1,0:T(8,128)(2,1)S(1)} collective-permute-done((bf16[5,256,128]{2,1,0:T(8,128)(2,1)S(1)}, bf16[5,256,128]{2,1,0:T(8,128)(2,1)S(1)}, u32[]{:S(2)}, u32[]{:S(2)}) %collective-permute-start.8) | collective-permute-done | bytes 327712 | tf_op jit(solution)/shard_map/ppermute | solution.py:252
  73.0 3.8 %collective-permute-done.6 = bf16[10,128,128]{2,1,0:T(8,128)(2,1)S(1)} collective-permute-done((bf16[10,128,128]{2,1,0:T(8,128)(2,1)}, bf16[10,128,128]{2,1,0:T(8,128)(2,1)S(1)}, u32[]{:S(2)}, u32[]{:S(2)}) %collective-permute-start.6) | collective-permute-done | bytes 327712 | tf_op jit(solution)/shard_map/ppermute | solution.py:252
  76.8 1.3 collective-permute-done.7
  78.1 1.4 broadcast_in_dim.4
  80.8 3.9 %all-to-all-start.2 = ((bf16[20,256,128]{2,1,0:T(8,128)(2,1)}), bf16[20,256,128]{2,1,0:T(8,128)(2,1)S(1)}, u32[]{:S(2)}, u32[]{:S(2)}) async-start(bf16[20,256,128]{2,1,0:T(8,128)(2,1)} %bitcast.8), calls=%async_computation.2 | async-start | bytes 2621440 | tf_op jit(solution)/shard_map/all_to_all | solution.py:264
  84.7 1.4 collective-permute-start.13
  87.2 3.5 %collective-permute-start.11 = (bf16[10,128,128]{2,1,0:T(8,128)(2,1)S(1)}, bf16[10,128,128]{2,1,0:T(8,128)(2,1)S(1)}, u32[]{:S(2)}, u32[]{:S(2)}) collective-permute-start(bf16[10,128,128]{2,1,0:T(8,128)(2,1)S(1)} %add_convert_fusion.4.refs_4_), channel_id=1, source_target_pairs={{0,64},{32,96},{64,0},{96,32},{1,65},{33,97},{65,1},{97,33},{2,66}... | collective-permute-start | bytes 983048 | tf_op jit(solution)/shard_map/ppermute | solution.py:252
  91.8 6.8 %collective-permute-done.13 = bf16[5,256,128]{2,1,0:T(8,128)(2,1)S(1)} collective-permute-done((bf16[5,256,128]{2,1,0:T(8,128)(2,1)S(1)}, bf16[5,256,128]{2,1,0:T(8,128)(2,1)S(1)}, u32[]{:S(2)}, u32[]{:S(2)}) %collective-permute-start.13) | collective-permute-done | bytes 327712 | tf_op jit(solution)/shard_map/ppermute | solution.py:252
  98.7 5.0 %collective-permute-done.11.refs_6_ = bf16[10,128,128]{2,1,0:T(8,128)(2,1)S(1)} collective-permute-done((bf16[10,128,128]{2,1,0:T(8,128)(2,1)S(1)}, bf16[10,128,128]{2,1,0:T(8,128)(2,1)S(1)}, u32[]{:S(2)}, u32[]{:S(2)}) %collective-permute-start.11) | collective-permute-done | bytes 327712 | tf_op jit(solution)/shard_map/ppermute | solution.py:252
  104.4 1.5 %broadcast_in_dim.5 = bf16[4,5,256,128]{3,2,1,0:T(8,128)(2,1)} broadcast(bf16[5,256,128]{2,1,0:T(8,128)(2,1)S(1)} %add_convert_fusion.1), dimensions={1,2,3} | broadcast | bytes 1638400 | tf_op jit(solution)/shard_map/broadcast_in_dim | solution.py:284
  105.9 2.7 %collective-permute-start.18 = (bf16[20,256,128]{2,1,0:T(8,128)(2,1)S(1)}, bf16[20,256,128]{2,1,0:T(8,128)(2,1)}, u32[]{:S(2)}, u32[]{:S(2)}) collective-permute-start(bf16[20,256,128]{2,1,0:T(8,128)(2,1)S(1)} %all-to-all-done.2.refs_2_), channel_id=1, source_target_pairs={{0,1},{1,0},{2,3},{3,2},{4,5},{5,4},{6,7},{7,6},{8,9},{9,8},{10,11... | collective-permute-start | bytes 3932168 | tf_op jit(solution)/shard_map/ppermute | solution.py:252
  108.6 4.2 %all-to-all-start.3 = ((bf16[20,256,128]{2,1,0:T(8,128)(2,1)}), bf16[20,256,128]{2,1,0:T(8,128)(2,1)S(1)}, u32[]{:S(2)}, u32[]{:S(2)}) async-start(bf16[20,256,128]{2,1,0:T(8,128)(2,1)} %bitcast.9), calls=%async_computation.3 | async-start | bytes 2621440 | tf_op jit(solution)/shard_map/all_to_all | solution.py:264
  112.8 2.3 %collective-permute-start.16 = (bf16[10,128,128]{2,1,0:T(8,128)(2,1)S(1)}, bf16[10,128,128]{2,1,0:T(8,128)(2,1)}, u32[]{:S(2)}, u32[]{:S(2)}) collective-permute-start(bf16[10,128,128]{2,1,0:T(8,128)(2,1)S(1)} %add_convert_fusion.refs_4_), channel_id=1, source_target_pairs={{0,64},{32,96},{64,0},{96,32},{1,65},{33,97},{65,1},{97,33},{2,66}... | collective-permute-start | bytes 983048 | tf_op jit(solution)/shard_map/ppermute | solution.py:252
  116.2 7.0 %product.1.refs_8_ = f32[8,256,128]{2,1,0:T(8,128)} custom-call(s32[5]{0:T(128)} %stack.27.refs_0_, s32[8]{0:T(128)} %refs_1_.11, bf16[20,256,128]{2,1,0:T(8,128)(2,1)} %copy-done, bf16[20,256,128]{2,1,0:T(8,128)(2,1)} %collective-permute-done.18.refs_3_, bf16[10,128,128]{2,1,0:T(8,128)(2,1)} %copy-done.6, bf16[10,128,128]{2,1,0:T(8,128)(2,1)} %copy-done.10, ...), custom_call_target="tpu_custom_call" | custom-call | flops 335544320 | bytes 6291456 | tf_op jit(solution)/shard_map/product/pallas_call | solution.py:232
  123.4 6.5 %collective-permute-done.16.refs_6_ = bf16[10,128,128]{2,1,0:T(8,128)(2,1)} collective-permute-done((bf16[10,128,128]{2,1,0:T(8,128)(2,1)S(1)}, bf16[10,128,128]{2,1,0:T(8,128)(2,1)}, u32[]{:S(2)}, u32[]{:S(2)}) %collective-permute-start.16) | collective-permute-done | bytes 327712 | tf_op jit(solution)/shard_map/ppermute | solution.py:252
  130.6 1.3 collective-permute-start.19
  132.5 2.1 %collective-permute-done.19.refs_3_ = bf16[20,256,128]{2,1,0:T(8,128)(2,1)S(1)} collective-permute-done((bf16[20,256,128]{2,1,0:T(8,128)(2,1)S(1)}, bf16[20,256,128]{2,1,0:T(8,128)(2,1)S(1)}, u32[]{:S(2)}, u32[]{:S(2)}) %collective-permute-start.19) | collective-permute-done | bytes 1310752 | tf_op jit(solution)/shard_map/ppermute | solution.py:252
  135.7 7.1 %product_end.1 = bf16[8,256,128]{2,1,0:T(8,128)(2,1)} custom-call(s32[5]{0:T(128)} %add.69.refs_0_, s32[8]{0:T(128)} %refs_1_.11, bf16[20,256,128]{2,1,0:T(8,128)(2,1)} %copy-done.1, bf16[20,256,128]{2,1,0:T(8,128)(2,1)} %copy-done.5, bf16[10,128,128]{2,1,0:T(8,128)(2,1)} %copy-done.2, bf16[10,128,128]{2,1,0:T(8,128)(2,1)} %copy-done.7, ...), custom_call_target="tpu_custom_call" | custom-call | flops 335544320 | bytes 6291456 | tf_op jit(solution)/shard_map/product_end/pallas_call | solution.py:232
  (65 shorter events, 15.1 us)
Async XLA Ops:
  4.7 9.1 %collective-permute-start = (bf16[20,256,128]{2,1,0:T(8,128)(2,1)}, bf16[20,256,128]{2,1,0:T(8,128)(2,1)S(1)}, u32[]{:S(2)}, u32[]{:S(2)}) collective-permute-start(bf16[20,256,128]{2,1,0:T(8,128)(2,1)} %left.2), channel_id=1, source_target_pairs={{0,1},{1,0},{2,3},{3,2},{4,5},{5,4},{6,7},{7,6},{8,9},{9,8},{10,11... | collective-permute-start | bytes 3932168 | tf_op jit(solution)/shard_map/ppermute | solution.py:252
  25.9 17.1 %collective-permute-start.4 = (bf16[20,256,128]{2,1,0:T(8,128)(2,1)}, bf16[20,256,128]{2,1,0:T(8,128)(2,1)S(1)}, u32[]{:S(2)}, u32[]{:S(2)}) collective-permute-start(bf16[20,256,128]{2,1,0:T(8,128)(2,1)} %left.3), channel_id=1, source_target_pairs={{0,1},{1,0},{2,3},{3,2},{4,5},{5,4},{6,7},{7,6},{8,9},{9,8},{10,11... | collective-permute-start | bytes 3932168 | tf_op jit(solution)/shard_map/ppermute | solution.py:252
  26.0 24.2 %all-to-all-start = ((bf16[20,256,128]{2,1,0:T(8,128)(2,1)}), bf16[20,256,128]{2,1,0:T(8,128)(2,1)S(1)}, u32[]{:S(2)}, u32[]{:S(2)}) async-start(bf16[20,256,128]{2,1,0:T(8,128)(2,1)} %left_add.2), calls=%async_computation | async-start | bytes 2621440 | tf_op jit(solution)/shard_map/all_to_all | solution.py:264
  30.3 19.9 %collective-permute-start.1 = (bf16[10,128,128]{2,1,0:T(8,128)(2,1)}, bf16[10,128,128]{2,1,0:T(8,128)(2,1)S(1)}, u32[]{:S(2)}, u32[]{:S(2)}) collective-permute-start(bf16[10,128,128]{2,1,0:T(8,128)(2,1)} %get-tuple-element.93), channel_id=1, source_target_pairs={{0,32},{32,64},{64,96},{96,0},{1,33},{33,65},{65,97},{97,1},{2,34}... | collective-permute-start | bytes 983048 | tf_op jit(solution)/shard_map/ppermute | solution.py:252
  31.9 18.3 %collective-permute-start.2 = (bf16[10,128,128]{2,1,0:T(8,128)(2,1)}, bf16[10,128,128]{2,1,0:T(8,128)(2,1)S(1)}, u32[]{:S(2)}, u32[]{:S(2)}) collective-permute-start(bf16[10,128,128]{2,1,0:T(8,128)(2,1)} %get-tuple-element.94), channel_id=1, source_target_pairs={{0,64},{32,96},{64,0},{96,32},{1,65},{33,97},{65,1},{97,33},{2,66}... | collective-permute-start | bytes 983048 | tf_op jit(solution)/shard_map/ppermute | solution.py:252
  35.2 15.0 %collective-permute-start.3 = (bf16[10,128,128]{2,1,0:T(8,128)(2,1)}, bf16[10,128,128]{2,1,0:T(8,128)(2,1)}, u32[]{:S(2)}, u32[]{:S(2)}) collective-permute-start(bf16[10,128,128]{2,1,0:T(8,128)(2,1)} %get-tuple-element.95), channel_id=1, source_target_pairs={{0,96},{32,0},{64,32},{96,64},{1,97},{33,1},{65,33},{97,65},{2,98}... | collective-permute-start | bytes 983048 | tf_op jit(solution)/shard_map/ppermute | solution.py:252
  52.3 25.7 %all-to-all-start.1 = ((bf16[20,256,128]{2,1,0:T(8,128)(2,1)}), bf16[20,256,128]{2,1,0:T(8,128)(2,1)S(1)}, u32[]{:S(2)}, u32[]{:S(2)}) async-start(bf16[20,256,128]{2,1,0:T(8,128)(2,1)} %left_add.3), calls=%async_computation.1 | async-start | bytes 2621440 | tf_op jit(solution)/shard_map/all_to_all | solution.py:264
  56.7 6.9 %collective-permute-start.9 = (bf16[10,128,128]{2,1,0:T(8,128)(2,1)S(1)}, bf16[10,128,128]{2,1,0:T(8,128)(2,1)S(1)}, u32[]{:S(2)}, u32[]{:S(2)}) collective-permute-start(bf16[10,128,128]{2,1,0:T(8,128)(2,1)S(1)} %add_convert_fusion.6), channel_id=1, source_target_pairs={{0,16},{16,0},{1,17},{17,1},{2,18},{18,2},{3,19},{19,3},{4,20},{20... | collective-permute-start | bytes 983048 | tf_op jit(solution)/shard_map/ppermute | solution.py:252
  57.9 14.9 %collective-permute-start.8 = (bf16[5,256,128]{2,1,0:T(8,128)(2,1)S(1)}, bf16[5,256,128]{2,1,0:T(8,128)(2,1)S(1)}, u32[]{:S(2)}, u32[]{:S(2)}) collective-permute-start(bf16[5,256,128]{2,1,0:T(8,128)(2,1)S(1)} %add_convert_fusion.7), channel_id=1, source_target_pairs={{0,2},{2,0},{1,3},{3,1},{4,6},{6,4},{5,7},{7,5},{8,10},{10,8},{9,1... | collective-permute-start | bytes 983048 | tf_op jit(solution)/shard_map/ppermute | solution.py:252
  60.4 12.6 %collective-permute-start.5 = (bf16[10,128,128]{2,1,0:T(8,128)(2,1)}, bf16[10,128,128]{2,1,0:T(8,128)(2,1)S(1)}, u32[]{:S(2)}, u32[]{:S(2)}) collective-permute-start(bf16[10,128,128]{2,1,0:T(8,128)(2,1)} %get-tuple-element.124), channel_id=1, source_target_pairs={{0,32},{32,64},{64,96},{96,0},{1,33},{33,65},{65,97},{97,1},{2,34}... | collective-permute-start | bytes 983048 | tf_op jit(solution)/shard_map/ppermute | solution.py:252
  61.1 15.6 %collective-permute-start.6 = (bf16[10,128,128]{2,1,0:T(8,128)(2,1)}, bf16[10,128,128]{2,1,0:T(8,128)(2,1)S(1)}, u32[]{:S(2)}, u32[]{:S(2)}) collective-permute-start(bf16[10,128,128]{2,1,0:T(8,128)(2,1)} %get-tuple-element.125), channel_id=1, source_target_pairs={{0,64},{32,96},{64,0},{96,32},{1,65},{33,97},{65,1},{97,33},{2,66}... | collective-permute-start | bytes 983048 | tf_op jit(solution)/shard_map/ppermute | solution.py:252
  63.1 14.9 %collective-permute-start.7 = (bf16[10,128,128]{2,1,0:T(8,128)(2,1)}, bf16[10,128,128]{2,1,0:T(8,128)(2,1)}, u32[]{:S(2)}, u32[]{:S(2)}) collective-permute-start(bf16[10,128,128]{2,1,0:T(8,128)(2,1)} %get-tuple-element.126), channel_id=1, source_target_pairs={{0,96},{32,0},{64,32},{96,64},{1,97},{33,1},{65,33},{97,65},{2,98}... | collective-permute-start | bytes 983048 | tf_op jit(solution)/shard_map/ppermute | solution.py:252
  63.7 26.9 %copy-start.6 = (bf16[10,128,128]{2,1,0:T(8,128)(2,1)}, bf16[10,128,128]{2,1,0:T(8,128)(2,1)S(1)}, u32[]{:S(2)}) copy-start(bf16[10,128,128]{2,1,0:T(8,128)(2,1)S(1)} %add_convert_fusion.4.refs_4_) | copy-start | bytes 983044
  73.0 6.7 %copy-start.8 = (bf16[10,128,128]{2,1,0:T(8,128)(2,1)S(1)}, bf16[10,128,128]{2,1,0:T(8,128)(2,1)}, u32[]{:S(2)}) copy-start(bf16[10,128,128]{2,1,0:T(8,128)(2,1)} %get-tuple-element.130) | copy-start | bytes 983044
  80.8 23.7 %all-to-all-start.2 = ((bf16[20,256,128]{2,1,0:T(8,128)(2,1)}), bf16[20,256,128]{2,1,0:T(8,128)(2,1)S(1)}, u32[]{:S(2)}, u32[]{:S(2)}) async-start(bf16[20,256,128]{2,1,0:T(8,128)(2,1)} %bitcast.8), calls=%async_computation.2 | async-start | bytes 2621440 | tf_op jit(solution)/shard_map/all_to_all | solution.py:264
  84.7 7.0 %collective-permute-start.14 = (bf16[10,128,128]{2,1,0:T(8,128)(2,1)S(1)}, bf16[10,128,128]{2,1,0:T(8,128)(2,1)S(1)}, u32[]{:S(2)}, u32[]{:S(2)}) collective-permute-start(bf16[10,128,128]{2,1,0:T(8,128)(2,1)S(1)} %add_convert_fusion.2), channel_id=1, source_target_pairs={{0,16},{16,0},{1,17},{17,1},{2,18},{18,2},{3,19},{19,3},{4,20},{20... | collective-permute-start | bytes 983048 | tf_op jit(solution)/shard_map/ppermute | solution.py:252
  84.7 13.9 %collective-permute-start.13 = (bf16[5,256,128]{2,1,0:T(8,128)(2,1)S(1)}, bf16[5,256,128]{2,1,0:T(8,128)(2,1)S(1)}, u32[]{:S(2)}, u32[]{:S(2)}) collective-permute-start(bf16[5,256,128]{2,1,0:T(8,128)(2,1)S(1)} %add_convert_fusion.3), channel_id=1, source_target_pairs={{0,2},{2,0},{1,3},{3,1},{4,6},{6,4},{5,7},{7,5},{8,10},{10,8},{9,1... | collective-permute-start | bytes 983048 | tf_op jit(solution)/shard_map/ppermute | solution.py:252
  86.1 12.6 %collective-permute-start.10 = (bf16[10,128,128]{2,1,0:T(8,128)(2,1)S(1)}, bf16[10,128,128]{2,1,0:T(8,128)(2,1)S(1)}, u32[]{:S(2)}, u32[]{:S(2)}) collective-permute-start(bf16[10,128,128]{2,1,0:T(8,128)(2,1)S(1)} %add_convert_fusion.4.refs_4_), channel_id=1, source_target_pairs={{0,32},{32,64},{64,96},{96,0},{1,33},{33,65},{65,97},{97,1},{2,34}... | collective-permute-start | bytes 983048 | tf_op jit(solution)/shard_map/ppermute | solution.py:252
  87.2 16.5 %collective-permute-start.11 = (bf16[10,128,128]{2,1,0:T(8,128)(2,1)S(1)}, bf16[10,128,128]{2,1,0:T(8,128)(2,1)S(1)}, u32[]{:S(2)}, u32[]{:S(2)}) collective-permute-start(bf16[10,128,128]{2,1,0:T(8,128)(2,1)S(1)} %add_convert_fusion.4.refs_4_), channel_id=1, source_target_pairs={{0,64},{32,96},{64,0},{96,32},{1,65},{33,97},{65,1},{97,33},{2,66}... | collective-permute-start | bytes 983048 | tf_op jit(solution)/shard_map/ppermute | solution.py:252
  90.7 13.8 %collective-permute-start.12 = (bf16[10,128,128]{2,1,0:T(8,128)(2,1)S(1)}, bf16[10,128,128]{2,1,0:T(8,128)(2,1)}, u32[]{:S(2)}, u32[]{:S(2)}) collective-permute-start(bf16[10,128,128]{2,1,0:T(8,128)(2,1)S(1)} %add_convert_fusion.4.refs_4_), channel_id=1, source_target_pairs={{0,96},{32,0},{64,32},{96,64},{1,97},{33,1},{65,33},{97,65},{2,98}... | collective-permute-start | bytes 983048 | tf_op jit(solution)/shard_map/ppermute | solution.py:252
  91.7 23.4 %copy-start.2 = (bf16[10,128,128]{2,1,0:T(8,128)(2,1)}, bf16[10,128,128]{2,1,0:T(8,128)(2,1)S(1)}, u32[]{:S(2)}) copy-start(bf16[10,128,128]{2,1,0:T(8,128)(2,1)S(1)} %add_convert_fusion.refs_4_) | copy-start | bytes 983044
  98.7 5.0 %copy-start.10 = (bf16[10,128,128]{2,1,0:T(8,128)(2,1)}, bf16[10,128,128]{2,1,0:T(8,128)(2,1)S(1)}, u32[]{:S(2)}) copy-start(bf16[10,128,128]{2,1,0:T(8,128)(2,1)S(1)} %collective-permute-done.10.refs_5_) | copy-start | bytes 983044
  104.4 4.1 %copy-start = (bf16[20,256,128]{2,1,0:T(8,128)(2,1)}, bf16[20,256,128]{2,1,0:T(8,128)(2,1)S(1)}, u32[]{:S(2)}) copy-start(bf16[20,256,128]{2,1,0:T(8,128)(2,1)S(1)} %all-to-all-done.2.refs_2_) | copy-start | bytes 3932164
  105.9 10.3 %collective-permute-start.18 = (bf16[20,256,128]{2,1,0:T(8,128)(2,1)S(1)}, bf16[20,256,128]{2,1,0:T(8,128)(2,1)}, u32[]{:S(2)}, u32[]{:S(2)}) collective-permute-start(bf16[20,256,128]{2,1,0:T(8,128)(2,1)S(1)} %all-to-all-done.2.refs_2_), channel_id=1, source_target_pairs={{0,1},{1,0},{2,3},{3,2},{4,5},{5,4},{6,7},{7,6},{8,9},{9,8},{10,11... | collective-permute-start | bytes 3932168 | tf_op jit(solution)/shard_map/ppermute | solution.py:252
  108.6 22.0 %all-to-all-start.3 = ((bf16[20,256,128]{2,1,0:T(8,128)(2,1)}), bf16[20,256,128]{2,1,0:T(8,128)(2,1)S(1)}, u32[]{:S(2)}, u32[]{:S(2)}) async-start(bf16[20,256,128]{2,1,0:T(8,128)(2,1)} %bitcast.9), calls=%async_computation.3 | async-start | bytes 2621440 | tf_op jit(solution)/shard_map/all_to_all | solution.py:264
  112.8 10.6 %collective-permute-start.15 = (bf16[10,128,128]{2,1,0:T(8,128)(2,1)S(1)}, bf16[10,128,128]{2,1,0:T(8,128)(2,1)S(1)}, u32[]{:S(2)}, u32[]{:S(2)}) collective-permute-start(bf16[10,128,128]{2,1,0:T(8,128)(2,1)S(1)} %add_convert_fusion.refs_4_), channel_id=1, source_target_pairs={{0,32},{32,64},{64,96},{96,0},{1,33},{33,65},{65,97},{97,1},{2,34}... | collective-permute-start | bytes 983048 | tf_op jit(solution)/shard_map/ppermute | solution.py:252
  112.8 17.1 %collective-permute-start.16 = (bf16[10,128,128]{2,1,0:T(8,128)(2,1)S(1)}, bf16[10,128,128]{2,1,0:T(8,128)(2,1)}, u32[]{:S(2)}, u32[]{:S(2)}) collective-permute-start(bf16[10,128,128]{2,1,0:T(8,128)(2,1)S(1)} %add_convert_fusion.refs_4_), channel_id=1, source_target_pairs={{0,64},{32,96},{64,0},{96,32},{1,65},{33,97},{65,1},{97,33},{2,66}... | collective-permute-start | bytes 983048 | tf_op jit(solution)/shard_map/ppermute | solution.py:252
  115.2 15.4 %collective-permute-start.17 = (bf16[10,128,128]{2,1,0:T(8,128)(2,1)S(1)}, bf16[10,128,128]{2,1,0:T(8,128)(2,1)}, u32[]{:S(2)}, u32[]{:S(2)}) collective-permute-start(bf16[10,128,128]{2,1,0:T(8,128)(2,1)S(1)} %add_convert_fusion.refs_4_), channel_id=1, source_target_pairs={{0,96},{32,0},{64,32},{96,64},{1,97},{33,1},{65,33},{97,65},{2,98}... | collective-permute-start | bytes 983048 | tf_op jit(solution)/shard_map/ppermute | solution.py:252
  116.2 15.7 %copy-start.12 = (s32[5]{0:T(128)S(1)}, s32[5]{0:T(128)}, u32[]{:S(2)}) copy-start(s32[5]{0:T(128)} %stack.27.refs_0_) | copy-start | bytes 64
  116.2 15.7 %copy-start.13 = (s32[5]{0:T(128)S(1)}, s32[5]{0:T(128)}, u32[]{:S(2)}) copy-start(s32[5]{0:T(128)} %constant.37.clone) | copy-start | bytes 64
  123.4 11.2 %copy-start.7 = (bf16[10,128,128]{2,1,0:T(8,128)(2,1)}, bf16[10,128,128]{2,1,0:T(8,128)(2,1)S(1)}, u32[]{:S(2)}) copy-start(bf16[10,128,128]{2,1,0:T(8,128)(2,1)S(1)} %collective-permute-done.15.refs_5_) | copy-start | bytes 983044
  130.6 4.0 %collective-permute-start.19 = (bf16[20,256,128]{2,1,0:T(8,128)(2,1)S(1)}, bf16[20,256,128]{2,1,0:T(8,128)(2,1)S(1)}, u32[]{:S(2)}, u32[]{:S(2)}) collective-permute-start(bf16[20,256,128]{2,1,0:T(8,128)(2,1)S(1)} %all-to-all-done.3.refs_2_), channel_id=1, source_target_pairs={{0,1},{1,0},{2,3},{3,2},{4,5},{5,4},{6,7},{7,6},{8,9},{9,8},{10,11... | collective-permute-start | bytes 3932168 | tf_op jit(solution)/shard_map/ppermute | solution.py:252
  (6 other events, 8.9 us)

commit v3 on v2

--- a/solution.py
+++ b/solution.py
@@ -14,6 +14,7 @@
 ONE = HALF // Y
 TWO = PART // Z
 HBM = pl.BlockSpec(memory_space=pltpu.HBM)
+ANY = pl.BlockSpec(memory_space=pl.ANY)
 VMEM = pl.BlockSpec(memory_space=pltpu.VMEM)
 SMEM = pl.BlockSpec(memory_space=pltpu.SMEM)
 PARAMS = pltpu.CompilerParams(vmem_limit_bytes=60 * 2**20)
@@ -22,9 +23,9 @@
 def packed(size_ref, lo, hi):
     first, chunk, plan = 0, 0, []
     for s in range(size_ref.shape[0]):
-        blocks = (size_ref[s] + (WIDTH - 1)) // WIDTH
+        blocks = lax.shift_right_logical(size_ref[s] + (WIDTH - 1), 7)
         begin, end = jnp.clip(lo - first, 0, blocks), jnp.clip(hi - first, 0, blocks)
-        chunks = (end - begin + (CHUNK - 1)) // CHUNK
+        chunks = lax.shift_right_logical(end - begin + (CHUNK - 1), 2)
         plan.append((first, begin, end, chunk, chunks))
         first, chunk = first + blocks, chunk + chunks
     return plan, first
@@ -34,22 +35,13 @@
     return (slots + sectors * (CHUNK - 1)) // CHUNK
 
 
-def left_kernel(add, at_ref, size_ref, edge_ref, site_ref, *rest):
-    if add:
-        other_ref, out_ref, edge_buf, site_buf, edge_sem, site_sem, other_buf, other_sem = rest
-        other = pltpu.make_async_copy(other_ref, other_buf, other_sem)
-    else:
-        out_ref, edge_buf, site_buf, edge_sem, site_sem = rest
-    lo = at_ref[0]
-    plan, used = packed(size_ref, lo, lo + HALF)
-    last = site_ref.shape[2] // WIDTH - CHUNK
-
-    def block_of(s, c):
-        return jnp.minimum(plan[s][1] + c * CHUNK, last)
-
+def left_kernel(at_ref, size_ref, edge_ref, site_ref, *rest):
+    outs, (out_buf, edge_buf, site_buf, edge_sem, site_sem, out_sem) = rest[: 2 * CORE], rest[2 * CORE :]
+    core = at_ref[0]
+    plan, used = packed(size_ref, 0, 2 * PART)
     def fetch(s, c):
         at = plan[s][3] + c
-        columns = pl.ds(pl.multiple_of(block_of(s, c) * WIDTH, WIDTH), CHUNK * WIDTH)
+        columns = pl.ds(pl.multiple_of(c * (CHUNK * WIDTH), CHUNK * WIDTH), CHUNK * WIDTH)
         return pltpu.make_async_copy(site_ref.at[s, :, columns], site_buf.at[at], site_sem.at[at])
 
     edges = [pltpu.make_async_copy(edge_ref.at[s], edge_buf.at[s], edge_sem.at[s]) for s in range(len(plan))]
@@ -60,63 +52,61 @@
         def _(c):
             fetch(s, c).start()
 
-    if add:
-        other.start()
-
-    @pl.loop(jnp.clip(used - lo, 0, HALF), HALF)
-    def _(q):
-        out_ref[q] = jnp.zeros(out_ref.shape[1:], out_ref.dtype)
-
-    if add:
-        other.wait()
-    for s in range(len(plan)):
-        first, begin, end, chunk, chunks = plan[s]
+    for s in range(len(plan)):
+        first, _, _, chunk, chunks = plan[s]
         edges[s].wait()
 
         @pl.loop(0, chunks)
         def _(c):
             fetch(s, c).wait()
-            block = block_of(s, c)
             term = jnp.dot(edge_buf[s], site_buf[chunk + c], preferred_element_type=jnp.float32)
             for k in range(CHUNK):
-
-                @pl.when((block + k >= begin) & (block + k < end))
-                def _():
-                    q = first + block + k - lo
-                    part = term[:, k * WIDTH : (k + 1) * WIDTH]
-                    if add:
-                        part = part + other_buf[q].astype(jnp.float32)
-                    out_ref[q] = part.astype(out_ref.dtype)
-
-
-def left_terms(first_slot, sizes, edge, site, *other):
+                out_buf[first + c * CHUNK + k] = term[:, k * WIDTH : (k + 1) * WIDTH].astype(out_buf.dtype)
+
+    @pl.loop(used, 2 * PART)
+    def _(q):
+        out_buf[q] = jnp.zeros(out_buf.shape[1:], out_buf.dtype)
+
+    copies = [
+        pltpu.make_async_copy(
+            out_buf.at[pl.ds(part * PART + which * HALF, HALF)], outs[part * CORE + k], out_sem.at[part * CORE + k]
+        )
+        for part in range(2)
+        for k, which in enumerate((1 - core, core))
+    ]
+    for copy in copies:
+        copy.start()
+    for copy in copies:
+        copy.wait()
+
+
+def left_terms(core, sizes, edge, site):
     sectors, rows, depth = edge.shape
-    most = most_chunks(HALF, sectors)
-    add = bool(other)
-    slots = (HALF, rows, WIDTH)
+    most = most_chunks(2 * PART - 2, sectors)
     return pl.pallas_call(
-        lambda *refs: left_kernel(add, *refs),
-        out_shape=jax.ShapeDtypeStruct(slots, jnp.bfloat16),
-        in_specs=[SMEM, SMEM, HBM, HBM] + [HBM] * add,
-        out_specs=VMEM,
+        left_kernel,
+        out_shape=[jax.ShapeDtypeStruct((HALF, rows, WIDTH), jnp.bfloat16)] * (2 * CORE),
+        in_specs=[SMEM, SMEM, HBM, HBM],
+        out_specs=[ANY] * (2 * CORE),
         scratch_shapes=[
+            pltpu.VMEM((2 * PART + CHUNK, rows, WIDTH), jnp.bfloat16),
             pltpu.VMEM((sectors, rows, depth), jnp.bfloat16),
             pltpu.VMEM((most, depth, CHUNK * WIDTH), jnp.bfloat16),
             pltpu.SemaphoreType.DMA((sectors,)),
             pltpu.SemaphoreType.DMA((most,)),
-        ]
-        + [pltpu.VMEM(slots, jnp.bfloat16), pltpu.SemaphoreType.DMA] * add,
+            pltpu.SemaphoreType.DMA((2 * CORE,)),
+        ],
         compiler_params=PARAMS,
         cost_estimate=pl.CostEstimate(
-            flops=2 * HALF * rows * depth * WIDTH, bytes_accessed=6 * 2**20, transcendentals=0
+            flops=4 * PART * rows * depth * WIDTH, bytes_accessed=12 * 2**20, transcendentals=0
         ),
-        name="left_add" if add else "left",
-    )(first_slot.reshape(1).astype(jnp.int32), sizes, edge, site, *other)
-
-
-def right_kernel(at_ref, size_ref, edge_ref, site_ref, *rest):
+        name="left",
+    )(core.reshape(1).astype(jnp.int32), sizes, edge, site)
+
+
+def right_kernel(lo, at_ref, size_ref, edge_ref, site_ref, *rest):
     outs, (site_buf, edge_buf, term_buf, site_sem, edge_sem) = rest[:Z], rest[Z:]
-    lo, z = at_ref[0], at_ref[1]
+    z = at_ref[0]
     plan, _ = packed(size_ref, lo, lo + PART)
     last = edge_ref.shape[1] // WIDTH - CHUNK
 
@@ -130,7 +120,7 @@
 
     sites = [pltpu.make_async_copy(site_ref.at[s], site_buf.at[s], site_sem.at[s]) for s in range(len(plan))]
     for s in range(len(plan)):
-        sites[s].start()
+        pl.when(plan[s][4] > 0)(sites[s].start)
 
         @pl.loop(0, plan[s][4])
         def _(c):
@@ -138,7 +128,7 @@
 
     for s in range(len(plan)):
         first, _, _, chunk, chunks = plan[s]
-        sites[s].wait()
+        pl.when(chunks > 0)(sites[s].wait)
 
         @pl.loop(0, chunks)
         def _(c):
@@ -153,11 +143,11 @@
             outs[step][k : k + 2] = term_buf[pl.ds(base + k, 2)]
 
 
-def right_terms(first_slot, z, sizes, edge, site):
+def right_terms(part, z, sizes, edge, site):
     sectors, depth, cols = site.shape
     most = most_chunks(PART, sectors)
     return pl.pallas_call(
-        right_kernel,
+        lambda *refs: right_kernel(part, *refs),
         out_shape=[jax.ShapeDtypeStruct((TWO, WIDTH, cols), jnp.bfloat16)] * Z,
         in_specs=[SMEM, SMEM, HBM, HBM],
         out_specs=[VMEM] * Z,
@@ -173,16 +163,16 @@
             flops=2 * PART * WIDTH * depth * cols, bytes_accessed=10 * 2**20, transcendentals=0
         ),
         name="right",
-    )(jnp.stack([first_slot, z]).astype(jnp.int32), sizes, edge, site)
-
-
-def product_kernel(scale, at_ref, size_ref, own_ref, other_ref, *rest):
+    )(z.reshape(1).astype(jnp.int32), sizes, edge, site)
+
+
+def product_kernel(lo, scale, at_ref, size_ref, own_ref, other_ref, *rest):
     rights, rest = rest[:Z], rest[Z:]
     if scale is None:
         out_ref, one_buf, two_buf, sems = rest
     else:
         before_ref, out_ref, one_buf, two_buf, sems, before_buf = rest
-    lo, core, z, row_first, col_first = (at_ref[k] for k in range(5))
+    core, z, row_first, col_first = (at_ref[k] for k in range(4))
     plan, _ = packed(size_ref, lo, lo + PART)
     copies = [
         pltpu.make_async_copy(own_ref, one_buf.at[pl.ds(core * HALF, HALF)], sems.at[0]),
@@ -225,14 +215,14 @@
             out_ref[s] = jnp.where(live, total * jnp.float32(scale), jnp.float32(0.0)).astype(out_ref.dtype)
 
 
-def product(scale, at, sizes, own, other, rights, *before):
+def product(part, scale, at, sizes, own, other, rights, *before):
     rows, cols, sectors = own.shape[1], rights[0].shape[2], sizes.shape[0]
     shape = (sectors, rows, cols)
     end = bool(before)
     return pl.pallas_call(
-        lambda *refs: product_kernel(scale, *refs),
+        lambda *refs: product_kernel(part, scale, *refs),
         out_shape=jax.ShapeDtypeStruct(shape, jnp.bfloat16 if end else jnp.float32),
-        in_specs=[SMEM, SMEM] + [HBM] * (2 + Z + end),
+        in_specs=[SMEM, SMEM] + [ANY] * (2 + Z + end),
         out_specs=VMEM,
         scratch_shapes=[
             pltpu.VMEM((PART + CHUNK, rows, WIDTH), jnp.bfloat16),
@@ -283,56 +273,43 @@
     def left_copies(own):
         return jnp.broadcast_to(own[None], (Y,) + own.shape).reshape(HALF, rows, WIDTH)
 
-    def left_for_other(part, edges):
-        return left_terms(part + (1 - core) * HALF, sizes, *edges)
-
-    def left_chip(part, edges, came):
-        return left_terms(part + core * HALF, sizes, *edges, came)
-
-    left, right = (edge_left, site_left), (edge_right, site_right)
-    goes = left_for_other(A, left)
-    came = swap(goes, "core")
-    goes, right = fence((goes, right))
-    right_a = right_terms(jnp.int32(A), z, sizes, *right)
-    right_a, left, came = fence((right_a, left, came))
-    left_a = left_chip(A, left, came)
-
-    right_a, left_a, left, right = fence((right_a, left_a, left, right))
+    goes_a, keeps_a, goes_b, keeps_b = left_terms(core, sizes, edge_left, site_left)
+    came_a, came_b = swap(goes_a, "core"), swap(goes_b, "core")
+    goes_a, right = fence((goes_a, (edge_right, site_right)))
+    right_a = right_terms(A, z, sizes, *right)
+    right_a, right, came_a = fence((right_a, right, came_a))
+    left_a = total(keeps_a, came_a)
+
+    came_a = over_z(right_a)
+    left_a, right, keeps_b = fence((left_a, right, keeps_b))
     spread_a = over_y(left_a)
-    came_a = over_z(right_a)
-    goes = left_for_other(B, left)
-    came = swap(goes, "core")
-    goes, right = fence((goes, right))
-    right_b = right_terms(jnp.int32(B), z, sizes, *right)
-    right_b, left, came = fence((right_b, left, came))
-    left_b = left_chip(B, left, came)
+    right_b = right_terms(B, z, sizes, *right)
+    left_b = total(keeps_b, came_b)
     spread_a, came_a, right_b, left_b = fence((spread_a, came_a, right_b, left_b))
 
+    came_b = over_z(right_b)
     one_a, two_a = left_sums(spread_a), total(right_a[0], *came_a)
-    one_a, two_a, right_b, left_b = fence((one_a, two_a, right_b, left_b))
+    one_a, two_a, left_b = fence((one_a, two_a, left_b))
     spread_b = over_y(left_b)
-    came_b = over_z(right_b)
     one_x, two_x = swap(one_a, "xh"), swap(two_a, "xl")
     one_a, two_a = total(one_a, one_x), total(two_a, two_x)
+    spread_b, came_b, one_a, two_a = fence((spread_b, came_b, one_a, two_a))
+
+    rights_a = [two_a] + over_z([two_a] * Z)
     copies_a = left_copies(one_a)
-    spread_b, came_b, copies_a, two_a = fence((spread_b, came_b, copies_a, two_a))
-
     one_b, two_b = left_sums(spread_b), total(right_b[0], *came_b)
-    one_b, two_b, copies_a, two_a = fence((one_b, two_b, copies_a, two_a))
+    one_b, two_b, copies_a = fence((one_b, two_b, copies_a))
     half_a = over_y(copies_a)
-    rights_a = [two_a] + over_z([two_a] * Z)
     one_x, two_x = swap(one_b, "xh"), swap(two_b, "xl")
     one_b, two_b = total(one_b, one_x), total(two_b, two_x)
-    copies_b = left_copies(one_b)
-    half_a, rights_a, copies_b, two_b = fence((half_a, rights_a, copies_b, two_b))
-
-    at = jnp.stack([jnp.int32(A), core, z, row_first, col_first]).astype(jnp.int32)
-    half_b = over_y(copies_b)
+    half_a, rights_a, one_b, two_b = fence((half_a, rights_a, one_b, two_b))
+
     rights_b = [two_b] + over_z([two_b] * Z)
-    product_a = product(None, at, sizes, half_a, swap(half_a, "core"), rights_a)
+    at = jnp.stack([core, z, row_first, col_first]).astype(jnp.int32)
+    half_b = over_y(left_copies(one_b))
+    product_a = product(A, None, at, sizes, half_a, swap(half_a, "core"), rights_a)
     half_b, rights_b, product_a = fence((half_b, rights_b, product_a))
-    at = at + jnp.array([B - A, 0, 0, 0, 0], jnp.int32)
-    return product(order ** (-0.5), at, sizes, half_b, swap(half_b, "core"), rights_b, product_a)
+    return product(B, order ** (-0.5), at, sizes, half_b, swap(half_b, "core"), rights_b, product_a)
 
 
 def solution(mesh):

time: 143 us -> 137 us (0.958)
  Pallas kernels: 49.9 us -> 34.5 us
  waiting for transfers between devices: 36.7 us -> 46.9 us
  starting transfers between devices: 43.6 us -> 39.5 us
  other arithmetic: 4.18 us -> 7.81 us
    pallas_call x8 -> x5, Pallas kernels: 49.9 us -> 34.5 us  [the longest x2 12.8 us: product(): pl.pallas_call(lambda *refs: product_kernel(part, scale, *refs), out_shap...]
    ppermute x20, waiting for transfers between devices: 36.6 us -> 46.9 us  [shift(): lax.ppermute(array, axis, [(i, (i + step) % size) for i in range(size)])]
    convert_element_type x8 -> x10, other arithmetic: 3.03 us -> 7.2 us  [total(): sum((term.astype(jnp.float32) for term in terms)).astype(jnp.bfloat16)]
    ppermute x20, starting transfers between devices: 26.8 us -> 23.1 us  [shift(): lax.ppermute(array, axis, [(i, (i + step) % size) for i in range(size)])]
  transfers between devices with their start and end apart: 24 -> 24, of which waited for: 12 -> 11; matrix products, arithmetic and copies ran while one was open for 2% -> 5% of each run, Pallas kernels for 19% -> 14%
where the time goes in v3:
time: 137 us; the launch traced here: 136 us
  waiting for transfers between devices  46.9 us (34%)
  starting transfers between devices  39.5 us (29%)
  Pallas kernels  34.5 us (25%)
  other arithmetic  7.81 us (6%)
  local copies, waits for them, and re-layouts  6.83 us (5%)
    ppermute x20, waiting for transfers between devices, shift(): lax.ppermute(array, axis, [(i, (i + step) % size) for i in range(size)])  46.9 us
    ppermute x20, starting transfers between devices, shift(): lax.ppermute(array, axis, [(i, (i + step) % size) for i in range(size)])  23.1 us
    all_to_all x4, starting transfers between devices, over_y(): return lax.all_to_all(array, 'y', 0, 0, tiled=True)  16.4 us
    pallas_call x2, Pallas kernels, product(): pl.pallas_call(lambda *refs: product_kernel(part, scale, *refs), out_shap...  12.8 us
    pallas_call x2, Pallas kernels, right_terms(): pl.pallas_call(lambda *refs: right_kernel(part, *refs), out_shape=[jax.Sh...  12.5 us
    pallas_call x1, Pallas kernels, left_terms(): pl.pallas_call(left_kernel, out_shape=[jax.ShapeDtypeStruct((HALF, rows,...  9.06 us
    convert_element_type x10, other arithmetic, total(): sum((term.astype(jnp.float32) for term in terms)).astype(jnp.bfloat16)  7.2 us
    unnamed x28, local copies, waits for them, and re-layouts  4.09 us
  transfers between devices with their start and end apart: 24, of which 11 were waited for; matrix products, arithmetic and copies ran while one was open for 5% of the time, Pallas kernels for 14%

profile of v3, /device:TPU:1, one launch (start us, length us, event | category | flops | bytes accessed | tf_op | source)
XLA Modules:
  0.0 135.9 jit_solution(11084778068813747027)
XLA Ops:
  0.0 9.1 %left.1 = (bf16[20,256,128]{2,1,0:T(8,128)(2,1)}, bf16[20,256,128]{2,1,0:T(8,128)(2,1)}, bf16[20,256,128]{2,1,0:T(8,128)(2,1)}, bf16[20,256,128]{2,1,0:T(8,128)(2,1)}) custom-call(s32[1]{0:T(128)} %bitcast.at_ref, s32[8]{0:T(128)} %refs_1_.7, bf16[8,256,256]{2,1,0:T(8,128)(2,1)} %edge_ref.1, bf16[8,256,2048]{2,1,0:T(8,128)(2,1)} %site_ref.1), custom_call_target="tpu_custom_call" | custom-call | flops 1342177280 | bytes 12582912 | tf_op jit(solution)/shard_map/left/pallas_call | solution.py:86
  9.1 1.5 %collective-permute-start = (bf16[20,256,128]{2,1,0:T(8,128)(2,1)}, bf16[20,256,128]{2,1,0:T(8,128)(2,1)S(1)}, u32[]{:S(2)}, u32[]{:S(2)}) collective-permute-start(bf16[20,256,128]{2,1,0:T(8,128)(2,1)} %get-tuple-element.65), channel_id=1, source_target_pairs={{0,1},{1,0},{2,3},{3,2},{4,5},{5,4},{6,7},{7,6},{8,9},{9,8},{10,11... | collective-permute-start | bytes 3932168 | tf_op jit(solution)/shard_map/ppermute | solution.py:242
  10.7 6.4 %right.2 = (bf16[10,128,128]{2,1,0:T(8,128)(2,1)}, bf16[10,128,128]{2,1,0:T(8,128)(2,1)}, bf16[10,128,128]{2,1,0:T(8,128)(2,1)}, bf16[10,128,128]{2,1,0:T(8,128)(2,1)}) custom-call(s32[1]{0:T(128)} %bitcast.1.refs_0_, s32[8]{0:T(128)} %refs_1_.7, bf16[8,2048,512]{2,1,0:T(8,128)(2,1)} %refs_2_.1, bf16[8,512,128]{2,1,0:T(8,128)(2,1)} %refs_3_.1), custom_call_target="tpu_custom_call" | custom-call | flops 671088640 | bytes 10485760 | tf_op jit(solution)/shard_map/right/pallas_call | solution.py:149
  17.1 1.4 %add_convert_fusion.1 = bf16[20,256,128]{2,1,0:T(8,128)(2,1)} fusion(bf16[20,256,128]{2,1,0:T(8,128)(2,1)S(1)} %collective-permute-done, bf16[20,256,128]{2,1,0:T(8,128)(2,1)S(1)} %copy-done.4), kind=kLoop, calls=%fused_computation.1 | loop fusion | flops 2621440 | bytes 3932160 | tf_op jit(solution)/shard_map/convert_element_type | solution.py:246
  18.5 4.3 %all-to-all-start = ((bf16[20,256,128]{2,1,0:T(8,128)(2,1)}), bf16[20,256,128]{2,1,0:T(8,128)(2,1)S(1)}, u32[]{:S(2)}, u32[]{:S(2)}) async-start(bf16[20,256,128]{2,1,0:T(8,128)(2,1)} %add_convert_fusion.1), calls=%async_computation | async-start | bytes 2621440 | tf_op jit(solution)/shard_map/all_to_all | solution.py:254
  22.8 1.6 %collective-permute-start.1 = (bf16[10,128,128]{2,1,0:T(8,128)(2,1)}, bf16[10,128,128]{2,1,0:T(8,128)(2,1)S(1)}, u32[]{:S(2)}, u32[]{:S(2)}) collective-permute-start(bf16[10,128,128]{2,1,0:T(8,128)(2,1)} %get-tuple-element.77), channel_id=1, source_target_pairs={{0,32},{32,64},{64,96},{96,0},{1,33},{33,65},{65,97},{97,1},{2,34}... | collective-permute-start | bytes 983048 | tf_op jit(solution)/shard_map/ppermute | solution.py:242
  24.4 3.3 %collective-permute-start.2 = (bf16[10,128,128]{2,1,0:T(8,128)(2,1)}, bf16[10,128,128]{2,1,0:T(8,128)(2,1)S(1)}, u32[]{:S(2)}, u32[]{:S(2)}) collective-permute-start(bf16[10,128,128]{2,1,0:T(8,128)(2,1)} %get-tuple-element.78), channel_id=1, source_target_pairs={{0,64},{32,96},{64,0},{96,32},{1,65},{33,97},{65,1},{97,33},{2,66}... | collective-permute-start | bytes 983048 | tf_op jit(solution)/shard_map/ppermute | solution.py:242
  28.4 6.2 %right.3 = (bf16[10,128,128]{2,1,0:T(8,128)(2,1)}, bf16[10,128,128]{2,1,0:T(8,128)(2,1)}, bf16[10,128,128]{2,1,0:T(8,128)(2,1)}, bf16[10,128,128]{2,1,0:T(8,128)(2,1)}) custom-call(s32[1]{0:T(128)} %bitcast.1.refs_0_, s32[8]{0:T(128)} %refs_1_.7, bf16[8,2048,512]{2,1,0:T(8,128)(2,1)} %refs_2_.1, bf16[8,512,128]{2,1,0:T(8,128)(2,1)} %refs_3_.1), custom_call_target="tpu_custom_call" | custom-call | flops 671088640 | bytes 10485760 | tf_op jit(solution)/shard_map/right/pallas_call | solution.py:149
  34.6 2.7 %add_convert_fusion = bf16[20,256,128]{2,1,0:T(8,128)(2,1)} fusion(bf16[20,256,128]{2,1,0:T(8,128)(2,1)} %collective-permute-done.4, bf16[20,256,128]{2,1,0:T(8,128)(2,1)S(1)} %copy-done.3), kind=kLoop, calls=%fused_computation | loop fusion | flops 2621440 | bytes 3932160 | tf_op jit(solution)/shard_map/convert_element_type | solution.py:246
  37.4 4.7 %collective-permute-done.2 = bf16[10,128,128]{2,1,0:T(8,128)(2,1)S(1)} collective-permute-done((bf16[10,128,128]{2,1,0:T(8,128)(2,1)}, bf16[10,128,128]{2,1,0:T(8,128)(2,1)S(1)}, u32[]{:S(2)}, u32[]{:S(2)}) %collective-permute-start.2) | collective-permute-done | bytes 327712 | tf_op jit(solution)/shard_map/ppermute | solution.py:242
  42.3 1.2 add_convert_fusion.8
  43.4 3.9 %all-to-all-start.1 = ((bf16[20,256,128]{2,1,0:T(8,128)(2,1)}), bf16[20,256,128]{2,1,0:T(8,128)(2,1)S(1)}, u32[]{:S(2)}, u32[]{:S(2)}) async-start(bf16[20,256,128]{2,1,0:T(8,128)(2,1)} %add_convert_fusion), calls=%async_computation.1 | async-start | bytes 2621440 | tf_op jit(solution)/shard_map/all_to_all | solution.py:254
  47.3 2.7 %collective-permute-start.8 = (bf16[5,256,128]{2,1,0:T(8,128)(2,1)S(1)}, bf16[5,256,128]{2,1,0:T(8,128)(2,1)S(1)}, u32[]{:S(2)}, u32[]{:S(2)}) collective-permute-start(bf16[5,256,128]{2,1,0:T(8,128)(2,1)S(1)} %add_convert_fusion.9), channel_id=1, source_target_pairs={{0,2},{2,0},{1,3},{3,1},{4,6},{6,4},{5,7},{7,5},{8,10},{10,8},{9,1... | collective-permute-start | bytes 983048 | tf_op jit(solution)/shard_map/ppermute | solution.py:242
  50.4 1.9 %collective-permute-start.5 = (bf16[10,128,128]{2,1,0:T(8,128)(2,1)}, bf16[10,128,128]{2,1,0:T(8,128)(2,1)S(1)}, u32[]{:S(2)}, u32[]{:S(2)}) collective-permute-start(bf16[10,128,128]{2,1,0:T(8,128)(2,1)} %get-tuple-element.95), channel_id=1, source_target_pairs={{0,32},{32,64},{64,96},{96,0},{1,33},{33,65},{65,97},{97,1},{2,34}... | collective-permute-start | bytes 983048 | tf_op jit(solution)/shard_map/ppermute | solution.py:242
  52.3 2.6 %collective-permute-start.6 = (bf16[10,128,128]{2,1,0:T(8,128)(2,1)}, bf16[10,128,128]{2,1,0:T(8,128)(2,1)S(1)}, u32[]{:S(2)}, u32[]{:S(2)}) collective-permute-start(bf16[10,128,128]{2,1,0:T(8,128)(2,1)} %get-tuple-element.96), channel_id=1, source_target_pairs={{0,64},{32,96},{64,0},{96,32},{1,65},{33,97},{65,1},{97,33},{2,66}... | collective-permute-start | bytes 983048 | tf_op jit(solution)/shard_map/ppermute | solution.py:242
  56.0 7.0 %collective-permute-done.9 = bf16[10,128,128]{2,1,0:T(8,128)(2,1)S(1)} collective-permute-done((bf16[10,128,128]{2,1,0:T(8,128)(2,1)S(1)}, bf16[10,128,128]{2,1,0:T(8,128)(2,1)S(1)}, u32[]{:S(2)}, u32[]{:S(2)}) %collective-permute-start.9) | collective-permute-done | bytes 327712 | tf_op jit(solution)/shard_map/ppermute | solution.py:242
  63.1 5.4 %collective-permute-done.6 = bf16[10,128,128]{2,1,0:T(8,128)(2,1)S(1)} collective-permute-done((bf16[10,128,128]{2,1,0:T(8,128)(2,1)}, bf16[10,128,128]{2,1,0:T(8,128)(2,1)S(1)}, u32[]{:S(2)}, u32[]{:S(2)}) %collective-permute-start.6) | collective-permute-done | bytes 327712 | tf_op jit(solution)/shard_map/ppermute | solution.py:242
  71.4 1.4 %broadcast_in_dim.4 = bf16[4,5,256,128]{3,2,1,0:T(8,128)(2,1)} broadcast(bf16[5,256,128]{2,1,0:T(8,128)(2,1)S(1)} %add_convert_fusion.7), dimensions={1,2,3} | broadcast | bytes 1638400 | tf_op jit(solution)/shard_map/broadcast_in_dim | solution.py:274
  72.7 4.0 %all-to-all-start.2 = ((bf16[20,256,128]{2,1,0:T(8,128)(2,1)}), bf16[20,256,128]{2,1,0:T(8,128)(2,1)S(1)}, u32[]{:S(2)}, u32[]{:S(2)}) async-start(bf16[20,256,128]{2,1,0:T(8,128)(2,1)} %bitcast.4), calls=%async_computation.2 | async-start | bytes 2621440 | tf_op jit(solution)/shard_map/all_to_all | solution.py:254
  76.7 1.7 %collective-permute-start.13 = (bf16[5,256,128]{2,1,0:T(8,128)(2,1)S(1)}, bf16[5,256,128]{2,1,0:T(8,128)(2,1)S(1)}, u32[]{:S(2)}, u32[]{:S(2)}) collective-permute-start(bf16[5,256,128]{2,1,0:T(8,128)(2,1)S(1)} %add_convert_fusion.5), channel_id=1, source_target_pairs={{0,2},{2,0},{1,3},{3,1},{4,6},{6,4},{5,7},{7,5},{8,10},{10,8},{9,1... | collective-permute-start | bytes 983048 | tf_op jit(solution)/shard_map/ppermute | solution.py:242
  78.4 2.9 %collective-permute-start.12 = (bf16[10,128,128]{2,1,0:T(8,128)(2,1)S(1)}, bf16[10,128,128]{2,1,0:T(8,128)(2,1)S(1)}, u32[]{:S(2)}, u32[]{:S(2)}) collective-permute-start(bf16[10,128,128]{2,1,0:T(8,128)(2,1)S(1)} %add_convert_fusion.6.refs_4_), channel_id=1, source_target_pairs={{0,96},{32,0},{64,32},{96,64},{1,97},{33,1},{65,33},{97,65},{2,98}... | collective-permute-start | bytes 983048 | tf_op jit(solution)/shard_map/ppermute | solution.py:242
  81.9 2.7 %collective-permute-done.13 = bf16[5,256,128]{2,1,0:T(8,128)(2,1)S(1)} collective-permute-done((bf16[5,256,128]{2,1,0:T(8,128)(2,1)S(1)}, bf16[5,256,128]{2,1,0:T(8,128)(2,1)S(1)}, u32[]{:S(2)}, u32[]{:S(2)}) %collective-permute-start.13) | collective-permute-done | bytes 327712 | tf_op jit(solution)/shard_map/ppermute | solution.py:242
  84.7 5.6 %collective-permute-done.14 = bf16[10,128,128]{2,1,0:T(8,128)(2,1)S(1)} collective-permute-done((bf16[10,128,128]{2,1,0:T(8,128)(2,1)S(1)}, bf16[10,128,128]{2,1,0:T(8,128)(2,1)S(1)}, u32[]{:S(2)}, u32[]{:S(2)}) %collective-permute-start.14) | collective-permute-done | bytes 327712 | tf_op jit(solution)/shard_map/ppermute | solution.py:242
  91.9 7.6 %collective-permute-done.10.refs_5_ = bf16[10,128,128]{2,1,0:T(8,128)(2,1)} collective-permute-done((bf16[10,128,128]{2,1,0:T(8,128)(2,1)S(1)}, bf16[10,128,128]{2,1,0:T(8,128)(2,1)}, u32[]{:S(2)}, u32[]{:S(2)}) %collective-permute-start.10) | collective-permute-done | bytes 327712 | tf_op jit(solution)/shard_map/ppermute | solution.py:242
  100.1 1.4 %broadcast_in_dim.5 = bf16[4,5,256,128]{3,2,1,0:T(8,128)(2,1)} broadcast(bf16[5,256,128]{2,1,0:T(8,128)(2,1)S(1)} %add_convert_fusion.3), dimensions={1,2,3} | broadcast | bytes 1638400 | tf_op jit(solution)/shard_map/broadcast_in_dim | solution.py:274
  101.4 4.2 %all-to-all-start.3 = ((bf16[20,256,128]{2,1,0:T(8,128)(2,1)}), bf16[20,256,128]{2,1,0:T(8,128)(2,1)S(1)}, u32[]{:S(2)}, u32[]{:S(2)}) async-start(bf16[20,256,128]{2,1,0:T(8,128)(2,1)} %bitcast.5), calls=%async_computation.3 | async-start | bytes 2621440 | tf_op jit(solution)/shard_map/all_to_all | solution.py:254
  105.7 1.3 collective-permute-start.17
  108.2 6.3 %product.1.refs_8_ = f32[8,256,128]{2,1,0:T(8,128)} custom-call(s32[4]{0:T(128)} %pad_add_fusion.refs_0_, s32[8]{0:T(128)} %refs_1_.7, bf16[20,256,128]{2,1,0:T(8,128)(2,1)} %copy-done, bf16[20,256,128]{2,1,0:T(8,128)(2,1)} %collective-permute-done.18.refs_3_, bf16[10,128,128]{2,1,0:T(8,128)(2,1)} %copy-done.6, ...), custom_call_target="tpu_custom_call" | custom-call | flops 335544320 | bytes 6291456 | tf_op jit(solution)/shard_map/product/pallas_call | solution.py:222
  114.6 2.7 %collective-permute-done.16.refs_6_ = bf16[10,128,128]{2,1,0:T(8,128)(2,1)} collective-permute-done((bf16[10,128,128]{2,1,0:T(8,128)(2,1)S(1)}, bf16[10,128,128]{2,1,0:T(8,128)(2,1)}, u32[]{:S(2)}, u32[]{:S(2)}) %collective-permute-start.16) | collective-permute-done | bytes 327712 | tf_op jit(solution)/shard_map/ppermute | solution.py:242
  117.4 7.3 %collective-permute-done.15.refs_5_ = bf16[10,128,128]{2,1,0:T(8,128)(2,1)} collective-permute-done((bf16[10,128,128]{2,1,0:T(8,128)(2,1)S(1)}, bf16[10,128,128]{2,1,0:T(8,128)(2,1)}, u32[]{:S(2)}, u32[]{:S(2)}) %collective-permute-start.15) | collective-permute-done | bytes 327712 | tf_op jit(solution)/shard_map/ppermute | solution.py:242
  125.5 2.7 %collective-permute-done.19.refs_3_ = bf16[20,256,128]{2,1,0:T(8,128)(2,1)S(1)} collective-permute-done((bf16[20,256,128]{2,1,0:T(8,128)(2,1)S(1)}, bf16[20,256,128]{2,1,0:T(8,128)(2,1)S(1)}, u32[]{:S(2)}, u32[]{:S(2)}) %collective-permute-start.19) | collective-permute-done | bytes 1310752 | tf_op jit(solution)/shard_map/ppermute | solution.py:242
  129.2 6.6 %product_end.1 = bf16[8,256,128]{2,1,0:T(8,128)(2,1)} custom-call(s32[4]{0:T(128)} %pad_add_fusion.refs_0_, s32[8]{0:T(128)} %refs_1_.7, bf16[20,256,128]{2,1,0:T(8,128)(2,1)} %copy-done.1, bf16[20,256,128]{2,1,0:T(8,128)(2,1)} %copy-done.5, bf16[10,128,128]{2,1,0:T(8,128)(2,1)} %copy-done.2, bf16[10,128,128]{2,1,0:T(8,128)(2,1)} %collective-permute-done.15.refs_5_, ...), custom_call_target="tpu_custom_call" | custom-call | flops 335544320 | bytes 6291456 | tf_op jit(solution)/shard_map/product_end/pallas_call | solution.py:222
  (62 shorter events, 11.4 us)
Async XLA Ops:
  9.1 8.0 %collective-permute-start = (bf16[20,256,128]{2,1,0:T(8,128)(2,1)}, bf16[20,256,128]{2,1,0:T(8,128)(2,1)S(1)}, u32[]{:S(2)}, u32[]{:S(2)}) collective-permute-start(bf16[20,256,128]{2,1,0:T(8,128)(2,1)} %get-tuple-element.65), channel_id=1, source_target_pairs={{0,1},{1,0},{2,3},{3,2},{4,5},{5,4},{6,7},{7,6},{8,9},{9,8},{10,11... | collective-permute-start | bytes 3932168 | tf_op jit(solution)/shard_map/ppermute | solution.py:242
  10.6 24.0 %collective-permute-start.4 = (bf16[20,256,128]{2,1,0:T(8,128)(2,1)}, bf16[20,256,128]{2,1,0:T(8,128)(2,1)}, u32[]{:S(2)}, u32[]{:S(2)}) collective-permute-start(bf16[20,256,128]{2,1,0:T(8,128)(2,1)} %get-tuple-element.87), channel_id=1, source_target_pairs={{0,1},{1,0},{2,3},{3,2},{4,5},{5,4},{6,7},{7,6},{8,9},{9,8},{10,11... | collective-permute-start | bytes 3932168 | tf_op jit(solution)/shard_map/ppermute | solution.py:242
  10.7 6.4 %copy-start.4 = (bf16[20,256,128]{2,1,0:T(8,128)(2,1)S(1)}, bf16[20,256,128]{2,1,0:T(8,128)(2,1)}, u32[]{:S(2)}) copy-start(bf16[20,256,128]{2,1,0:T(8,128)(2,1)} %get-tuple-element.64) | copy-start | bytes 3932164
  18.5 23.6 %all-to-all-start = ((bf16[20,256,128]{2,1,0:T(8,128)(2,1)}), bf16[20,256,128]{2,1,0:T(8,128)(2,1)S(1)}, u32[]{:S(2)}, u32[]{:S(2)}) async-start(bf16[20,256,128]{2,1,0:T(8,128)(2,1)} %add_convert_fusion.1), calls=%async_computation | async-start | bytes 2621440 | tf_op jit(solution)/shard_map/all_to_all | solution.py:254
  22.8 11.8 %copy-start.3 = (bf16[20,256,128]{2,1,0:T(8,128)(2,1)S(1)}, bf16[20,256,128]{2,1,0:T(8,128)(2,1)}, u32[]{:S(2)}) copy-start(bf16[20,256,128]{2,1,0:T(8,128)(2,1)} %get-tuple-element.86) | copy-start | bytes 3932164
  22.8 14.6 %collective-permute-start.1 = (bf16[10,128,128]{2,1,0:T(8,128)(2,1)}, bf16[10,128,128]{2,1,0:T(8,128)(2,1)S(1)}, u32[]{:S(2)}, u32[]{:S(2)}) collective-permute-start(bf16[10,128,128]{2,1,0:T(8,128)(2,1)} %get-tuple-element.77), channel_id=1, source_target_pairs={{0,32},{32,64},{64,96},{96,0},{1,33},{33,65},{65,97},{97,1},{2,34}... | collective-permute-start | bytes 983048 | tf_op jit(solution)/shard_map/ppermute | solution.py:242
  24.4 17.6 %collective-permute-start.2 = (bf16[10,128,128]{2,1,0:T(8,128)(2,1)}, bf16[10,128,128]{2,1,0:T(8,128)(2,1)S(1)}, u32[]{:S(2)}, u32[]{:S(2)}) collective-permute-start(bf16[10,128,128]{2,1,0:T(8,128)(2,1)} %get-tuple-element.78), channel_id=1, source_target_pairs={{0,64},{32,96},{64,0},{96,32},{1,65},{33,97},{65,1},{97,33},{2,66}... | collective-permute-start | bytes 983048 | tf_op jit(solution)/shard_map/ppermute | solution.py:242
  27.7 14.3 %collective-permute-start.3 = (bf16[10,128,128]{2,1,0:T(8,128)(2,1)}, bf16[10,128,128]{2,1,0:T(8,128)(2,1)}, u32[]{:S(2)}, u32[]{:S(2)}) collective-permute-start(bf16[10,128,128]{2,1,0:T(8,128)(2,1)} %get-tuple-element.79), channel_id=1, source_target_pairs={{0,96},{32,0},{64,32},{96,64},{1,97},{33,1},{65,33},{97,65},{2,98}... | collective-permute-start | bytes 983048 | tf_op jit(solution)/shard_map/ppermute | solution.py:242
  37.4 4.9 %copy-start.9 = (bf16[10,128,128]{2,1,0:T(8,128)(2,1)S(1)}, bf16[10,128,128]{2,1,0:T(8,128)(2,1)}, u32[]{:S(2)}) copy-start(bf16[10,128,128]{2,1,0:T(8,128)(2,1)} %get-tuple-element.89) | copy-start | bytes 983044
  43.4 25.8 %all-to-all-start.1 = ((bf16[20,256,128]{2,1,0:T(8,128)(2,1)}), bf16[20,256,128]{2,1,0:T(8,128)(2,1)S(1)}, u32[]{:S(2)}, u32[]{:S(2)}) async-start(bf16[20,256,128]{2,1,0:T(8,128)(2,1)} %add_convert_fusion), calls=%async_computation.1 | async-start | bytes 2621440 | tf_op jit(solution)/shard_map/all_to_all | solution.py:254
  47.3 8.6 %collective-permute-start.8 = (bf16[5,256,128]{2,1,0:T(8,128)(2,1)S(1)}, bf16[5,256,128]{2,1,0:T(8,128)(2,1)S(1)}, u32[]{:S(2)}, u32[]{:S(2)}) collective-permute-start(bf16[5,256,128]{2,1,0:T(8,128)(2,1)S(1)} %add_convert_fusion.9), channel_id=1, source_target_pairs={{0,2},{2,0},{1,3},{3,1},{4,6},{6,4},{5,7},{7,5},{8,10},{10,8},{9,1... | collective-permute-start | bytes 983048 | tf_op jit(solution)/shard_map/ppermute | solution.py:242
  50.1 12.9 %collective-permute-start.9 = (bf16[10,128,128]{2,1,0:T(8,128)(2,1)S(1)}, bf16[10,128,128]{2,1,0:T(8,128)(2,1)S(1)}, u32[]{:S(2)}, u32[]{:S(2)}) collective-permute-start(bf16[10,128,128]{2,1,0:T(8,128)(2,1)S(1)} %add_convert_fusion.8), channel_id=1, source_target_pairs={{0,16},{16,0},{1,17},{17,1},{2,18},{18,2},{3,19},{19,3},{4,20},{20... | collective-permute-start | bytes 983048 | tf_op jit(solution)/shard_map/ppermute | solution.py:242
  50.4 12.7 %collective-permute-start.5 = (bf16[10,128,128]{2,1,0:T(8,128)(2,1)}, bf16[10,128,128]{2,1,0:T(8,128)(2,1)S(1)}, u32[]{:S(2)}, u32[]{:S(2)}) collective-permute-start(bf16[10,128,128]{2,1,0:T(8,128)(2,1)} %get-tuple-element.95), channel_id=1, source_target_pairs={{0,32},{32,64},{64,96},{96,0},{1,33},{33,65},{65,97},{97,1},{2,34}... | collective-permute-start | bytes 983048 | tf_op jit(solution)/shard_map/ppermute | solution.py:242
  52.3 16.2 %collective-permute-start.6 = (bf16[10,128,128]{2,1,0:T(8,128)(2,1)}, bf16[10,128,128]{2,1,0:T(8,128)(2,1)S(1)}, u32[]{:S(2)}, u32[]{:S(2)}) collective-permute-start(bf16[10,128,128]{2,1,0:T(8,128)(2,1)} %get-tuple-element.96), channel_id=1, source_target_pairs={{0,64},{32,96},{64,0},{96,32},{1,65},{33,97},{65,1},{97,33},{2,66}... | collective-permute-start | bytes 983048 | tf_op jit(solution)/shard_map/ppermute | solution.py:242
  54.9 14.4 %collective-permute-start.7 = (bf16[10,128,128]{2,1,0:T(8,128)(2,1)}, bf16[10,128,128]{2,1,0:T(8,128)(2,1)}, u32[]{:S(2)}, u32[]{:S(2)}) collective-permute-start(bf16[10,128,128]{2,1,0:T(8,128)(2,1)} %get-tuple-element.97), channel_id=1, source_target_pairs={{0,96},{32,0},{64,32},{96,64},{1,97},{33,1},{65,33},{97,65},{2,98}... | collective-permute-start | bytes 983048 | tf_op jit(solution)/shard_map/ppermute | solution.py:242
  56.0 13.4 %copy-start.8 = (bf16[10,128,128]{2,1,0:T(8,128)(2,1)S(1)}, bf16[10,128,128]{2,1,0:T(8,128)(2,1)}, u32[]{:S(2)}) copy-start(bf16[10,128,128]{2,1,0:T(8,128)(2,1)} %get-tuple-element.101) | copy-start | bytes 983044
  63.1 18.7 %copy-start.6 = (bf16[10,128,128]{2,1,0:T(8,128)(2,1)}, bf16[10,128,128]{2,1,0:T(8,128)(2,1)S(1)}, u32[]{:S(2)}) copy-start(bf16[10,128,128]{2,1,0:T(8,128)(2,1)S(1)} %add_convert_fusion.6.refs_4_) | copy-start | bytes 983044
  72.7 26.8 %all-to-all-start.2 = ((bf16[20,256,128]{2,1,0:T(8,128)(2,1)}), bf16[20,256,128]{2,1,0:T(8,128)(2,1)S(1)}, u32[]{:S(2)}, u32[]{:S(2)}) async-start(bf16[20,256,128]{2,1,0:T(8,128)(2,1)} %bitcast.4), calls=%async_computation.2 | async-start | bytes 2621440 | tf_op jit(solution)/shard_map/all_to_all | solution.py:254
  76.7 7.9 %collective-permute-start.13 = (bf16[5,256,128]{2,1,0:T(8,128)(2,1)S(1)}, bf16[5,256,128]{2,1,0:T(8,128)(2,1)S(1)}, u32[]{:S(2)}, u32[]{:S(2)}) collective-permute-start(bf16[5,256,128]{2,1,0:T(8,128)(2,1)S(1)} %add_convert_fusion.5), channel_id=1, source_target_pairs={{0,2},{2,0},{1,3},{3,1},{4,6},{6,4},{5,7},{7,5},{8,10},{10,8},{9,1... | collective-permute-start | bytes 983048 | tf_op jit(solution)/shard_map/ppermute | solution.py:242
  78.4 11.9 %collective-permute-start.14 = (bf16[10,128,128]{2,1,0:T(8,128)(2,1)S(1)}, bf16[10,128,128]{2,1,0:T(8,128)(2,1)S(1)}, u32[]{:S(2)}, u32[]{:S(2)}) collective-permute-start(bf16[10,128,128]{2,1,0:T(8,128)(2,1)S(1)} %add_convert_fusion.4), channel_id=1, source_target_pairs={{0,16},{16,0},{1,17},{17,1},{2,18},{18,2},{3,19},{19,3},{4,20},{20... | collective-permute-start | bytes 983048 | tf_op jit(solution)/shard_map/ppermute | solution.py:242
  78.4 12.0 %collective-permute-start.12 = (bf16[10,128,128]{2,1,0:T(8,128)(2,1)S(1)}, bf16[10,128,128]{2,1,0:T(8,128)(2,1)S(1)}, u32[]{:S(2)}, u32[]{:S(2)}) collective-permute-start(bf16[10,128,128]{2,1,0:T(8,128)(2,1)S(1)} %add_convert_fusion.6.refs_4_), channel_id=1, source_target_pairs={{0,96},{32,0},{64,32},{96,64},{1,97},{33,1},{65,33},{97,65},{2,98}... | collective-permute-start | bytes 983048 | tf_op jit(solution)/shard_map/ppermute | solution.py:242
  81.3 9.2 %collective-permute-start.11 = (bf16[10,128,128]{2,1,0:T(8,128)(2,1)S(1)}, bf16[10,128,128]{2,1,0:T(8,128)(2,1)S(1)}, u32[]{:S(2)}, u32[]{:S(2)}) collective-permute-start(bf16[10,128,128]{2,1,0:T(8,128)(2,1)S(1)} %add_convert_fusion.6.refs_4_), channel_id=1, source_target_pairs={{0,64},{32,96},{64,0},{96,32},{1,65},{33,97},{65,1},{97,33},{2,66}... | collective-permute-start | bytes 983048 | tf_op jit(solution)/shard_map/ppermute | solution.py:242
  81.8 17.7 %collective-permute-start.10 = (bf16[10,128,128]{2,1,0:T(8,128)(2,1)S(1)}, bf16[10,128,128]{2,1,0:T(8,128)(2,1)}, u32[]{:S(2)}, u32[]{:S(2)}) collective-permute-start(bf16[10,128,128]{2,1,0:T(8,128)(2,1)S(1)} %add_convert_fusion.6.refs_4_), channel_id=1, source_target_pairs={{0,32},{32,64},{64,96},{96,0},{1,33},{33,65},{65,97},{97,1},{2,34}... | collective-permute-start | bytes 983048 | tf_op jit(solution)/shard_map/ppermute | solution.py:242
  90.4 16.6 %copy-start.2 = (bf16[10,128,128]{2,1,0:T(8,128)(2,1)}, bf16[10,128,128]{2,1,0:T(8,128)(2,1)S(1)}, u32[]{:S(2)}) copy-start(bf16[10,128,128]{2,1,0:T(8,128)(2,1)S(1)} %add_convert_fusion.2.refs_4_) | copy-start | bytes 983044
  99.6 8.6 %collective-permute-start.18 = (bf16[20,256,128]{2,1,0:T(8,128)(2,1)S(1)}, bf16[20,256,128]{2,1,0:T(8,128)(2,1)}, u32[]{:S(2)}, u32[]{:S(2)}) collective-permute-start(bf16[20,256,128]{2,1,0:T(8,128)(2,1)S(1)} %all-to-all-done.2.refs_2_), channel_id=1, source_target_pairs={{0,1},{1,0},{2,3},{3,2},{4,5},{5,4},{6,7},{7,6},{8,9},{9,8},{10,11... | collective-permute-start | bytes 3932168 | tf_op jit(solution)/shard_map/ppermute | solution.py:242
  101.4 23.2 %all-to-all-start.3 = ((bf16[20,256,128]{2,1,0:T(8,128)(2,1)}), bf16[20,256,128]{2,1,0:T(8,128)(2,1)S(1)}, u32[]{:S(2)}, u32[]{:S(2)}) async-start(bf16[20,256,128]{2,1,0:T(8,128)(2,1)} %bitcast.5), calls=%async_computation.3 | async-start | bytes 2621440 | tf_op jit(solution)/shard_map/all_to_all | solution.py:254
  105.7 9.0 %collective-permute-start.17 = (bf16[10,128,128]{2,1,0:T(8,128)(2,1)S(1)}, bf16[10,128,128]{2,1,0:T(8,128)(2,1)S(1)}, u32[]{:S(2)}, u32[]{:S(2)}) collective-permute-start(bf16[10,128,128]{2,1,0:T(8,128)(2,1)S(1)} %add_convert_fusion.2.refs_4_), channel_id=1, source_target_pairs={{0,96},{32,0},{64,32},{96,64},{1,97},{33,1},{65,33},{97,65},{2,98}... | collective-permute-start | bytes 983048 | tf_op jit(solution)/shard_map/ppermute | solution.py:242
  107.0 10.4 %collective-permute-start.16 = (bf16[10,128,128]{2,1,0:T(8,128)(2,1)S(1)}, bf16[10,128,128]{2,1,0:T(8,128)(2,1)}, u32[]{:S(2)}, u32[]{:S(2)}) collective-permute-start(bf16[10,128,128]{2,1,0:T(8,128)(2,1)S(1)} %add_convert_fusion.2.refs_4_), channel_id=1, source_target_pairs={{0,64},{32,96},{64,0},{96,32},{1,65},{33,97},{65,1},{97,33},{2,66}... | collective-permute-start | bytes 983048 | tf_op jit(solution)/shard_map/ppermute | solution.py:242
  107.0 17.7 %collective-permute-start.15 = (bf16[10,128,128]{2,1,0:T(8,128)(2,1)S(1)}, bf16[10,128,128]{2,1,0:T(8,128)(2,1)}, u32[]{:S(2)}, u32[]{:S(2)}) collective-permute-start(bf16[10,128,128]{2,1,0:T(8,128)(2,1)S(1)} %add_convert_fusion.2.refs_4_), channel_id=1, source_target_pairs={{0,32},{32,64},{64,96},{96,0},{1,33},{33,65},{65,97},{97,1},{2,34}... | collective-permute-start | bytes 983048 | tf_op jit(solution)/shard_map/ppermute | solution.py:242
  114.6 13.5 %copy-start.7 = (bf16[10,128,128]{2,1,0:T(8,128)(2,1)}, bf16[10,128,128]{2,1,0:T(8,128)(2,1)S(1)}, u32[]{:S(2)}) copy-start(bf16[10,128,128]{2,1,0:T(8,128)(2,1)S(1)} %collective-permute-done.17.refs_7_) | copy-start | bytes 983044
  124.7 3.5 %copy-start.1 = (bf16[20,256,128]{2,1,0:T(8,128)(2,1)}, bf16[20,256,128]{2,1,0:T(8,128)(2,1)S(1)}, u32[]{:S(2)}) copy-start(bf16[20,256,128]{2,1,0:T(8,128)(2,1)S(1)} %all-to-all-done.3.refs_2_) | copy-start | bytes 3932164
  124.7 3.4 %collective-permute-start.19 = (bf16[20,256,128]{2,1,0:T(8,128)(2,1)S(1)}, bf16[20,256,128]{2,1,0:T(8,128)(2,1)S(1)}, u32[]{:S(2)}, u32[]{:S(2)}) collective-permute-start(bf16[20,256,128]{2,1,0:T(8,128)(2,1)S(1)} %all-to-all-done.3.refs_2_), channel_id=1, source_target_pairs={{0,1},{1,0},{2,3},{3,2},{4,5},{5,4},{6,7},{7,6},{8,9},{9,8},{10,11... | collective-permute-start | bytes 3932168 | tf_op jit(solution)/shard_map/ppermute | solution.py:242
  (6 other events, 6.1 us)

commit v4 on v3

--- a/solution.py
+++ b/solution.py
@@ -230,7 +230,7 @@
             pltpu.SemaphoreType.DMA((2 + Z + end,)),
         ]
         + [pltpu.VMEM(shape, jnp.float32)] * end,
-        compiler_params=PARAMS,
+        compiler_params=pltpu.CompilerParams(vmem_limit_bytes=16 * 2**20),
         cost_estimate=pl.CostEstimate(
             flops=2 * PART * rows * WIDTH * cols, bytes_accessed=6 * 2**20, transcendentals=0
         ),
@@ -285,20 +285,20 @@
     spread_a = over_y(left_a)
     right_b = right_terms(B, z, sizes, *right)
     left_b = total(keeps_b, came_b)
-    spread_a, came_a, right_b, left_b = fence((spread_a, came_a, right_b, left_b))
+    spread_a, right_b, left_b = fence((spread_a, right_b, left_b))
 
     came_b = over_z(right_b)
     one_a, two_a = left_sums(spread_a), total(right_a[0], *came_a)
-    one_a, two_a, left_b = fence((one_a, two_a, left_b))
+    one_a, left_b = fence((one_a, left_b))
     spread_b = over_y(left_b)
     one_x, two_x = swap(one_a, "xh"), swap(two_a, "xl")
     one_a, two_a = total(one_a, one_x), total(two_a, two_x)
-    spread_b, came_b, one_a, two_a = fence((spread_b, came_b, one_a, two_a))
+    spread_b, one_a, two_a = fence((spread_b, one_a, two_a))
 
     rights_a = [two_a] + over_z([two_a] * Z)
     copies_a = left_copies(one_a)
     one_b, two_b = left_sums(spread_b), total(right_b[0], *came_b)
-    one_b, two_b, copies_a = fence((one_b, two_b, copies_a))
+    one_b, copies_a = fence((one_b, copies_a))
     half_a = over_y(copies_a)
     one_x, two_x = swap(one_b, "xh"), swap(two_b, "xl")
     one_b, two_b = total(one_b, one_x), total(two_b, two_x)

time: 137 us -> 133 us (0.971)
  waiting for transfers between devices: 46.9 us -> 35.7 us
  starting transfers between devices: 39.5 us -> 46 us
  local copies, waits for them, and re-layouts: 6.83 us -> 8.88 us
  Pallas kernels: 34.5 us -> 33.1 us
    ppermute x20, waiting for transfers between devices: 46.9 us -> 33 us  [shift(): lax.ppermute(array, axis, [(i, (i + step) % size) for i in range(size)])]
    ppermute x20, starting transfers between devices: 23.1 us -> 30.3 us  [shift(): lax.ppermute(array, axis, [(i, (i + step) % size) for i in range(size)])]
    all_to_all x4, waiting for transfers between devices: 0.01 us -> 2.76 us  [over_y(): return lax.all_to_all(array, 'y', 0, 0, tiled=True)]
    pallas_call x2, Pallas kernels: 12.8 us -> 10.5 us  [product(): pl.pallas_call(lambda *refs: product_kernel(part, scale, *refs), out_shap...]
    unnamed x28 -> x26, local copies, waits for them, and re-layouts: 4.09 us -> 5.15 us
  transfers between devices with their start and end apart: 24 -> 24, of which waited for: 11 -> 9; matrix products, arithmetic and copies ran while one was open for 5% -> 9% of each run, Pallas kernels for 14% -> 14%
where the time goes in v4:
time: 133 us; the launch traced here: 132 us
  starting transfers between devices  46 us (35%)
  waiting for transfers between devices  35.7 us (27%)
  Pallas kernels  33.1 us (25%)
  local copies, waits for them, and re-layouts  8.88 us (7%)
  other arithmetic  8.2 us (6%)
    ppermute x20, waiting for transfers between devices, shift(): lax.ppermute(array, axis, [(i, (i + step) % size) for i in range(size)])  33 us
    ppermute x20, starting transfers between devices, shift(): lax.ppermute(array, axis, [(i, (i + step) % size) for i in range(size)])  30.3 us
    all_to_all x4, starting transfers between devices, over_y(): return lax.all_to_all(array, 'y', 0, 0, tiled=True)  15.7 us
    pallas_call x2, Pallas kernels, right_terms(): pl.pallas_call(lambda *refs: right_kernel(part, *refs), out_shape=[jax.Sh...  13.1 us
    pallas_call x2, Pallas kernels, product(): pl.pallas_call(lambda *refs: product_kernel(part, scale, *refs), out_shap...  10.5 us
    pallas_call x1, Pallas kernels, left_terms(): pl.pallas_call(left_kernel, out_shape=[jax.ShapeDtypeStruct((HALF, rows,...  9.52 us
    convert_element_type x10, other arithmetic, total(): sum((term.astype(jnp.float32) for term in terms)).astype(jnp.bfloat16)  8.13 us
    unnamed x26, local copies, waits for them, and re-layouts  5.15 us
  transfers between devices with their start and end apart: 24, of which 9 were waited for; matrix products, arithmetic and copies ran while one was open for 9% of the time, Pallas kernels for 14%

profile of v4, /device:TPU:1, one launch (start us, length us, event | category | flops | bytes accessed | tf_op | source)
XLA Modules:
  0.0 132.3 jit_solution(589857123348857205)
XLA Ops:
  0.0 9.5 %left.1 = (bf16[20,256,128]{2,1,0:T(8,128)(2,1)}, bf16[20,256,128]{2,1,0:T(8,128)(2,1)}, bf16[20,256,128]{2,1,0:T(8,128)(2,1)}, bf16[20,256,128]{2,1,0:T(8,128)(2,1)}) custom-call(s32[1]{0:T(128)} %bitcast.at_ref, s32[8]{0:T(128)} %refs_1_.7, bf16[8,256,256]{2,1,0:T(8,128)(2,1)} %edge_ref.1, bf16[8,256,2048]{2,1,0:T(8,128)(2,1)} %site_ref.1), custom_call_target="tpu_custom_call" | custom-call | flops 1342177280 | bytes 12582912 | tf_op jit(solution)/shard_map/left/pallas_call | solution.py:86
  9.5 1.5 %collective-permute-start = (bf16[20,256,128]{2,1,0:T(8,128)(2,1)}, bf16[20,256,128]{2,1,0:T(8,128)(2,1)S(1)}, u32[]{:S(2)}, u32[]{:S(2)}) collective-permute-start(bf16[20,256,128]{2,1,0:T(8,128)(2,1)} %get-tuple-element.57), channel_id=1, source_target_pairs={{0,1},{1,0},{2,3},{3,2},{4,5},{5,4},{6,7},{7,6},{8,9},{9,8},{10,11... | collective-permute-start | bytes 3932168 | tf_op jit(solution)/shard_map/ppermute | solution.py:242
  11.1 6.9 %right.2 = (bf16[10,128,128]{2,1,0:T(8,128)(2,1)}, bf16[10,128,128]{2,1,0:T(8,128)(2,1)}, bf16[10,128,128]{2,1,0:T(8,128)(2,1)}, bf16[10,128,128]{2,1,0:T(8,128)(2,1)}) custom-call(s32[1]{0:T(128)} %bitcast.1.refs_0_, s32[8]{0:T(128)} %refs_1_.7, bf16[8,2048,512]{2,1,0:T(8,128)(2,1)} %refs_2_.1, bf16[8,512,128]{2,1,0:T(8,128)(2,1)} %refs_3_.1), custom_call_target="tpu_custom_call" | custom-call | flops 671088640 | bytes 10485760 | tf_op jit(solution)/shard_map/right/pallas_call | solution.py:149
  18.1 1.4 %add_convert_fusion.1 = bf16[20,256,128]{2,1,0:T(8,128)(2,1)} fusion(bf16[20,256,128]{2,1,0:T(8,128)(2,1)S(1)} %collective-permute-done, bf16[20,256,128]{2,1,0:T(8,128)(2,1)S(1)} %copy-done.10), kind=kLoop, calls=%fused_computation.1 | loop fusion | flops 2621440 | bytes 3932160 | tf_op jit(solution)/shard_map/convert_element_type | solution.py:246
  19.6 4.4 %all-to-all-start = ((bf16[20,256,128]{2,1,0:T(8,128)(2,1)}), bf16[20,256,128]{2,1,0:T(8,128)(2,1)S(1)}, u32[]{:S(2)}, u32[]{:S(2)}) async-start(bf16[20,256,128]{2,1,0:T(8,128)(2,1)} %add_convert_fusion.1), calls=%async_computation | async-start | bytes 2621440 | tf_op jit(solution)/shard_map/all_to_all | solution.py:254
  24.0 1.6 %collective-permute-start.3 = (bf16[10,128,128]{2,1,0:T(8,128)(2,1)}, bf16[10,128,128]{2,1,0:T(8,128)(2,1)}, u32[]{:S(2)}, u32[]{:S(2)}) collective-permute-start(bf16[10,128,128]{2,1,0:T(8,128)(2,1)} %get-tuple-element.82), channel_id=1, source_target_pairs={{0,32},{32,64},{64,96},{96,0},{1,33},{33,65},{65,97},{97,1},{2,34}... | collective-permute-start | bytes 983048 | tf_op jit(solution)/shard_map/ppermute | solution.py:242
  25.6 3.3 %collective-permute-start.4 = (bf16[10,128,128]{2,1,0:T(8,128)(2,1)}, bf16[10,128,128]{2,1,0:T(8,128)(2,1)}, u32[]{:S(2)}, u32[]{:S(2)}) collective-permute-start(bf16[10,128,128]{2,1,0:T(8,128)(2,1)} %get-tuple-element.83), channel_id=1, source_target_pairs={{0,64},{32,96},{64,0},{96,32},{1,65},{33,97},{65,1},{97,33},{2,66}... | collective-permute-start | bytes 983048 | tf_op jit(solution)/shard_map/ppermute | solution.py:242
  29.6 2.7 %add_convert_fusion = bf16[20,256,128]{2,1,0:T(8,128)(2,1)} fusion(bf16[20,256,128]{2,1,0:T(8,128)(2,1)} %collective-permute-done.1, bf16[20,256,128]{2,1,0:T(8,128)(2,1)S(1)} %copy-done.9), kind=kLoop, calls=%fused_computation | loop fusion | flops 2621440 | bytes 3932160 | tf_op jit(solution)/shard_map/convert_element_type | solution.py:246
  32.4 6.2 %right.3 = (bf16[10,128,128]{2,1,0:T(8,128)(2,1)}, bf16[10,128,128]{2,1,0:T(8,128)(2,1)}, bf16[10,128,128]{2,1,0:T(8,128)(2,1)}, bf16[10,128,128]{2,1,0:T(8,128)(2,1)}) custom-call(s32[1]{0:T(128)} %bitcast.1.refs_0_, s32[8]{0:T(128)} %refs_1_.7, bf16[8,2048,512]{2,1,0:T(8,128)(2,1)} %refs_2_.1, bf16[8,512,128]{2,1,0:T(8,128)(2,1)} %refs_3_.1), custom_call_target="tpu_custom_call" | custom-call | flops 671088640 | bytes 10485760 | tf_op jit(solution)/shard_map/right/pallas_call | solution.py:149
  38.6 2.8 %all-to-all-done = bf16[20,256,128]{2,1,0:T(8,128)(2,1)S(1)} async-done(((bf16[20,256,128]{2,1,0:T(8,128)(2,1)}), bf16[20,256,128]{2,1,0:T(8,128)(2,1)S(1)}, u32[]{:S(2)}, u32[]{:S(2)}) %all-to-all-start) | async-done | bytes 1310752 | tf_op jit(solution)/shard_map/all_to_all | solution.py:254
  41.5 3.7 %all-to-all-start.1 = ((bf16[20,256,128]{2,1,0:T(8,128)(2,1)}), bf16[20,256,128]{2,1,0:T(8,128)(2,1)S(1)}, u32[]{:S(2)}, u32[]{:S(2)}) async-start(bf16[20,256,128]{2,1,0:T(8,128)(2,1)} %add_convert_fusion), calls=%async_computation.1 | async-start | bytes 2621440 | tf_op jit(solution)/shard_map/all_to_all | solution.py:254
  45.2 1.4 %add_convert_fusion.7 = bf16[10,128,128]{2,1,0:T(8,128)(2,1)S(1)} fusion(bf16[10,128,128]{2,1,0:T(8,128)(2,1)} %collective-permute-done.5, bf16[10,128,128]{2,1,0:T(8,128)(2,1)} %collective-permute-done.4, bf16[10,128,128]{2,1,0:T(8,128)(2,1)} %collective-permute-done.3, bf16[10,128,128]{2,1,0:T(8,128)(2,1)S(1)} %copy-done.12), kind=kLoop, calls=%fused_computation.7 | loop fusion | flops 1310720 | bytes 1638400 | tf_op jit(solution)/shard_map/convert_element_type | solution.py:246
  47.9 2.5 %collective-permute-start.2 = (bf16[5,256,128]{2,1,0:T(8,128)(2,1)S(1)}, bf16[5,256,128]{2,1,0:T(8,128)(2,1)S(1)}, u32[]{:S(2)}, u32[]{:S(2)}) collective-permute-start(bf16[5,256,128]{2,1,0:T(8,128)(2,1)S(1)} %add_convert_fusion.9), channel_id=1, source_target_pairs={{0,2},{2,0},{1,3},{3,1},{4,6},{6,4},{5,7},{7,5},{8,10},{10,8},{9,1... | collective-permute-start | bytes 983048 | tf_op jit(solution)/shard_map/ppermute | solution.py:242
  50.3 4.0 %collective-permute-done.6 = bf16[10,128,128]{2,1,0:T(8,128)(2,1)S(1)} collective-permute-done((bf16[10,128,128]{2,1,0:T(8,128)(2,1)S(1)}, bf16[10,128,128]{2,1,0:T(8,128)(2,1)S(1)}, u32[]{:S(2)}, u32[]{:S(2)}) %collective-permute-start.6) | collective-permute-done | bytes 327712 | tf_op jit(solution)/shard_map/ppermute | solution.py:242
  54.5 1.5 %collective-permute-start.11 = (bf16[10,128,128]{2,1,0:T(8,128)(2,1)}, bf16[10,128,128]{2,1,0:T(8,128)(2,1)S(1)}, u32[]{:S(2)}, u32[]{:S(2)}) collective-permute-start(bf16[10,128,128]{2,1,0:T(8,128)(2,1)} %get-tuple-element.91), channel_id=1, source_target_pairs={{0,32},{32,64},{64,96},{96,0},{1,33},{33,65},{65,97},{97,1},{2,34}... | collective-permute-start | bytes 983048 | tf_op jit(solution)/shard_map/ppermute | solution.py:242
  56.0 3.3 %collective-permute-start.12 = (bf16[10,128,128]{2,1,0:T(8,128)(2,1)}, bf16[10,128,128]{2,1,0:T(8,128)(2,1)S(1)}, u32[]{:S(2)}, u32[]{:S(2)}) collective-permute-start(bf16[10,128,128]{2,1,0:T(8,128)(2,1)} %get-tuple-element.92), channel_id=1, source_target_pairs={{0,64},{32,96},{64,0},{96,32},{1,65},{33,97},{65,1},{97,33},{2,66}... | collective-permute-start | bytes 983048 | tf_op jit(solution)/shard_map/ppermute | solution.py:242
  60.1 3.5 %collective-permute-done.2 = bf16[5,256,128]{2,1,0:T(8,128)(2,1)S(1)} collective-permute-done((bf16[5,256,128]{2,1,0:T(8,128)(2,1)S(1)}, bf16[5,256,128]{2,1,0:T(8,128)(2,1)S(1)}, u32[]{:S(2)}, u32[]{:S(2)}) %collective-permute-start.2) | collective-permute-done | bytes 327712 | tf_op jit(solution)/shard_map/ppermute | solution.py:242
  63.9 1.4 %broadcast_in_dim.4 = bf16[4,5,256,128]{3,2,1,0:T(8,128)(2,1)} broadcast(bf16[5,256,128]{2,1,0:T(8,128)(2,1)S(1)} %add_convert_fusion.8), dimensions={1,2,3} | broadcast | bytes 1638400 | tf_op jit(solution)/shard_map/broadcast_in_dim | solution.py:274
  65.3 4.0 %all-to-all-start.2 = ((bf16[20,256,128]{2,1,0:T(8,128)(2,1)}), bf16[20,256,128]{2,1,0:T(8,128)(2,1)S(1)}, u32[]{:S(2)}, u32[]{:S(2)}) async-start(bf16[20,256,128]{2,1,0:T(8,128)(2,1)} %bitcast.4), calls=%async_computation.2 | async-start | bytes 2621440 | tf_op jit(solution)/shard_map/all_to_all | solution.py:254
  72.9 2.5 %collective-permute-start.10 = (bf16[5,256,128]{2,1,0:T(8,128)(2,1)S(1)}, bf16[5,256,128]{2,1,0:T(8,128)(2,1)S(1)}, u32[]{:S(2)}, u32[]{:S(2)}) collective-permute-start(bf16[5,256,128]{2,1,0:T(8,128)(2,1)S(1)} %add_convert_fusion.5), channel_id=1, source_target_pairs={{0,2},{2,0},{1,3},{3,1},{4,6},{6,4},{5,7},{7,5},{8,10},{10,8},{9,1... | collective-permute-start | bytes 983048 | tf_op jit(solution)/shard_map/ppermute | solution.py:242
  75.4 3.6 %collective-permute-start.9 = (bf16[10,128,128]{2,1,0:T(8,128)(2,1)S(1)}, bf16[10,128,128]{2,1,0:T(8,128)(2,1)S(1)}, u32[]{:S(2)}, u32[]{:S(2)}) collective-permute-start(bf16[10,128,128]{2,1,0:T(8,128)(2,1)S(1)} %add_convert_fusion.6.refs_4_), channel_id=1, source_target_pairs={{0,96},{32,0},{64,32},{96,64},{1,97},{33,1},{65,33},{97,65},{2,98}... | collective-permute-start | bytes 983048 | tf_op jit(solution)/shard_map/ppermute | solution.py:242
  79.0 1.7 %collective-permute-start.8 = (bf16[10,128,128]{2,1,0:T(8,128)(2,1)S(1)}, bf16[10,128,128]{2,1,0:T(8,128)(2,1)S(1)}, u32[]{:S(2)}, u32[]{:S(2)}) collective-permute-start(bf16[10,128,128]{2,1,0:T(8,128)(2,1)S(1)} %add_convert_fusion.6.refs_4_), channel_id=1, source_target_pairs={{0,64},{32,96},{64,0},{96,32},{1,65},{33,97},{65,1},{97,33},{2,66}... | collective-permute-start | bytes 983048 | tf_op jit(solution)/shard_map/ppermute | solution.py:242
  80.7 4.7 %collective-permute-done.10 = bf16[5,256,128]{2,1,0:T(8,128)(2,1)S(1)} collective-permute-done((bf16[5,256,128]{2,1,0:T(8,128)(2,1)S(1)}, bf16[5,256,128]{2,1,0:T(8,128)(2,1)S(1)}, u32[]{:S(2)}, u32[]{:S(2)}) %collective-permute-start.10) | collective-permute-done | bytes 327712 | tf_op jit(solution)/shard_map/ppermute | solution.py:242
  86.7 9.1 %collective-permute-done.7.refs_5_ = bf16[10,128,128]{2,1,0:T(8,128)(2,1)S(1)} collective-permute-done((bf16[10,128,128]{2,1,0:T(8,128)(2,1)S(1)}, bf16[10,128,128]{2,1,0:T(8,128)(2,1)S(1)}, u32[]{:S(2)}, u32[]{:S(2)}) %collective-permute-start.7) | collective-permute-done | bytes 327712 | tf_op jit(solution)/shard_map/ppermute | solution.py:242
  95.8 1.8 %collective-permute-start.18 = (bf16[20,256,128]{2,1,0:T(8,128)(2,1)S(1)}, bf16[20,256,128]{2,1,0:T(8,128)(2,1)}, u32[]{:S(2)}, u32[]{:S(2)}) collective-permute-start(bf16[20,256,128]{2,1,0:T(8,128)(2,1)S(1)} %all-to-all-done.2.refs_2_), channel_id=1, source_target_pairs={{0,1},{1,0},{2,3},{3,2},{4,5},{5,4},{6,7},{7,6},{8,9},{9,8},{10,11... | collective-permute-start | bytes 3932168 | tf_op jit(solution)/shard_map/ppermute | solution.py:242
  97.6 2.4 %broadcast_in_dim.5 = bf16[4,5,256,128]{3,2,1,0:T(8,128)(2,1)} broadcast(bf16[5,256,128]{2,1,0:T(8,128)(2,1)} %add_convert_fusion.4), dimensions={1,2,3} | broadcast | bytes 1638400 | tf_op jit(solution)/shard_map/broadcast_in_dim | solution.py:274
  100.0 3.6 %all-to-all-start.3 = ((bf16[20,256,128]{2,1,0:T(8,128)(2,1)}), bf16[20,256,128]{2,1,0:T(8,128)(2,1)S(1)}, u32[]{:S(2)}, u32[]{:S(2)}) async-start(bf16[20,256,128]{2,1,0:T(8,128)(2,1)} %bitcast.6), calls=%async_computation.3 | async-start | bytes 2621440 | tf_op jit(solution)/shard_map/all_to_all | solution.py:254
  103.9 1.7 %collective-permute-start.16 = (bf16[10,128,128]{2,1,0:T(8,128)(2,1)S(1)}, bf16[10,128,128]{2,1,0:T(8,128)(2,1)}, u32[]{:S(2)}, u32[]{:S(2)}) collective-permute-start(bf16[10,128,128]{2,1,0:T(8,128)(2,1)S(1)} %add_convert_fusion.2.refs_4_), channel_id=1, source_target_pairs={{0,64},{32,96},{64,0},{96,32},{1,65},{33,97},{65,1},{97,33},{2,66}... | collective-permute-start | bytes 983048 | tf_op jit(solution)/shard_map/ppermute | solution.py:242
  109.0 5.0 %product.1.refs_8_ = f32[8,256,128]{2,1,0:T(8,128)S(1)} custom-call(s32[4]{0:T(128)S(1)} %pad_add_fusion.refs_0_, s32[8]{0:T(128)S(1)} %copy-done.8, bf16[20,256,128]{2,1,0:T(8,128)(2,1)S(1)} %all-to-all-done.2.refs_2_, bf16[20,256,128]{2,1,0:T(8,128)(2,1)} %collective-permute-done.18.refs_3_, bf16[10,128,128]{2,1,0:T(8,128)(2,1)S(1)} %add_convert_fusion.6.refs_4_, ...), custom_call_target="tpu_custom_call" | custom-call | flops 335544320 | bytes 6291456 | tf_op jit(solution)/shard_map/product/pallas_call | solution.py:222
  114.9 7.3 %collective-permute-done.15.refs_5_ = bf16[10,128,128]{2,1,0:T(8,128)(2,1)} collective-permute-done((bf16[10,128,128]{2,1,0:T(8,128)(2,1)S(1)}, bf16[10,128,128]{2,1,0:T(8,128)(2,1)}, u32[]{:S(2)}, u32[]{:S(2)}) %collective-permute-start.15) | collective-permute-done | bytes 327712 | tf_op jit(solution)/shard_map/ppermute | solution.py:242
  122.7 2.7 %collective-permute-done.19.refs_3_ = bf16[20,256,128]{2,1,0:T(8,128)(2,1)S(1)} collective-permute-done((bf16[20,256,128]{2,1,0:T(8,128)(2,1)S(1)}, bf16[20,256,128]{2,1,0:T(8,128)(2,1)S(1)}, u32[]{:S(2)}, u32[]{:S(2)}) %collective-permute-start.19) | collective-permute-done | bytes 1310752 | tf_op jit(solution)/shard_map/ppermute | solution.py:242
  126.6 5.5 %product_end.1 = bf16[8,256,128]{2,1,0:T(8,128)(2,1)} custom-call(s32[4]{0:T(128)S(1)} %pad_add_fusion.refs_0_, s32[8]{0:T(128)S(1)} %copy-done.8, bf16[20,256,128]{2,1,0:T(8,128)(2,1)S(1)} %all-to-all-done.3.refs_2_, bf16[20,256,128]{2,1,0:T(8,128)(2,1)S(1)} %collective-permute-done.19.refs_3_, bf16[10,128,128]{2,1,0:T(8,128)(2,1)S(1)} %add_convert_fusion.2.refs_4_, ...), custom_call_target="tpu_custom_call" | custom-call | flops 335544320 | bytes 6291456 | tf_op jit(solution)/shard_map/product_end/pallas_call | solution.py:222
  (60 shorter events, 14.9 us)
Async XLA Ops:
  9.5 8.6 %collective-permute-start = (bf16[20,256,128]{2,1,0:T(8,128)(2,1)}, bf16[20,256,128]{2,1,0:T(8,128)(2,1)S(1)}, u32[]{:S(2)}, u32[]{:S(2)}) collective-permute-start(bf16[20,256,128]{2,1,0:T(8,128)(2,1)} %get-tuple-element.57), channel_id=1, source_target_pairs={{0,1},{1,0},{2,3},{3,2},{4,5},{5,4},{6,7},{7,6},{8,9},{9,8},{10,11... | collective-permute-start | bytes 3932168 | tf_op jit(solution)/shard_map/ppermute | solution.py:242
  11.0 18.6 %collective-permute-start.1 = (bf16[20,256,128]{2,1,0:T(8,128)(2,1)}, bf16[20,256,128]{2,1,0:T(8,128)(2,1)}, u32[]{:S(2)}, u32[]{:S(2)}) collective-permute-start(bf16[20,256,128]{2,1,0:T(8,128)(2,1)} %get-tuple-element.76), channel_id=1, source_target_pairs={{0,1},{1,0},{2,3},{3,2},{4,5},{5,4},{6,7},{7,6},{8,9},{9,8},{10,11... | collective-permute-start | bytes 3932168 | tf_op jit(solution)/shard_map/ppermute | solution.py:242
  11.1 7.0 %copy-start.10 = (bf16[20,256,128]{2,1,0:T(8,128)(2,1)S(1)}, bf16[20,256,128]{2,1,0:T(8,128)(2,1)}, u32[]{:S(2)}) copy-start(bf16[20,256,128]{2,1,0:T(8,128)(2,1)} %get-tuple-element.56) | copy-start | bytes 3932164
  19.5 10.1 %copy-start.9 = (bf16[20,256,128]{2,1,0:T(8,128)(2,1)S(1)}, bf16[20,256,128]{2,1,0:T(8,128)(2,1)}, u32[]{:S(2)}) copy-start(bf16[20,256,128]{2,1,0:T(8,128)(2,1)} %get-tuple-element.75) | copy-start | bytes 3932164
  19.6 21.8 %all-to-all-start = ((bf16[20,256,128]{2,1,0:T(8,128)(2,1)}), bf16[20,256,128]{2,1,0:T(8,128)(2,1)S(1)}, u32[]{:S(2)}, u32[]{:S(2)}) async-start(bf16[20,256,128]{2,1,0:T(8,128)(2,1)} %add_convert_fusion.1), calls=%async_computation | async-start | bytes 2621440 | tf_op jit(solution)/shard_map/all_to_all | solution.py:254
  24.0 21.2 %collective-permute-start.3 = (bf16[10,128,128]{2,1,0:T(8,128)(2,1)}, bf16[10,128,128]{2,1,0:T(8,128)(2,1)}, u32[]{:S(2)}, u32[]{:S(2)}) collective-permute-start(bf16[10,128,128]{2,1,0:T(8,128)(2,1)} %get-tuple-element.82), channel_id=1, source_target_pairs={{0,32},{32,64},{64,96},{96,0},{1,33},{33,65},{65,97},{97,1},{2,34}... | collective-permute-start | bytes 983048 | tf_op jit(solution)/shard_map/ppermute | solution.py:242
  25.6 19.6 %collective-permute-start.4 = (bf16[10,128,128]{2,1,0:T(8,128)(2,1)}, bf16[10,128,128]{2,1,0:T(8,128)(2,1)}, u32[]{:S(2)}, u32[]{:S(2)}) collective-permute-start(bf16[10,128,128]{2,1,0:T(8,128)(2,1)} %get-tuple-element.83), channel_id=1, source_target_pairs={{0,64},{32,96},{64,0},{96,32},{1,65},{33,97},{65,1},{97,33},{2,66}... | collective-permute-start | bytes 983048 | tf_op jit(solution)/shard_map/ppermute | solution.py:242
  28.9 16.3 %collective-permute-start.5 = (bf16[10,128,128]{2,1,0:T(8,128)(2,1)}, bf16[10,128,128]{2,1,0:T(8,128)(2,1)}, u32[]{:S(2)}, u32[]{:S(2)}) collective-permute-start(bf16[10,128,128]{2,1,0:T(8,128)(2,1)} %get-tuple-element.84), channel_id=1, source_target_pairs={{0,96},{32,0},{64,32},{96,64},{1,97},{33,1},{65,33},{97,65},{2,98}... | collective-permute-start | bytes 983048 | tf_op jit(solution)/shard_map/ppermute | solution.py:242
  41.5 3.7 %copy-start.12 = (bf16[10,128,128]{2,1,0:T(8,128)(2,1)S(1)}, bf16[10,128,128]{2,1,0:T(8,128)(2,1)}, u32[]{:S(2)}) copy-start(bf16[10,128,128]{2,1,0:T(8,128)(2,1)} %get-tuple-element.81) | copy-start | bytes 983044
  41.5 22.2 %all-to-all-start.1 = ((bf16[20,256,128]{2,1,0:T(8,128)(2,1)}), bf16[20,256,128]{2,1,0:T(8,128)(2,1)S(1)}, u32[]{:S(2)}, u32[]{:S(2)}) async-start(bf16[20,256,128]{2,1,0:T(8,128)(2,1)} %add_convert_fusion), calls=%async_computation.1 | async-start | bytes 2621440 | tf_op jit(solution)/shard_map/all_to_all | solution.py:254
  46.6 7.8 %collective-permute-start.6 = (bf16[10,128,128]{2,1,0:T(8,128)(2,1)S(1)}, bf16[10,128,128]{2,1,0:T(8,128)(2,1)S(1)}, u32[]{:S(2)}, u32[]{:S(2)}) collective-permute-start(bf16[10,128,128]{2,1,0:T(8,128)(2,1)S(1)} %add_convert_fusion.7), channel_id=1, source_target_pairs={{0,16},{16,0},{1,17},{17,1},{2,18},{18,2},{3,19},{19,3},{4,20},{20... | collective-permute-start | bytes 983048 | tf_op jit(solution)/shard_map/ppermute | solution.py:242
  47.9 15.7 %collective-permute-start.2 = (bf16[5,256,128]{2,1,0:T(8,128)(2,1)S(1)}, bf16[5,256,128]{2,1,0:T(8,128)(2,1)S(1)}, u32[]{:S(2)}, u32[]{:S(2)}) collective-permute-start(bf16[5,256,128]{2,1,0:T(8,128)(2,1)S(1)} %add_convert_fusion.9), channel_id=1, source_target_pairs={{0,2},{2,0},{1,3},{3,1},{4,6},{6,4},{5,7},{7,5},{8,10},{10,8},{9,1... | collective-permute-start | bytes 983048 | tf_op jit(solution)/shard_map/ppermute | solution.py:242
  54.5 14.8 %collective-permute-start.11 = (bf16[10,128,128]{2,1,0:T(8,128)(2,1)}, bf16[10,128,128]{2,1,0:T(8,128)(2,1)S(1)}, u32[]{:S(2)}, u32[]{:S(2)}) collective-permute-start(bf16[10,128,128]{2,1,0:T(8,128)(2,1)} %get-tuple-element.91), channel_id=1, source_target_pairs={{0,32},{32,64},{64,96},{96,0},{1,33},{33,65},{65,97},{97,1},{2,34}... | collective-permute-start | bytes 983048 | tf_op jit(solution)/shard_map/ppermute | solution.py:242
  56.0 13.4 %collective-permute-start.12 = (bf16[10,128,128]{2,1,0:T(8,128)(2,1)}, bf16[10,128,128]{2,1,0:T(8,128)(2,1)S(1)}, u32[]{:S(2)}, u32[]{:S(2)}) collective-permute-start(bf16[10,128,128]{2,1,0:T(8,128)(2,1)} %get-tuple-element.92), channel_id=1, source_target_pairs={{0,64},{32,96},{64,0},{96,32},{1,65},{33,97},{65,1},{97,33},{2,66}... | collective-permute-start | bytes 983048 | tf_op jit(solution)/shard_map/ppermute | solution.py:242
  59.3 11.2 %collective-permute-start.13 = (bf16[10,128,128]{2,1,0:T(8,128)(2,1)}, bf16[10,128,128]{2,1,0:T(8,128)(2,1)}, u32[]{:S(2)}, u32[]{:S(2)}) collective-permute-start(bf16[10,128,128]{2,1,0:T(8,128)(2,1)} %get-tuple-element.93), channel_id=1, source_target_pairs={{0,96},{32,0},{64,32},{96,64},{1,97},{33,1},{65,33},{97,65},{2,98}... | collective-permute-start | bytes 983048 | tf_op jit(solution)/shard_map/ppermute | solution.py:242
  65.3 5.2 %copy-start.11 = (bf16[10,128,128]{2,1,0:T(8,128)(2,1)S(1)}, bf16[10,128,128]{2,1,0:T(8,128)(2,1)}, u32[]{:S(2)}) copy-start(bf16[10,128,128]{2,1,0:T(8,128)(2,1)} %get-tuple-element.90) | copy-start | bytes 983044
  65.3 30.5 %all-to-all-start.2 = ((bf16[20,256,128]{2,1,0:T(8,128)(2,1)}), bf16[20,256,128]{2,1,0:T(8,128)(2,1)S(1)}, u32[]{:S(2)}, u32[]{:S(2)}) async-start(bf16[20,256,128]{2,1,0:T(8,128)(2,1)} %bitcast.4), calls=%async_computation.2 | async-start | bytes 2621440 | tf_op jit(solution)/shard_map/all_to_all | solution.py:254
  71.6 9.0 %collective-permute-start.14 = (bf16[10,128,128]{2,1,0:T(8,128)(2,1)S(1)}, bf16[10,128,128]{2,1,0:T(8,128)(2,1)S(1)}, u32[]{:S(2)}, u32[]{:S(2)}) collective-permute-start(bf16[10,128,128]{2,1,0:T(8,128)(2,1)S(1)} %add_convert_fusion.3), channel_id=1, source_target_pairs={{0,16},{16,0},{1,17},{17,1},{2,18},{18,2},{3,19},{19,3},{4,20},{20... | collective-permute-start | bytes 983048 | tf_op jit(solution)/shard_map/ppermute | solution.py:242
  72.9 12.5 %collective-permute-start.10 = (bf16[5,256,128]{2,1,0:T(8,128)(2,1)S(1)}, bf16[5,256,128]{2,1,0:T(8,128)(2,1)S(1)}, u32[]{:S(2)}, u32[]{:S(2)}) collective-permute-start(bf16[5,256,128]{2,1,0:T(8,128)(2,1)S(1)} %add_convert_fusion.5), channel_id=1, source_target_pairs={{0,2},{2,0},{1,3},{3,1},{4,6},{6,4},{5,7},{7,5},{8,10},{10,8},{9,1... | collective-permute-start | bytes 983048 | tf_op jit(solution)/shard_map/ppermute | solution.py:242
  75.4 10.9 %collective-permute-start.9 = (bf16[10,128,128]{2,1,0:T(8,128)(2,1)S(1)}, bf16[10,128,128]{2,1,0:T(8,128)(2,1)S(1)}, u32[]{:S(2)}, u32[]{:S(2)}) collective-permute-start(bf16[10,128,128]{2,1,0:T(8,128)(2,1)S(1)} %add_convert_fusion.6.refs_4_), channel_id=1, source_target_pairs={{0,96},{32,0},{64,32},{96,64},{1,97},{33,1},{65,33},{97,65},{2,98}... | collective-permute-start | bytes 983048 | tf_op jit(solution)/shard_map/ppermute | solution.py:242
  79.0 7.8 %collective-permute-start.8 = (bf16[10,128,128]{2,1,0:T(8,128)(2,1)S(1)}, bf16[10,128,128]{2,1,0:T(8,128)(2,1)S(1)}, u32[]{:S(2)}, u32[]{:S(2)}) collective-permute-start(bf16[10,128,128]{2,1,0:T(8,128)(2,1)S(1)} %add_convert_fusion.6.refs_4_), channel_id=1, source_target_pairs={{0,64},{32,96},{64,0},{96,32},{1,65},{33,97},{65,1},{97,33},{2,66}... | collective-permute-start | bytes 983048 | tf_op jit(solution)/shard_map/ppermute | solution.py:242
  80.6 15.2 %collective-permute-start.7 = (bf16[10,128,128]{2,1,0:T(8,128)(2,1)S(1)}, bf16[10,128,128]{2,1,0:T(8,128)(2,1)S(1)}, u32[]{:S(2)}, u32[]{:S(2)}) collective-permute-start(bf16[10,128,128]{2,1,0:T(8,128)(2,1)S(1)} %add_convert_fusion.6.refs_4_), channel_id=1, source_target_pairs={{0,32},{32,64},{64,96},{96,0},{1,33},{33,65},{65,97},{97,1},{2,34}... | collective-permute-start | bytes 983048 | tf_op jit(solution)/shard_map/ppermute | solution.py:242
  86.3 13.7 %copy-start.2 = (bf16[10,128,128]{2,1,0:T(8,128)(2,1)}, bf16[10,128,128]{2,1,0:T(8,128)(2,1)S(1)}, u32[]{:S(2)}) copy-start(bf16[10,128,128]{2,1,0:T(8,128)(2,1)S(1)} %collective-permute-done.9.refs_7_) | copy-start | bytes 983044
  86.7 13.3 %copy-start.4 = (bf16[10,128,128]{2,1,0:T(8,128)(2,1)}, bf16[10,128,128]{2,1,0:T(8,128)(2,1)S(1)}, u32[]{:S(2)}) copy-start(bf16[10,128,128]{2,1,0:T(8,128)(2,1)S(1)} %collective-permute-done.8.refs_6_) | copy-start | bytes 983044
  95.8 4.2 %copy-start.6 = (bf16[10,128,128]{2,1,0:T(8,128)(2,1)}, bf16[10,128,128]{2,1,0:T(8,128)(2,1)S(1)}, u32[]{:S(2)}) copy-start(bf16[10,128,128]{2,1,0:T(8,128)(2,1)S(1)} %collective-permute-done.7.refs_5_) | copy-start | bytes 983044
  95.8 10.2 %collective-permute-start.18 = (bf16[20,256,128]{2,1,0:T(8,128)(2,1)S(1)}, bf16[20,256,128]{2,1,0:T(8,128)(2,1)}, u32[]{:S(2)}, u32[]{:S(2)}) collective-permute-start(bf16[20,256,128]{2,1,0:T(8,128)(2,1)S(1)} %all-to-all-done.2.refs_2_), channel_id=1, source_target_pairs={{0,1},{1,0},{2,3},{3,2},{4,5},{5,4},{6,7},{7,6},{8,9},{9,8},{10,11... | collective-permute-start | bytes 3932168 | tf_op jit(solution)/shard_map/ppermute | solution.py:242
  100.0 6.1 %copy-start.8 = (s32[8]{0:T(128)S(1)}, s32[8]{0:T(128)}, u32[]{:S(2)}) copy-start(s32[8]{0:T(128)} %refs_1_.7) | copy-start | bytes 100
  100.0 22.2 %all-to-all-start.3 = ((bf16[20,256,128]{2,1,0:T(8,128)(2,1)}), bf16[20,256,128]{2,1,0:T(8,128)(2,1)S(1)}, u32[]{:S(2)}, u32[]{:S(2)}) async-start(bf16[20,256,128]{2,1,0:T(8,128)(2,1)} %bitcast.6), calls=%async_computation.3 | async-start | bytes 2621440 | tf_op jit(solution)/shard_map/all_to_all | solution.py:254
  103.6 11.4 %collective-permute-start.17 = (bf16[10,128,128]{2,1,0:T(8,128)(2,1)S(1)}, bf16[10,128,128]{2,1,0:T(8,128)(2,1)}, u32[]{:S(2)}, u32[]{:S(2)}) collective-permute-start(bf16[10,128,128]{2,1,0:T(8,128)(2,1)S(1)} %add_convert_fusion.2.refs_4_), channel_id=1, source_target_pairs={{0,96},{32,0},{64,32},{96,64},{1,97},{33,1},{65,33},{97,65},{2,98}... | collective-permute-start | bytes 983048 | tf_op jit(solution)/shard_map/ppermute | solution.py:242
  103.9 11.0 %collective-permute-start.16 = (bf16[10,128,128]{2,1,0:T(8,128)(2,1)S(1)}, bf16[10,128,128]{2,1,0:T(8,128)(2,1)}, u32[]{:S(2)}, u32[]{:S(2)}) collective-permute-start(bf16[10,128,128]{2,1,0:T(8,128)(2,1)S(1)} %add_convert_fusion.2.refs_4_), channel_id=1, source_target_pairs={{0,64},{32,96},{64,0},{96,32},{1,65},{33,97},{65,1},{97,33},{2,66}... | collective-permute-start | bytes 983048 | tf_op jit(solution)/shard_map/ppermute | solution.py:242
  105.6 16.6 %collective-permute-start.15 = (bf16[10,128,128]{2,1,0:T(8,128)(2,1)S(1)}, bf16[10,128,128]{2,1,0:T(8,128)(2,1)}, u32[]{:S(2)}, u32[]{:S(2)}) collective-permute-start(bf16[10,128,128]{2,1,0:T(8,128)(2,1)S(1)} %add_convert_fusion.2.refs_4_), channel_id=1, source_target_pairs={{0,32},{32,64},{64,96},{96,0},{1,33},{33,65},{65,97},{97,1},{2,34}... | collective-permute-start | bytes 983048 | tf_op jit(solution)/shard_map/ppermute | solution.py:242
  122.2 3.2 %collective-permute-start.19 = (bf16[20,256,128]{2,1,0:T(8,128)(2,1)S(1)}, bf16[20,256,128]{2,1,0:T(8,128)(2,1)S(1)}, u32[]{:S(2)}, u32[]{:S(2)}) collective-permute-start(bf16[20,256,128]{2,1,0:T(8,128)(2,1)S(1)} %all-to-all-done.3.refs_2_), channel_id=1, source_target_pairs={{0,1},{1,0},{2,3},{3,2},{4,5},{5,4},{6,7},{7,6},{8,9},{9,8},{10,11... | collective-permute-start | bytes 3932168 | tf_op jit(solution)/shard_map/ppermute | solution.py:242
  (5 other events, 5.1 us)

commit v5 on v4

--- a/solution.py
+++ b/solution.py
@@ -52,8 +52,17 @@
         def _(c):
             fetch(s, c).start()
 
-    for s in range(len(plan)):
-        first, _, _, chunk, chunks = plan[s]
+    def send(piece):
+        part, which = divmod(piece, CORE)
+        k = jnp.where(core == which, 1, 0)
+        for to in range(CORE):
+            copy = pltpu.make_async_copy(
+                out_buf.at[pl.ds(piece * HALF, HALF)], outs[part * CORE + to], out_sem.at[part * CORE + to]
+            )
+            pl.when(k == to)(copy.start)
+
+    for s in range(len(plan)):
+        first, _, blocks, chunk, chunks = plan[s]
         edges[s].wait()
 
         @pl.loop(0, chunks)
@@ -63,21 +72,18 @@
             for k in range(CHUNK):
                 out_buf[first + c * CHUNK + k] = term[:, k * WIDTH : (k + 1) * WIDTH].astype(out_buf.dtype)
 
+        for piece in range(2 * CORE):
+            edge = (piece + 1) * HALF
+            pl.when((first < edge) & (first + blocks >= edge))(lambda piece=piece: send(piece))
+
     @pl.loop(used, 2 * PART)
     def _(q):
         out_buf[q] = jnp.zeros(out_buf.shape[1:], out_buf.dtype)
 
-    copies = [
-        pltpu.make_async_copy(
-            out_buf.at[pl.ds(part * PART + which * HALF, HALF)], outs[part * CORE + k], out_sem.at[part * CORE + k]
-        )
-        for part in range(2)
-        for k, which in enumerate((1 - core, core))
-    ]
-    for copy in copies:
-        copy.start()
-    for copy in copies:
-        copy.wait()
+    for piece in range(2 * CORE):
+        pl.when(used < (piece + 1) * HALF)(lambda piece=piece: send(piece))
+    for k in range(2 * CORE):
+        pltpu.make_async_copy(out_buf.at[pl.ds(0, HALF)], outs[k], out_sem.at[k]).wait()
 
 
 def left_terms(core, sizes, edge, site):

time: 133 us -> 132 us (level)
  transfers between devices with their start and end apart: 24 -> 24, of which waited for: 9 -> 10; matrix products, arithmetic and copies ran while one was open for 9% -> 9% of each run, Pallas kernels for 14% -> 14%
where the time goes in v5:
time: 132 us; the launch traced here: 131 us
  starting transfers between devices  45.8 us (35%)
  waiting for transfers between devices  35.7 us (27%)
  Pallas kernels  32.5 us (25%)
  local copies, waits for them, and re-layouts  8.88 us (7%)
  other arithmetic  8.2 us (6%)
    ppermute x20, waiting for transfers between devices, shift(): lax.ppermute(array, axis, [(i, (i + step) % size) for i in range(size)])  33.2 us
    ppermute x20, starting transfers between devices, shift(): lax.ppermute(array, axis, [(i, (i + step) % size) for i in range(size)])  30.1 us
    all_to_all x4, starting transfers between devices, over_y(): return lax.all_to_all(array, 'y', 0, 0, tiled=True)  15.7 us
    pallas_call x2, Pallas kernels, right_terms(): pl.pallas_call(lambda *refs: right_kernel(part, *refs), out_shape=[jax.Sh...  13.4 us
    pallas_call x2, Pallas kernels, product(): pl.pallas_call(lambda *refs: product_kernel(part, scale, *refs), out_shap...  10.7 us
    pallas_call x1, Pallas kernels, left_terms(): pl.pallas_call(left_kernel, out_shape=[jax.ShapeDtypeStruct((HALF, rows,...  8.36 us
    convert_element_type x10, other arithmetic, total(): sum((term.astype(jnp.float32) for term in terms)).astype(jnp.bfloat16)  8.13 us
    unnamed x26, local copies, waits for them, and re-layouts  5.15 us
  transfers between devices with their start and end apart: 24, of which 10 were waited for; matrix products, arithmetic and copies ran while one was open for 9% of the time, Pallas kernels for 14%

profile of v5, /device:TPU:1, one launch (start us, length us, event | category | flops | bytes accessed | tf_op | source)
XLA Modules:
  0.0 131.4 jit_solution(5859463296332474878)
XLA Ops:
  0.0 8.4 %left.1 = (bf16[20,256,128]{2,1,0:T(8,128)(2,1)}, bf16[20,256,128]{2,1,0:T(8,128)(2,1)}, bf16[20,256,128]{2,1,0:T(8,128)(2,1)}, bf16[20,256,128]{2,1,0:T(8,128)(2,1)}) custom-call(s32[1]{0:T(128)} %bitcast.at_ref, s32[8]{0:T(128)} %refs_1_.7, bf16[8,256,256]{2,1,0:T(8,128)(2,1)} %edge_ref.1, bf16[8,256,2048]{2,1,0:T(8,128)(2,1)} %site_ref.1), custom_call_target="tpu_custom_call" | custom-call | flops 1342177280 | bytes 12582912 | tf_op jit(solution)/shard_map/left/pallas_call | solution.py:92
  8.4 1.5 %collective-permute-start = (bf16[20,256,128]{2,1,0:T(8,128)(2,1)}, bf16[20,256,128]{2,1,0:T(8,128)(2,1)S(1)}, u32[]{:S(2)}, u32[]{:S(2)}) collective-permute-start(bf16[20,256,128]{2,1,0:T(8,128)(2,1)} %get-tuple-element.57), channel_id=1, source_target_pairs={{0,1},{1,0},{2,3},{3,2},{4,5},{5,4},{6,7},{7,6},{8,9},{9,8},{10,11... | collective-permute-start | bytes 3932168 | tf_op jit(solution)/shard_map/ppermute | solution.py:248
  10.0 6.9 %right.2 = (bf16[10,128,128]{2,1,0:T(8,128)(2,1)}, bf16[10,128,128]{2,1,0:T(8,128)(2,1)}, bf16[10,128,128]{2,1,0:T(8,128)(2,1)}, bf16[10,128,128]{2,1,0:T(8,128)(2,1)}) custom-call(s32[1]{0:T(128)} %bitcast.1.refs_0_, s32[8]{0:T(128)} %refs_1_.7, bf16[8,2048,512]{2,1,0:T(8,128)(2,1)} %refs_2_.1, bf16[8,512,128]{2,1,0:T(8,128)(2,1)} %refs_3_.1), custom_call_target="tpu_custom_call" | custom-call | flops 671088640 | bytes 10485760 | tf_op jit(solution)/shard_map/right/pallas_call | solution.py:155
  16.9 1.4 %add_convert_fusion.1 = bf16[20,256,128]{2,1,0:T(8,128)(2,1)} fusion(bf16[20,256,128]{2,1,0:T(8,128)(2,1)S(1)} %collective-permute-done, bf16[20,256,128]{2,1,0:T(8,128)(2,1)S(1)} %copy-done.10), kind=kLoop, calls=%fused_computation.1 | loop fusion | flops 2621440 | bytes 3932160 | tf_op jit(solution)/shard_map/convert_element_type | solution.py:252
  18.4 4.4 %all-to-all-start = ((bf16[20,256,128]{2,1,0:T(8,128)(2,1)}), bf16[20,256,128]{2,1,0:T(8,128)(2,1)S(1)}, u32[]{:S(2)}, u32[]{:S(2)}) async-start(bf16[20,256,128]{2,1,0:T(8,128)(2,1)} %add_convert_fusion.1), calls=%async_computation | async-start | bytes 2621440 | tf_op jit(solution)/shard_map/all_to_all | solution.py:260
  22.8 1.6 %collective-permute-start.3 = (bf16[10,128,128]{2,1,0:T(8,128)(2,1)}, bf16[10,128,128]{2,1,0:T(8,128)(2,1)}, u32[]{:S(2)}, u32[]{:S(2)}) collective-permute-start(bf16[10,128,128]{2,1,0:T(8,128)(2,1)} %get-tuple-element.82), channel_id=1, source_target_pairs={{0,32},{32,64},{64,96},{96,0},{1,33},{33,65},{65,97},{97,1},{2,34}... | collective-permute-start | bytes 983048 | tf_op jit(solution)/shard_map/ppermute | solution.py:248
  24.4 3.3 %collective-permute-start.4 = (bf16[10,128,128]{2,1,0:T(8,128)(2,1)}, bf16[10,128,128]{2,1,0:T(8,128)(2,1)}, u32[]{:S(2)}, u32[]{:S(2)}) collective-permute-start(bf16[10,128,128]{2,1,0:T(8,128)(2,1)} %get-tuple-element.83), channel_id=1, source_target_pairs={{0,64},{32,96},{64,0},{96,32},{1,65},{33,97},{65,1},{97,33},{2,66}... | collective-permute-start | bytes 983048 | tf_op jit(solution)/shard_map/ppermute | solution.py:248
  28.4 2.7 %add_convert_fusion = bf16[20,256,128]{2,1,0:T(8,128)(2,1)} fusion(bf16[20,256,128]{2,1,0:T(8,128)(2,1)} %collective-permute-done.1, bf16[20,256,128]{2,1,0:T(8,128)(2,1)S(1)} %copy-done.9), kind=kLoop, calls=%fused_computation | loop fusion | flops 2621440 | bytes 3932160 | tf_op jit(solution)/shard_map/convert_element_type | solution.py:252
  31.2 6.5 %right.3 = (bf16[10,128,128]{2,1,0:T(8,128)(2,1)}, bf16[10,128,128]{2,1,0:T(8,128)(2,1)}, bf16[10,128,128]{2,1,0:T(8,128)(2,1)}, bf16[10,128,128]{2,1,0:T(8,128)(2,1)}) custom-call(s32[1]{0:T(128)} %bitcast.1.refs_0_, s32[8]{0:T(128)} %refs_1_.7, bf16[8,2048,512]{2,1,0:T(8,128)(2,1)} %refs_2_.1, bf16[8,512,128]{2,1,0:T(8,128)(2,1)} %refs_3_.1), custom_call_target="tpu_custom_call" | custom-call | flops 671088640 | bytes 10485760 | tf_op jit(solution)/shard_map/right/pallas_call | solution.py:155
  37.7 2.5 %all-to-all-done = bf16[20,256,128]{2,1,0:T(8,128)(2,1)S(1)} async-done(((bf16[20,256,128]{2,1,0:T(8,128)(2,1)}), bf16[20,256,128]{2,1,0:T(8,128)(2,1)S(1)}, u32[]{:S(2)}, u32[]{:S(2)}) %all-to-all-start) | async-done | bytes 1310752 | tf_op jit(solution)/shard_map/all_to_all | solution.py:260
  40.4 3.7 %all-to-all-start.1 = ((bf16[20,256,128]{2,1,0:T(8,128)(2,1)}), bf16[20,256,128]{2,1,0:T(8,128)(2,1)S(1)}, u32[]{:S(2)}, u32[]{:S(2)}) async-start(bf16[20,256,128]{2,1,0:T(8,128)(2,1)} %add_convert_fusion), calls=%async_computation.1 | async-start | bytes 2621440 | tf_op jit(solution)/shard_map/all_to_all | solution.py:260
  44.1 1.4 %add_convert_fusion.7 = bf16[10,128,128]{2,1,0:T(8,128)(2,1)S(1)} fusion(bf16[10,128,128]{2,1,0:T(8,128)(2,1)} %collective-permute-done.5, bf16[10,128,128]{2,1,0:T(8,128)(2,1)} %collective-permute-done.4, bf16[10,128,128]{2,1,0:T(8,128)(2,1)} %collective-permute-done.3, bf16[10,128,128]{2,1,0:T(8,128)(2,1)S(1)} %copy-done.12), kind=kLoop, calls=%fused_computation.7 | loop fusion | flops 1310720 | bytes 1638400 | tf_op jit(solution)/shard_map/convert_element_type | solution.py:252
  46.7 2.5 %collective-permute-start.2 = (bf16[5,256,128]{2,1,0:T(8,128)(2,1)S(1)}, bf16[5,256,128]{2,1,0:T(8,128)(2,1)S(1)}, u32[]{:S(2)}, u32[]{:S(2)}) collective-permute-start(bf16[5,256,128]{2,1,0:T(8,128)(2,1)S(1)} %add_convert_fusion.9), channel_id=1, source_target_pairs={{0,2},{2,0},{1,3},{3,1},{4,6},{6,4},{5,7},{7,5},{8,10},{10,8},{9,1... | collective-permute-start | bytes 983048 | tf_op jit(solution)/shard_map/ppermute | solution.py:248
  49.2 4.1 %collective-permute-done.6 = bf16[10,128,128]{2,1,0:T(8,128)(2,1)S(1)} collective-permute-done((bf16[10,128,128]{2,1,0:T(8,128)(2,1)S(1)}, bf16[10,128,128]{2,1,0:T(8,128)(2,1)S(1)}, u32[]{:S(2)}, u32[]{:S(2)}) %collective-permute-start.6) | collective-permute-done | bytes 327712 | tf_op jit(solution)/shard_map/ppermute | solution.py:248
  53.4 1.5 %collective-permute-start.11 = (bf16[10,128,128]{2,1,0:T(8,128)(2,1)}, bf16[10,128,128]{2,1,0:T(8,128)(2,1)S(1)}, u32[]{:S(2)}, u32[]{:S(2)}) collective-permute-start(bf16[10,128,128]{2,1,0:T(8,128)(2,1)} %get-tuple-element.91), channel_id=1, source_target_pairs={{0,32},{32,64},{64,96},{96,0},{1,33},{33,65},{65,97},{97,1},{2,34}... | collective-permute-start | bytes 983048 | tf_op jit(solution)/shard_map/ppermute | solution.py:248
  54.9 3.3 %collective-permute-start.12 = (bf16[10,128,128]{2,1,0:T(8,128)(2,1)}, bf16[10,128,128]{2,1,0:T(8,128)(2,1)S(1)}, u32[]{:S(2)}, u32[]{:S(2)}) collective-permute-start(bf16[10,128,128]{2,1,0:T(8,128)(2,1)} %get-tuple-element.92), channel_id=1, source_target_pairs={{0,64},{32,96},{64,0},{96,32},{1,65},{33,97},{65,1},{97,33},{2,66}... | collective-permute-start | bytes 983048 | tf_op jit(solution)/shard_map/ppermute | solution.py:248
  58.9 3.6 %collective-permute-done.2 = bf16[5,256,128]{2,1,0:T(8,128)(2,1)S(1)} collective-permute-done((bf16[5,256,128]{2,1,0:T(8,128)(2,1)S(1)}, bf16[5,256,128]{2,1,0:T(8,128)(2,1)S(1)}, u32[]{:S(2)}, u32[]{:S(2)}) %collective-permute-start.2) | collective-permute-done | bytes 327712 | tf_op jit(solution)/shard_map/ppermute | solution.py:248
  62.8 1.4 %broadcast_in_dim.4 = bf16[4,5,256,128]{3,2,1,0:T(8,128)(2,1)} broadcast(bf16[5,256,128]{2,1,0:T(8,128)(2,1)S(1)} %add_convert_fusion.8), dimensions={1,2,3} | broadcast | bytes 1638400 | tf_op jit(solution)/shard_map/broadcast_in_dim | solution.py:280
  64.2 4.0 %all-to-all-start.2 = ((bf16[20,256,128]{2,1,0:T(8,128)(2,1)}), bf16[20,256,128]{2,1,0:T(8,128)(2,1)S(1)}, u32[]{:S(2)}, u32[]{:S(2)}) async-start(bf16[20,256,128]{2,1,0:T(8,128)(2,1)} %bitcast.4), calls=%async_computation.2 | async-start | bytes 2621440 | tf_op jit(solution)/shard_map/all_to_all | solution.py:260
  71.9 2.5 %collective-permute-start.10 = (bf16[5,256,128]{2,1,0:T(8,128)(2,1)S(1)}, bf16[5,256,128]{2,1,0:T(8,128)(2,1)S(1)}, u32[]{:S(2)}, u32[]{:S(2)}) collective-permute-start(bf16[5,256,128]{2,1,0:T(8,128)(2,1)S(1)} %add_convert_fusion.5), channel_id=1, source_target_pairs={{0,2},{2,0},{1,3},{3,1},{4,6},{6,4},{5,7},{7,5},{8,10},{10,8},{9,1... | collective-permute-start | bytes 983048 | tf_op jit(solution)/shard_map/ppermute | solution.py:248
  74.4 3.6 %collective-permute-start.9 = (bf16[10,128,128]{2,1,0:T(8,128)(2,1)S(1)}, bf16[10,128,128]{2,1,0:T(8,128)(2,1)S(1)}, u32[]{:S(2)}, u32[]{:S(2)}) collective-permute-start(bf16[10,128,128]{2,1,0:T(8,128)(2,1)S(1)} %add_convert_fusion.6.refs_4_), channel_id=1, source_target_pairs={{0,96},{32,0},{64,32},{96,64},{1,97},{33,1},{65,33},{97,65},{2,98}... | collective-permute-start | bytes 983048 | tf_op jit(solution)/shard_map/ppermute | solution.py:248
  77.9 1.6 %collective-permute-start.8 = (bf16[10,128,128]{2,1,0:T(8,128)(2,1)S(1)}, bf16[10,128,128]{2,1,0:T(8,128)(2,1)S(1)}, u32[]{:S(2)}, u32[]{:S(2)}) collective-permute-start(bf16[10,128,128]{2,1,0:T(8,128)(2,1)S(1)} %add_convert_fusion.6.refs_4_), channel_id=1, source_target_pairs={{0,64},{32,96},{64,0},{96,32},{1,65},{33,97},{65,1},{97,33},{2,66}... | collective-permute-start | bytes 983048 | tf_op jit(solution)/shard_map/ppermute | solution.py:248
  79.7 4.8 %collective-permute-done.10 = bf16[5,256,128]{2,1,0:T(8,128)(2,1)S(1)} collective-permute-done((bf16[5,256,128]{2,1,0:T(8,128)(2,1)S(1)}, bf16[5,256,128]{2,1,0:T(8,128)(2,1)S(1)}, u32[]{:S(2)}, u32[]{:S(2)}) %collective-permute-start.10) | collective-permute-done | bytes 327712 | tf_op jit(solution)/shard_map/ppermute | solution.py:248
  85.7 9.1 %collective-permute-done.7.refs_5_ = bf16[10,128,128]{2,1,0:T(8,128)(2,1)S(1)} collective-permute-done((bf16[10,128,128]{2,1,0:T(8,128)(2,1)S(1)}, bf16[10,128,128]{2,1,0:T(8,128)(2,1)S(1)}, u32[]{:S(2)}, u32[]{:S(2)}) %collective-permute-start.7) | collective-permute-done | bytes 327712 | tf_op jit(solution)/shard_map/ppermute | solution.py:248
  94.8 1.8 %collective-permute-start.18 = (bf16[20,256,128]{2,1,0:T(8,128)(2,1)S(1)}, bf16[20,256,128]{2,1,0:T(8,128)(2,1)}, u32[]{:S(2)}, u32[]{:S(2)}) collective-permute-start(bf16[20,256,128]{2,1,0:T(8,128)(2,1)S(1)} %all-to-all-done.2.refs_2_), channel_id=1, source_target_pairs={{0,1},{1,0},{2,3},{3,2},{4,5},{5,4},{6,7},{7,6},{8,9},{9,8},{10,11... | collective-permute-start | bytes 3932168 | tf_op jit(solution)/shard_map/ppermute | solution.py:248
  96.6 2.4 %broadcast_in_dim.5 = bf16[4,5,256,128]{3,2,1,0:T(8,128)(2,1)} broadcast(bf16[5,256,128]{2,1,0:T(8,128)(2,1)} %add_convert_fusion.4), dimensions={1,2,3} | broadcast | bytes 1638400 | tf_op jit(solution)/shard_map/broadcast_in_dim | solution.py:280
  98.9 3.6 %all-to-all-start.3 = ((bf16[20,256,128]{2,1,0:T(8,128)(2,1)}), bf16[20,256,128]{2,1,0:T(8,128)(2,1)S(1)}, u32[]{:S(2)}, u32[]{:S(2)}) async-start(bf16[20,256,128]{2,1,0:T(8,128)(2,1)} %bitcast.6), calls=%async_computation.3 | async-start | bytes 2621440 | tf_op jit(solution)/shard_map/all_to_all | solution.py:260
  102.9 1.6 %collective-permute-start.16 = (bf16[10,128,128]{2,1,0:T(8,128)(2,1)S(1)}, bf16[10,128,128]{2,1,0:T(8,128)(2,1)}, u32[]{:S(2)}, u32[]{:S(2)}) collective-permute-start(bf16[10,128,128]{2,1,0:T(8,128)(2,1)S(1)} %add_convert_fusion.2.refs_4_), channel_id=1, source_target_pairs={{0,64},{32,96},{64,0},{96,32},{1,65},{33,97},{65,1},{97,33},{2,66}... | collective-permute-start | bytes 983048 | tf_op jit(solution)/shard_map/ppermute | solution.py:248
  107.9 5.0 %product.1.refs_8_ = f32[8,256,128]{2,1,0:T(8,128)S(1)} custom-call(s32[4]{0:T(128)S(1)} %pad_add_fusion.refs_0_, s32[8]{0:T(128)S(1)} %copy-done.8, bf16[20,256,128]{2,1,0:T(8,128)(2,1)S(1)} %all-to-all-done.2.refs_2_, bf16[20,256,128]{2,1,0:T(8,128)(2,1)} %collective-permute-done.18.refs_3_, bf16[10,128,128]{2,1,0:T(8,128)(2,1)S(1)} %add_convert_fusion.6.refs_4_, ...), custom_call_target="tpu_custom_call" | custom-call | flops 335544320 | bytes 6291456 | tf_op jit(solution)/shard_map/product/pallas_call | solution.py:228
  113.9 7.3 %collective-permute-done.15.refs_5_ = bf16[10,128,128]{2,1,0:T(8,128)(2,1)} collective-permute-done((bf16[10,128,128]{2,1,0:T(8,128)(2,1)S(1)}, bf16[10,128,128]{2,1,0:T(8,128)(2,1)}, u32[]{:S(2)}, u32[]{:S(2)}) %collective-permute-start.15) | collective-permute-done | bytes 327712 | tf_op jit(solution)/shard_map/ppermute | solution.py:248
  121.7 2.7 %collective-permute-done.19.refs_3_ = bf16[20,256,128]{2,1,0:T(8,128)(2,1)S(1)} collective-permute-done((bf16[20,256,128]{2,1,0:T(8,128)(2,1)S(1)}, bf16[20,256,128]{2,1,0:T(8,128)(2,1)S(1)}, u32[]{:S(2)}, u32[]{:S(2)}) %collective-permute-start.19) | collective-permute-done | bytes 1310752 | tf_op jit(solution)/shard_map/ppermute | solution.py:248
  125.5 5.7 %product_end.1 = bf16[8,256,128]{2,1,0:T(8,128)(2,1)} custom-call(s32[4]{0:T(128)S(1)} %pad_add_fusion.refs_0_, s32[8]{0:T(128)S(1)} %copy-done.8, bf16[20,256,128]{2,1,0:T(8,128)(2,1)S(1)} %all-to-all-done.3.refs_2_, bf16[20,256,128]{2,1,0:T(8,128)(2,1)S(1)} %collective-permute-done.19.refs_3_, bf16[10,128,128]{2,1,0:T(8,128)(2,1)S(1)} %add_convert_fusion.2.refs_4_, ...), custom_call_target="tpu_custom_call" | custom-call | flops 335544320 | bytes 6291456 | tf_op jit(solution)/shard_map/product_end/pallas_call | solution.py:228
  (60 shorter events, 14.8 us)
Async XLA Ops:
  8.4 8.6 %collective-permute-start = (bf16[20,256,128]{2,1,0:T(8,128)(2,1)}, bf16[20,256,128]{2,1,0:T(8,128)(2,1)S(1)}, u32[]{:S(2)}, u32[]{:S(2)}) collective-permute-start(bf16[20,256,128]{2,1,0:T(8,128)(2,1)} %get-tuple-element.57), channel_id=1, source_target_pairs={{0,1},{1,0},{2,3},{3,2},{4,5},{5,4},{6,7},{7,6},{8,9},{9,8},{10,11... | collective-permute-start | bytes 3932168 | tf_op jit(solution)/shard_map/ppermute | solution.py:248
  9.9 18.6 %collective-permute-start.1 = (bf16[20,256,128]{2,1,0:T(8,128)(2,1)}, bf16[20,256,128]{2,1,0:T(8,128)(2,1)}, u32[]{:S(2)}, u32[]{:S(2)}) collective-permute-start(bf16[20,256,128]{2,1,0:T(8,128)(2,1)} %get-tuple-element.76), channel_id=1, source_target_pairs={{0,1},{1,0},{2,3},{3,2},{4,5},{5,4},{6,7},{7,6},{8,9},{9,8},{10,11... | collective-permute-start | bytes 3932168 | tf_op jit(solution)/shard_map/ppermute | solution.py:248
  10.0 7.0 %copy-start.10 = (bf16[20,256,128]{2,1,0:T(8,128)(2,1)S(1)}, bf16[20,256,128]{2,1,0:T(8,128)(2,1)}, u32[]{:S(2)}) copy-start(bf16[20,256,128]{2,1,0:T(8,128)(2,1)} %get-tuple-element.56) | copy-start | bytes 3932164
  18.4 10.1 %copy-start.9 = (bf16[20,256,128]{2,1,0:T(8,128)(2,1)S(1)}, bf16[20,256,128]{2,1,0:T(8,128)(2,1)}, u32[]{:S(2)}) copy-start(bf16[20,256,128]{2,1,0:T(8,128)(2,1)} %get-tuple-element.75) | copy-start | bytes 3932164
  18.4 21.8 %all-to-all-start = ((bf16[20,256,128]{2,1,0:T(8,128)(2,1)}), bf16[20,256,128]{2,1,0:T(8,128)(2,1)S(1)}, u32[]{:S(2)}, u32[]{:S(2)}) async-start(bf16[20,256,128]{2,1,0:T(8,128)(2,1)} %add_convert_fusion.1), calls=%async_computation | async-start | bytes 2621440 | tf_op jit(solution)/shard_map/all_to_all | solution.py:260
  22.8 21.3 %collective-permute-start.3 = (bf16[10,128,128]{2,1,0:T(8,128)(2,1)}, bf16[10,128,128]{2,1,0:T(8,128)(2,1)}, u32[]{:S(2)}, u32[]{:S(2)}) collective-permute-start(bf16[10,128,128]{2,1,0:T(8,128)(2,1)} %get-tuple-element.82), channel_id=1, source_target_pairs={{0,32},{32,64},{64,96},{96,0},{1,33},{33,65},{65,97},{97,1},{2,34}... | collective-permute-start | bytes 983048 | tf_op jit(solution)/shard_map/ppermute | solution.py:248
  24.4 19.7 %collective-permute-start.4 = (bf16[10,128,128]{2,1,0:T(8,128)(2,1)}, bf16[10,128,128]{2,1,0:T(8,128)(2,1)}, u32[]{:S(2)}, u32[]{:S(2)}) collective-permute-start(bf16[10,128,128]{2,1,0:T(8,128)(2,1)} %get-tuple-element.83), channel_id=1, source_target_pairs={{0,64},{32,96},{64,0},{96,32},{1,65},{33,97},{65,1},{97,33},{2,66}... | collective-permute-start | bytes 983048 | tf_op jit(solution)/shard_map/ppermute | solution.py:248
  27.7 16.4 %collective-permute-start.5 = (bf16[10,128,128]{2,1,0:T(8,128)(2,1)}, bf16[10,128,128]{2,1,0:T(8,128)(2,1)}, u32[]{:S(2)}, u32[]{:S(2)}) collective-permute-start(bf16[10,128,128]{2,1,0:T(8,128)(2,1)} %get-tuple-element.84), channel_id=1, source_target_pairs={{0,96},{32,0},{64,32},{96,64},{1,97},{33,1},{65,33},{97,65},{2,98}... | collective-permute-start | bytes 983048 | tf_op jit(solution)/shard_map/ppermute | solution.py:248
  40.4 3.7 %copy-start.12 = (bf16[10,128,128]{2,1,0:T(8,128)(2,1)S(1)}, bf16[10,128,128]{2,1,0:T(8,128)(2,1)}, u32[]{:S(2)}) copy-start(bf16[10,128,128]{2,1,0:T(8,128)(2,1)} %get-tuple-element.81) | copy-start | bytes 983044
  40.4 22.2 %all-to-all-start.1 = ((bf16[20,256,128]{2,1,0:T(8,128)(2,1)}), bf16[20,256,128]{2,1,0:T(8,128)(2,1)S(1)}, u32[]{:S(2)}, u32[]{:S(2)}) async-start(bf16[20,256,128]{2,1,0:T(8,128)(2,1)} %add_convert_fusion), calls=%async_computation.1 | async-start | bytes 2621440 | tf_op jit(solution)/shard_map/all_to_all | solution.py:260
  45.5 7.8 %collective-permute-start.6 = (bf16[10,128,128]{2,1,0:T(8,128)(2,1)S(1)}, bf16[10,128,128]{2,1,0:T(8,128)(2,1)S(1)}, u32[]{:S(2)}, u32[]{:S(2)}) collective-permute-start(bf16[10,128,128]{2,1,0:T(8,128)(2,1)S(1)} %add_convert_fusion.7), channel_id=1, source_target_pairs={{0,16},{16,0},{1,17},{17,1},{2,18},{18,2},{3,19},{19,3},{4,20},{20... | collective-permute-start | bytes 983048 | tf_op jit(solution)/shard_map/ppermute | solution.py:248
  46.7 15.8 %collective-permute-start.2 = (bf16[5,256,128]{2,1,0:T(8,128)(2,1)S(1)}, bf16[5,256,128]{2,1,0:T(8,128)(2,1)S(1)}, u32[]{:S(2)}, u32[]{:S(2)}) collective-permute-start(bf16[5,256,128]{2,1,0:T(8,128)(2,1)S(1)} %add_convert_fusion.9), channel_id=1, source_target_pairs={{0,2},{2,0},{1,3},{3,1},{4,6},{6,4},{5,7},{7,5},{8,10},{10,8},{9,1... | collective-permute-start | bytes 983048 | tf_op jit(solution)/shard_map/ppermute | solution.py:248
  53.4 14.8 %collective-permute-start.11 = (bf16[10,128,128]{2,1,0:T(8,128)(2,1)}, bf16[10,128,128]{2,1,0:T(8,128)(2,1)S(1)}, u32[]{:S(2)}, u32[]{:S(2)}) collective-permute-start(bf16[10,128,128]{2,1,0:T(8,128)(2,1)} %get-tuple-element.91), channel_id=1, source_target_pairs={{0,32},{32,64},{64,96},{96,0},{1,33},{33,65},{65,97},{97,1},{2,34}... | collective-permute-start | bytes 983048 | tf_op jit(solution)/shard_map/ppermute | solution.py:248
  54.9 13.4 %collective-permute-start.12 = (bf16[10,128,128]{2,1,0:T(8,128)(2,1)}, bf16[10,128,128]{2,1,0:T(8,128)(2,1)S(1)}, u32[]{:S(2)}, u32[]{:S(2)}) collective-permute-start(bf16[10,128,128]{2,1,0:T(8,128)(2,1)} %get-tuple-element.92), channel_id=1, source_target_pairs={{0,64},{32,96},{64,0},{96,32},{1,65},{33,97},{65,1},{97,33},{2,66}... | collective-permute-start | bytes 983048 | tf_op jit(solution)/shard_map/ppermute | solution.py:248
  58.2 11.3 %collective-permute-start.13 = (bf16[10,128,128]{2,1,0:T(8,128)(2,1)}, bf16[10,128,128]{2,1,0:T(8,128)(2,1)}, u32[]{:S(2)}, u32[]{:S(2)}) collective-permute-start(bf16[10,128,128]{2,1,0:T(8,128)(2,1)} %get-tuple-element.93), channel_id=1, source_target_pairs={{0,96},{32,0},{64,32},{96,64},{1,97},{33,1},{65,33},{97,65},{2,98}... | collective-permute-start | bytes 983048 | tf_op jit(solution)/shard_map/ppermute | solution.py:248
  64.2 5.3 %copy-start.11 = (bf16[10,128,128]{2,1,0:T(8,128)(2,1)S(1)}, bf16[10,128,128]{2,1,0:T(8,128)(2,1)}, u32[]{:S(2)}) copy-start(bf16[10,128,128]{2,1,0:T(8,128)(2,1)} %get-tuple-element.90) | copy-start | bytes 983044
  64.2 30.6 %all-to-all-start.2 = ((bf16[20,256,128]{2,1,0:T(8,128)(2,1)}), bf16[20,256,128]{2,1,0:T(8,128)(2,1)S(1)}, u32[]{:S(2)}, u32[]{:S(2)}) async-start(bf16[20,256,128]{2,1,0:T(8,128)(2,1)} %bitcast.4), calls=%async_computation.2 | async-start | bytes 2621440 | tf_op jit(solution)/shard_map/all_to_all | solution.py:260
  70.6 9.0 %collective-permute-start.14 = (bf16[10,128,128]{2,1,0:T(8,128)(2,1)S(1)}, bf16[10,128,128]{2,1,0:T(8,128)(2,1)S(1)}, u32[]{:S(2)}, u32[]{:S(2)}) collective-permute-start(bf16[10,128,128]{2,1,0:T(8,128)(2,1)S(1)} %add_convert_fusion.3), channel_id=1, source_target_pairs={{0,16},{16,0},{1,17},{17,1},{2,18},{18,2},{3,19},{19,3},{4,20},{20... | collective-permute-start | bytes 983048 | tf_op jit(solution)/shard_map/ppermute | solution.py:248
  71.9 12.6 %collective-permute-start.10 = (bf16[5,256,128]{2,1,0:T(8,128)(2,1)S(1)}, bf16[5,256,128]{2,1,0:T(8,128)(2,1)S(1)}, u32[]{:S(2)}, u32[]{:S(2)}) collective-permute-start(bf16[5,256,128]{2,1,0:T(8,128)(2,1)S(1)} %add_convert_fusion.5), channel_id=1, source_target_pairs={{0,2},{2,0},{1,3},{3,1},{4,6},{6,4},{5,7},{7,5},{8,10},{10,8},{9,1... | collective-permute-start | bytes 983048 | tf_op jit(solution)/shard_map/ppermute | solution.py:248
  74.4 10.9 %collective-permute-start.9 = (bf16[10,128,128]{2,1,0:T(8,128)(2,1)S(1)}, bf16[10,128,128]{2,1,0:T(8,128)(2,1)S(1)}, u32[]{:S(2)}, u32[]{:S(2)}) collective-permute-start(bf16[10,128,128]{2,1,0:T(8,128)(2,1)S(1)} %add_convert_fusion.6.refs_4_), channel_id=1, source_target_pairs={{0,96},{32,0},{64,32},{96,64},{1,97},{33,1},{65,33},{97,65},{2,98}... | collective-permute-start | bytes 983048 | tf_op jit(solution)/shard_map/ppermute | solution.py:248
  77.9 7.8 %collective-permute-start.8 = (bf16[10,128,128]{2,1,0:T(8,128)(2,1)S(1)}, bf16[10,128,128]{2,1,0:T(8,128)(2,1)S(1)}, u32[]{:S(2)}, u32[]{:S(2)}) collective-permute-start(bf16[10,128,128]{2,1,0:T(8,128)(2,1)S(1)} %add_convert_fusion.6.refs_4_), channel_id=1, source_target_pairs={{0,64},{32,96},{64,0},{96,32},{1,65},{33,97},{65,1},{97,33},{2,66}... | collective-permute-start | bytes 983048 | tf_op jit(solution)/shard_map/ppermute | solution.py:248
  79.6 15.2 %collective-permute-start.7 = (bf16[10,128,128]{2,1,0:T(8,128)(2,1)S(1)}, bf16[10,128,128]{2,1,0:T(8,128)(2,1)S(1)}, u32[]{:S(2)}, u32[]{:S(2)}) collective-permute-start(bf16[10,128,128]{2,1,0:T(8,128)(2,1)S(1)} %add_convert_fusion.6.refs_4_), channel_id=1, source_target_pairs={{0,32},{32,64},{64,96},{96,0},{1,33},{33,65},{65,97},{97,1},{2,34}... | collective-permute-start | bytes 983048 | tf_op jit(solution)/shard_map/ppermute | solution.py:248
  85.3 13.6 %copy-start.2 = (bf16[10,128,128]{2,1,0:T(8,128)(2,1)}, bf16[10,128,128]{2,1,0:T(8,128)(2,1)S(1)}, u32[]{:S(2)}) copy-start(bf16[10,128,128]{2,1,0:T(8,128)(2,1)S(1)} %collective-permute-done.9.refs_7_) | copy-start | bytes 983044
  85.7 13.3 %copy-start.4 = (bf16[10,128,128]{2,1,0:T(8,128)(2,1)}, bf16[10,128,128]{2,1,0:T(8,128)(2,1)S(1)}, u32[]{:S(2)}) copy-start(bf16[10,128,128]{2,1,0:T(8,128)(2,1)S(1)} %collective-permute-done.8.refs_6_) | copy-start | bytes 983044
  94.8 4.1 %copy-start.6 = (bf16[10,128,128]{2,1,0:T(8,128)(2,1)}, bf16[10,128,128]{2,1,0:T(8,128)(2,1)S(1)}, u32[]{:S(2)}) copy-start(bf16[10,128,128]{2,1,0:T(8,128)(2,1)S(1)} %collective-permute-done.7.refs_5_) | copy-start | bytes 983044
  94.8 10.2 %collective-permute-start.18 = (bf16[20,256,128]{2,1,0:T(8,128)(2,1)S(1)}, bf16[20,256,128]{2,1,0:T(8,128)(2,1)}, u32[]{:S(2)}, u32[]{:S(2)}) collective-permute-start(bf16[20,256,128]{2,1,0:T(8,128)(2,1)S(1)} %all-to-all-done.2.refs_2_), channel_id=1, source_target_pairs={{0,1},{1,0},{2,3},{3,2},{4,5},{5,4},{6,7},{7,6},{8,9},{9,8},{10,11... | collective-permute-start | bytes 3932168 | tf_op jit(solution)/shard_map/ppermute | solution.py:248
  98.9 6.1 %copy-start.8 = (s32[8]{0:T(128)S(1)}, s32[8]{0:T(128)}, u32[]{:S(2)}) copy-start(s32[8]{0:T(128)} %refs_1_.7) | copy-start | bytes 100
  98.9 22.2 %all-to-all-start.3 = ((bf16[20,256,128]{2,1,0:T(8,128)(2,1)}), bf16[20,256,128]{2,1,0:T(8,128)(2,1)S(1)}, u32[]{:S(2)}, u32[]{:S(2)}) async-start(bf16[20,256,128]{2,1,0:T(8,128)(2,1)} %bitcast.6), calls=%async_computation.3 | async-start | bytes 2621440 | tf_op jit(solution)/shard_map/all_to_all | solution.py:260
  102.5 11.4 %collective-permute-start.17 = (bf16[10,128,128]{2,1,0:T(8,128)(2,1)S(1)}, bf16[10,128,128]{2,1,0:T(8,128)(2,1)}, u32[]{:S(2)}, u32[]{:S(2)}) collective-permute-start(bf16[10,128,128]{2,1,0:T(8,128)(2,1)S(1)} %add_convert_fusion.2.refs_4_), channel_id=1, source_target_pairs={{0,96},{32,0},{64,32},{96,64},{1,97},{33,1},{65,33},{97,65},{2,98}... | collective-permute-start | bytes 983048 | tf_op jit(solution)/shard_map/ppermute | solution.py:248
  102.9 11.0 %collective-permute-start.16 = (bf16[10,128,128]{2,1,0:T(8,128)(2,1)S(1)}, bf16[10,128,128]{2,1,0:T(8,128)(2,1)}, u32[]{:S(2)}, u32[]{:S(2)}) collective-permute-start(bf16[10,128,128]{2,1,0:T(8,128)(2,1)S(1)} %add_convert_fusion.2.refs_4_), channel_id=1, source_target_pairs={{0,64},{32,96},{64,0},{96,32},{1,65},{33,97},{65,1},{97,33},{2,66}... | collective-permute-start | bytes 983048 | tf_op jit(solution)/shard_map/ppermute | solution.py:248
  104.5 16.6 %collective-permute-start.15 = (bf16[10,128,128]{2,1,0:T(8,128)(2,1)S(1)}, bf16[10,128,128]{2,1,0:T(8,128)(2,1)}, u32[]{:S(2)}, u32[]{:S(2)}) collective-permute-start(bf16[10,128,128]{2,1,0:T(8,128)(2,1)S(1)} %add_convert_fusion.2.refs_4_), channel_id=1, source_target_pairs={{0,32},{32,64},{64,96},{96,0},{1,33},{33,65},{65,97},{97,1},{2,34}... | collective-permute-start | bytes 983048 | tf_op jit(solution)/shard_map/ppermute | solution.py:248
  121.2 3.2 %collective-permute-start.19 = (bf16[20,256,128]{2,1,0:T(8,128)(2,1)S(1)}, bf16[20,256,128]{2,1,0:T(8,128)(2,1)S(1)}, u32[]{:S(2)}, u32[]{:S(2)}) collective-permute-start(bf16[20,256,128]{2,1,0:T(8,128)(2,1)S(1)} %all-to-all-done.3.refs_2_), channel_id=1, source_target_pairs={{0,1},{1,0},{2,3},{3,2},{4,5},{5,4},{6,7},{7,6},{8,9},{9,8},{10,11... | collective-permute-start | bytes 3932168 | tf_op jit(solution)/shard_map/ppermute | solution.py:248
  (5 other events, 5.1 us)

commit v6 on v5

--- a/solution.py
+++ b/solution.py
@@ -111,9 +111,9 @@
 
 
 def right_kernel(lo, at_ref, size_ref, edge_ref, site_ref, *rest):
-    outs, (site_buf, edge_buf, term_buf, site_sem, edge_sem) = rest[:Z], rest[Z:]
+    outs, (site_buf, edge_buf, term_buf, site_sem, edge_sem, out_sem) = rest[:Z], rest[Z:]
     z = at_ref[0]
-    plan, _ = packed(size_ref, lo, lo + PART)
+    plan, used = packed(size_ref, lo, lo + PART)
     last = edge_ref.shape[1] // WIDTH - CHUNK
 
     def block_of(s, c):
@@ -132,8 +132,14 @@
         def _(c):
             fetch(s, c).start()
 
-    for s in range(len(plan)):
-        first, _, _, chunk, chunks = plan[s]
+    def send(owner):
+        piece = term_buf.at[pl.ds(owner * TWO + CHUNK, TWO)]
+        for step in range(Z):
+            copy = pltpu.make_async_copy(piece, outs[step], out_sem.at[step])
+            pl.when(lax.rem(z + step, Z) == owner)(copy.start)
+
+    for s in range(len(plan)):
+        first, begin, end, chunk, chunks = plan[s]
         pl.when(chunks > 0)(sites[s].wait)
 
         @pl.loop(0, chunks)
@@ -143,10 +149,14 @@
             q = first + block_of(s, c) - lo + CHUNK
             term_buf[pl.ds(q, CHUNK)] = term.astype(jnp.bfloat16).reshape(CHUNK, WIDTH, term.shape[1])
 
+        for owner in range(Z):
+            edge = lo + (owner + 1) * TWO
+            pl.when((first + begin < edge) & (first + end >= edge))(lambda owner=owner: send(owner))
+
+    for owner in range(Z):
+        pl.when(used < lo + (owner + 1) * TWO)(lambda owner=owner: send(owner))
     for step in range(Z):
-        base = lax.rem(z + step, Z) * TWO + CHUNK
-        for k in range(0, TWO, 2):
-            outs[step][k : k + 2] = term_buf[pl.ds(base + k, 2)]
+        pltpu.make_async_copy(term_buf.at[pl.ds(0, TWO)], outs[step], out_sem.at[step]).wait()
 
 
 def right_terms(part, z, sizes, edge, site):
@@ -156,13 +166,14 @@
         lambda *refs: right_kernel(part, *refs),
         out_shape=[jax.ShapeDtypeStruct((TWO, WIDTH, cols), jnp.bfloat16)] * Z,
         in_specs=[SMEM, SMEM, HBM, HBM],
-        out_specs=[VMEM] * Z,
+        out_specs=[ANY] * Z,
         scratch_shapes=[
             pltpu.VMEM((sectors, depth, cols), jnp.bfloat16),
             pltpu.VMEM((most, CHUNK * WIDTH, depth), jnp.bfloat16),
             pltpu.VMEM((PART + 2 * CHUNK, WIDTH, cols), jnp.bfloat16),
             pltpu.SemaphoreType.DMA((sectors,)),
             pltpu.SemaphoreType.DMA((most,)),
+            pltpu.SemaphoreType.DMA((Z,)),
         ],
         compiler_params=PARAMS,
         cost_estimate=pl.CostEstimate(

time: 132 us -> 132 us (level)
  transfers between devices with their start and end apart: 24 -> 24, of which waited for: 10 -> 9; matrix products, arithmetic and copies ran while one was open for 9% -> 9% of each run, Pallas kernels for 14% -> 13%
where the time goes in v6:
time: 132 us; the launch traced here: 131 us
  starting transfers between devices  45.7 us (35%)
  waiting for transfers between devices  36.2 us (27%)
  Pallas kernels  31.4 us (24%)
  local copies, waits for them, and re-layouts  8.88 us (7%)
  other arithmetic  8.2 us (6%)
    ppermute x20, waiting for transfers between devices, shift(): lax.ppermute(array, axis, [(i, (i + step) % size) for i in range(size)])  33.4 us
    ppermute x20, starting transfers between devices, shift(): lax.ppermute(array, axis, [(i, (i + step) % size) for i in range(size)])  30 us
    all_to_all x4, starting transfers between devices, over_y(): return lax.all_to_all(array, 'y', 0, 0, tiled=True)  15.7 us
    pallas_call x2, Pallas kernels, right_terms(): pl.pallas_call(lambda *refs: right_kernel(part, *refs), out_shape=[jax.Sh...  12.6 us
    pallas_call x2, Pallas kernels, product(): pl.pallas_call(lambda *refs: product_kernel(part, scale, *refs), out_shap...  10.5 us
    pallas_call x1, Pallas kernels, left_terms(): pl.pallas_call(left_kernel, out_shape=[jax.ShapeDtypeStruct((HALF, rows,...  8.36 us
    convert_element_type x10, other arithmetic, total(): sum((term.astype(jnp.float32) for term in terms)).astype(jnp.bfloat16)  8.13 us
    unnamed x26, local copies, waits for them, and re-layouts  5.15 us
  transfers between devices with their start and end apart: 24, of which 9 were waited for; matrix products, arithmetic and copies ran while one was open for 9% of the time, Pallas kernels for 13%

profile of v6, /device:TPU:1, one launch (start us, length us, event | category | flops | bytes accessed | tf_op | source)
XLA Modules:
  0.0 130.7 jit_solution(10733872024999120194)
XLA Ops:
  0.0 8.4 %left.1 = (bf16[20,256,128]{2,1,0:T(8,128)(2,1)}, bf16[20,256,128]{2,1,0:T(8,128)(2,1)}, bf16[20,256,128]{2,1,0:T(8,128)(2,1)}, bf16[20,256,128]{2,1,0:T(8,128)(2,1)}) custom-call(s32[1]{0:T(128)} %bitcast.at_ref, s32[8]{0:T(128)} %refs_1_.7, bf16[8,256,256]{2,1,0:T(8,128)(2,1)} %edge_ref.1, bf16[8,256,2048]{2,1,0:T(8,128)(2,1)} %site_ref.1), custom_call_target="tpu_custom_call" | custom-call | flops 1342177280 | bytes 12582912 | tf_op jit(solution)/shard_map/left/pallas_call | solution.py:92
  8.4 1.5 %collective-permute-start = (bf16[20,256,128]{2,1,0:T(8,128)(2,1)}, bf16[20,256,128]{2,1,0:T(8,128)(2,1)S(1)}, u32[]{:S(2)}, u32[]{:S(2)}) collective-permute-start(bf16[20,256,128]{2,1,0:T(8,128)(2,1)} %get-tuple-element.57), channel_id=1, source_target_pairs={{0,1},{1,0},{2,3},{3,2},{4,5},{5,4},{6,7},{7,6},{8,9},{9,8},{10,11... | collective-permute-start | bytes 3932168 | tf_op jit(solution)/shard_map/ppermute | solution.py:259
  10.0 6.3 %right.2 = (bf16[10,128,128]{2,1,0:T(8,128)(2,1)}, bf16[10,128,128]{2,1,0:T(8,128)(2,1)}, bf16[10,128,128]{2,1,0:T(8,128)(2,1)}, bf16[10,128,128]{2,1,0:T(8,128)(2,1)}) custom-call(s32[1]{0:T(128)} %bitcast.1.refs_0_, s32[8]{0:T(128)} %refs_1_.7, bf16[8,2048,512]{2,1,0:T(8,128)(2,1)} %refs_2_.1, bf16[8,512,128]{2,1,0:T(8,128)(2,1)} %refs_3_.1), custom_call_target="tpu_custom_call" | custom-call | flops 671088640 | bytes 10485760 | tf_op jit(solution)/shard_map/right/pallas_call | solution.py:165
  16.4 1.4 %add_convert_fusion.1 = bf16[20,256,128]{2,1,0:T(8,128)(2,1)} fusion(bf16[20,256,128]{2,1,0:T(8,128)(2,1)S(1)} %collective-permute-done, bf16[20,256,128]{2,1,0:T(8,128)(2,1)S(1)} %copy-done.10), kind=kLoop, calls=%fused_computation.1 | loop fusion | flops 2621440 | bytes 3932160 | tf_op jit(solution)/shard_map/convert_element_type | solution.py:263
  17.8 4.4 %all-to-all-start = ((bf16[20,256,128]{2,1,0:T(8,128)(2,1)}), bf16[20,256,128]{2,1,0:T(8,128)(2,1)S(1)}, u32[]{:S(2)}, u32[]{:S(2)}) async-start(bf16[20,256,128]{2,1,0:T(8,128)(2,1)} %add_convert_fusion.1), calls=%async_computation | async-start | bytes 2621440 | tf_op jit(solution)/shard_map/all_to_all | solution.py:271
  22.2 1.6 %collective-permute-start.3 = (bf16[10,128,128]{2,1,0:T(8,128)(2,1)}, bf16[10,128,128]{2,1,0:T(8,128)(2,1)}, u32[]{:S(2)}, u32[]{:S(2)}) collective-permute-start(bf16[10,128,128]{2,1,0:T(8,128)(2,1)} %get-tuple-element.82), channel_id=1, source_target_pairs={{0,32},{32,64},{64,96},{96,0},{1,33},{33,65},{65,97},{97,1},{2,34}... | collective-permute-start | bytes 983048 | tf_op jit(solution)/shard_map/ppermute | solution.py:259
  23.8 3.3 %collective-permute-start.4 = (bf16[10,128,128]{2,1,0:T(8,128)(2,1)}, bf16[10,128,128]{2,1,0:T(8,128)(2,1)}, u32[]{:S(2)}, u32[]{:S(2)}) collective-permute-start(bf16[10,128,128]{2,1,0:T(8,128)(2,1)} %get-tuple-element.83), channel_id=1, source_target_pairs={{0,64},{32,96},{64,0},{96,32},{1,65},{33,97},{65,1},{97,33},{2,66}... | collective-permute-start | bytes 983048 | tf_op jit(solution)/shard_map/ppermute | solution.py:259
  27.8 2.7 %add_convert_fusion = bf16[20,256,128]{2,1,0:T(8,128)(2,1)} fusion(bf16[20,256,128]{2,1,0:T(8,128)(2,1)} %collective-permute-done.1, bf16[20,256,128]{2,1,0:T(8,128)(2,1)S(1)} %copy-done.9), kind=kLoop, calls=%fused_computation | loop fusion | flops 2621440 | bytes 3932160 | tf_op jit(solution)/shard_map/convert_element_type | solution.py:263
  30.6 6.2 %right.3 = (bf16[10,128,128]{2,1,0:T(8,128)(2,1)}, bf16[10,128,128]{2,1,0:T(8,128)(2,1)}, bf16[10,128,128]{2,1,0:T(8,128)(2,1)}, bf16[10,128,128]{2,1,0:T(8,128)(2,1)}) custom-call(s32[1]{0:T(128)} %bitcast.1.refs_0_, s32[8]{0:T(128)} %refs_1_.7, bf16[8,2048,512]{2,1,0:T(8,128)(2,1)} %refs_2_.1, bf16[8,512,128]{2,1,0:T(8,128)(2,1)} %refs_3_.1), custom_call_target="tpu_custom_call" | custom-call | flops 671088640 | bytes 10485760 | tf_op jit(solution)/shard_map/right/pallas_call | solution.py:165
  36.8 2.8 %all-to-all-done = bf16[20,256,128]{2,1,0:T(8,128)(2,1)S(1)} async-done(((bf16[20,256,128]{2,1,0:T(8,128)(2,1)}), bf16[20,256,128]{2,1,0:T(8,128)(2,1)S(1)}, u32[]{:S(2)}, u32[]{:S(2)}) %all-to-all-start) | async-done | bytes 1310752 | tf_op jit(solution)/shard_map/all_to_all | solution.py:271
  39.8 3.7 %all-to-all-start.1 = ((bf16[20,256,128]{2,1,0:T(8,128)(2,1)}), bf16[20,256,128]{2,1,0:T(8,128)(2,1)S(1)}, u32[]{:S(2)}, u32[]{:S(2)}) async-start(bf16[20,256,128]{2,1,0:T(8,128)(2,1)} %add_convert_fusion), calls=%async_computation.1 | async-start | bytes 2621440 | tf_op jit(solution)/shard_map/all_to_all | solution.py:271
  43.5 1.4 %add_convert_fusion.7 = bf16[10,128,128]{2,1,0:T(8,128)(2,1)S(1)} fusion(bf16[10,128,128]{2,1,0:T(8,128)(2,1)} %collective-permute-done.5, bf16[10,128,128]{2,1,0:T(8,128)(2,1)} %collective-permute-done.4, bf16[10,128,128]{2,1,0:T(8,128)(2,1)} %collective-permute-done.3, bf16[10,128,128]{2,1,0:T(8,128)(2,1)S(1)} %copy-done.12), kind=kLoop, calls=%fused_computation.7 | loop fusion | flops 1310720 | bytes 1638400 | tf_op jit(solution)/shard_map/convert_element_type | solution.py:263
  46.2 2.5 %collective-permute-start.2 = (bf16[5,256,128]{2,1,0:T(8,128)(2,1)S(1)}, bf16[5,256,128]{2,1,0:T(8,128)(2,1)S(1)}, u32[]{:S(2)}, u32[]{:S(2)}) collective-permute-start(bf16[5,256,128]{2,1,0:T(8,128)(2,1)S(1)} %add_convert_fusion.9), channel_id=1, source_target_pairs={{0,2},{2,0},{1,3},{3,1},{4,6},{6,4},{5,7},{7,5},{8,10},{10,8},{9,1... | collective-permute-start | bytes 983048 | tf_op jit(solution)/shard_map/ppermute | solution.py:259
  48.6 4.1 %collective-permute-done.6 = bf16[10,128,128]{2,1,0:T(8,128)(2,1)S(1)} collective-permute-done((bf16[10,128,128]{2,1,0:T(8,128)(2,1)S(1)}, bf16[10,128,128]{2,1,0:T(8,128)(2,1)S(1)}, u32[]{:S(2)}, u32[]{:S(2)}) %collective-permute-start.6) | collective-permute-done | bytes 327712 | tf_op jit(solution)/shard_map/ppermute | solution.py:259
  52.8 1.4 %collective-permute-start.11 = (bf16[10,128,128]{2,1,0:T(8,128)(2,1)}, bf16[10,128,128]{2,1,0:T(8,128)(2,1)S(1)}, u32[]{:S(2)}, u32[]{:S(2)}) collective-permute-start(bf16[10,128,128]{2,1,0:T(8,128)(2,1)} %get-tuple-element.91), channel_id=1, source_target_pairs={{0,32},{32,64},{64,96},{96,0},{1,33},{33,65},{65,97},{97,1},{2,34}... | collective-permute-start | bytes 983048 | tf_op jit(solution)/shard_map/ppermute | solution.py:259
  54.2 3.3 %collective-permute-start.12 = (bf16[10,128,128]{2,1,0:T(8,128)(2,1)}, bf16[10,128,128]{2,1,0:T(8,128)(2,1)S(1)}, u32[]{:S(2)}, u32[]{:S(2)}) collective-permute-start(bf16[10,128,128]{2,1,0:T(8,128)(2,1)} %get-tuple-element.92), channel_id=1, source_target_pairs={{0,64},{32,96},{64,0},{96,32},{1,65},{33,97},{65,1},{97,33},{2,66}... | collective-permute-start | bytes 983048 | tf_op jit(solution)/shard_map/ppermute | solution.py:259
  58.2 3.7 %collective-permute-done.2 = bf16[5,256,128]{2,1,0:T(8,128)(2,1)S(1)} collective-permute-done((bf16[5,256,128]{2,1,0:T(8,128)(2,1)S(1)}, bf16[5,256,128]{2,1,0:T(8,128)(2,1)S(1)}, u32[]{:S(2)}, u32[]{:S(2)}) %collective-permute-start.2) | collective-permute-done | bytes 327712 | tf_op jit(solution)/shard_map/ppermute | solution.py:259
  62.2 1.4 %broadcast_in_dim.4 = bf16[4,5,256,128]{3,2,1,0:T(8,128)(2,1)} broadcast(bf16[5,256,128]{2,1,0:T(8,128)(2,1)S(1)} %add_convert_fusion.8), dimensions={1,2,3} | broadcast | bytes 1638400 | tf_op jit(solution)/shard_map/broadcast_in_dim | solution.py:291
  63.6 4.0 %all-to-all-start.2 = ((bf16[20,256,128]{2,1,0:T(8,128)(2,1)}), bf16[20,256,128]{2,1,0:T(8,128)(2,1)S(1)}, u32[]{:S(2)}, u32[]{:S(2)}) async-start(bf16[20,256,128]{2,1,0:T(8,128)(2,1)} %bitcast.4), calls=%async_computation.2 | async-start | bytes 2621440 | tf_op jit(solution)/shard_map/all_to_all | solution.py:271
  71.2 2.5 %collective-permute-start.10 = (bf16[5,256,128]{2,1,0:T(8,128)(2,1)S(1)}, bf16[5,256,128]{2,1,0:T(8,128)(2,1)S(1)}, u32[]{:S(2)}, u32[]{:S(2)}) collective-permute-start(bf16[5,256,128]{2,1,0:T(8,128)(2,1)S(1)} %add_convert_fusion.5), channel_id=1, source_target_pairs={{0,2},{2,0},{1,3},{3,1},{4,6},{6,4},{5,7},{7,5},{8,10},{10,8},{9,1... | collective-permute-start | bytes 983048 | tf_op jit(solution)/shard_map/ppermute | solution.py:259
  73.6 3.6 %collective-permute-start.9 = (bf16[10,128,128]{2,1,0:T(8,128)(2,1)S(1)}, bf16[10,128,128]{2,1,0:T(8,128)(2,1)S(1)}, u32[]{:S(2)}, u32[]{:S(2)}) collective-permute-start(bf16[10,128,128]{2,1,0:T(8,128)(2,1)S(1)} %add_convert_fusion.6.refs_4_), channel_id=1, source_target_pairs={{0,96},{32,0},{64,32},{96,64},{1,97},{33,1},{65,33},{97,65},{2,98}... | collective-permute-start | bytes 983048 | tf_op jit(solution)/shard_map/ppermute | solution.py:259
  77.2 1.7 %collective-permute-start.8 = (bf16[10,128,128]{2,1,0:T(8,128)(2,1)S(1)}, bf16[10,128,128]{2,1,0:T(8,128)(2,1)S(1)}, u32[]{:S(2)}, u32[]{:S(2)}) collective-permute-start(bf16[10,128,128]{2,1,0:T(8,128)(2,1)S(1)} %add_convert_fusion.6.refs_4_), channel_id=1, source_target_pairs={{0,64},{32,96},{64,0},{96,32},{1,65},{33,97},{65,1},{97,33},{2,66}... | collective-permute-start | bytes 983048 | tf_op jit(solution)/shard_map/ppermute | solution.py:259
  79.0 4.8 %collective-permute-done.10 = bf16[5,256,128]{2,1,0:T(8,128)(2,1)S(1)} collective-permute-done((bf16[5,256,128]{2,1,0:T(8,128)(2,1)S(1)}, bf16[5,256,128]{2,1,0:T(8,128)(2,1)S(1)}, u32[]{:S(2)}, u32[]{:S(2)}) %collective-permute-start.10) | collective-permute-done | bytes 327712 | tf_op jit(solution)/shard_map/ppermute | solution.py:259
  85.0 9.1 %collective-permute-done.7.refs_5_ = bf16[10,128,128]{2,1,0:T(8,128)(2,1)S(1)} collective-permute-done((bf16[10,128,128]{2,1,0:T(8,128)(2,1)S(1)}, bf16[10,128,128]{2,1,0:T(8,128)(2,1)S(1)}, u32[]{:S(2)}, u32[]{:S(2)}) %collective-permute-start.7) | collective-permute-done | bytes 327712 | tf_op jit(solution)/shard_map/ppermute | solution.py:259
  94.1 1.8 %collective-permute-start.18 = (bf16[20,256,128]{2,1,0:T(8,128)(2,1)S(1)}, bf16[20,256,128]{2,1,0:T(8,128)(2,1)}, u32[]{:S(2)}, u32[]{:S(2)}) collective-permute-start(bf16[20,256,128]{2,1,0:T(8,128)(2,1)S(1)} %all-to-all-done.2.refs_2_), channel_id=1, source_target_pairs={{0,1},{1,0},{2,3},{3,2},{4,5},{5,4},{6,7},{7,6},{8,9},{9,8},{10,11... | collective-permute-start | bytes 3932168 | tf_op jit(solution)/shard_map/ppermute | solution.py:259
  95.9 2.4 %broadcast_in_dim.5 = bf16[4,5,256,128]{3,2,1,0:T(8,128)(2,1)} broadcast(bf16[5,256,128]{2,1,0:T(8,128)(2,1)} %add_convert_fusion.4), dimensions={1,2,3} | broadcast | bytes 1638400 | tf_op jit(solution)/shard_map/broadcast_in_dim | solution.py:291
  98.2 3.6 %all-to-all-start.3 = ((bf16[20,256,128]{2,1,0:T(8,128)(2,1)}), bf16[20,256,128]{2,1,0:T(8,128)(2,1)S(1)}, u32[]{:S(2)}, u32[]{:S(2)}) async-start(bf16[20,256,128]{2,1,0:T(8,128)(2,1)} %bitcast.6), calls=%async_computation.3 | async-start | bytes 2621440 | tf_op jit(solution)/shard_map/all_to_all | solution.py:271
  102.2 1.7 %collective-permute-start.16 = (bf16[10,128,128]{2,1,0:T(8,128)(2,1)S(1)}, bf16[10,128,128]{2,1,0:T(8,128)(2,1)}, u32[]{:S(2)}, u32[]{:S(2)}) collective-permute-start(bf16[10,128,128]{2,1,0:T(8,128)(2,1)S(1)} %add_convert_fusion.2.refs_4_), channel_id=1, source_target_pairs={{0,64},{32,96},{64,0},{96,32},{1,65},{33,97},{65,1},{97,33},{2,66}... | collective-permute-start | bytes 983048 | tf_op jit(solution)/shard_map/ppermute | solution.py:259
  107.2 4.7 %product.1.refs_8_ = f32[8,256,128]{2,1,0:T(8,128)S(1)} custom-call(s32[4]{0:T(128)S(1)} %pad_add_fusion.refs_0_, s32[8]{0:T(128)S(1)} %copy-done.8, bf16[20,256,128]{2,1,0:T(8,128)(2,1)S(1)} %all-to-all-done.2.refs_2_, bf16[20,256,128]{2,1,0:T(8,128)(2,1)} %collective-permute-done.18.refs_3_, bf16[10,128,128]{2,1,0:T(8,128)(2,1)S(1)} %add_convert_fusion.6.refs_4_, ...), custom_call_target="tpu_custom_call" | custom-call | flops 335544320 | bytes 6291456 | tf_op jit(solution)/shard_map/product/pallas_call | solution.py:239
  112.9 7.5 %collective-permute-done.15.refs_5_ = bf16[10,128,128]{2,1,0:T(8,128)(2,1)} collective-permute-done((bf16[10,128,128]{2,1,0:T(8,128)(2,1)S(1)}, bf16[10,128,128]{2,1,0:T(8,128)(2,1)}, u32[]{:S(2)}, u32[]{:S(2)}) %collective-permute-start.15) | collective-permute-done | bytes 327712 | tf_op jit(solution)/shard_map/ppermute | solution.py:259
  120.9 2.7 %collective-permute-done.19.refs_3_ = bf16[20,256,128]{2,1,0:T(8,128)(2,1)S(1)} collective-permute-done((bf16[20,256,128]{2,1,0:T(8,128)(2,1)S(1)}, bf16[20,256,128]{2,1,0:T(8,128)(2,1)S(1)}, u32[]{:S(2)}, u32[]{:S(2)}) %collective-permute-start.19) | collective-permute-done | bytes 1310752 | tf_op jit(solution)/shard_map/ppermute | solution.py:259
  124.8 5.7 %product_end.1 = bf16[8,256,128]{2,1,0:T(8,128)(2,1)} custom-call(s32[4]{0:T(128)S(1)} %pad_add_fusion.refs_0_, s32[8]{0:T(128)S(1)} %copy-done.8, bf16[20,256,128]{2,1,0:T(8,128)(2,1)S(1)} %all-to-all-done.3.refs_2_, bf16[20,256,128]{2,1,0:T(8,128)(2,1)S(1)} %collective-permute-done.19.refs_3_, bf16[10,128,128]{2,1,0:T(8,128)(2,1)S(1)} %add_convert_fusion.2.refs_4_, ...), custom_call_target="tpu_custom_call" | custom-call | flops 335544320 | bytes 6291456 | tf_op jit(solution)/shard_map/product_end/pallas_call | solution.py:239
  (60 shorter events, 14.7 us)
Async XLA Ops:
  8.4 8.0 %collective-permute-start = (bf16[20,256,128]{2,1,0:T(8,128)(2,1)}, bf16[20,256,128]{2,1,0:T(8,128)(2,1)S(1)}, u32[]{:S(2)}, u32[]{:S(2)}) collective-permute-start(bf16[20,256,128]{2,1,0:T(8,128)(2,1)} %get-tuple-element.57), channel_id=1, source_target_pairs={{0,1},{1,0},{2,3},{3,2},{4,5},{5,4},{6,7},{7,6},{8,9},{9,8},{10,11... | collective-permute-start | bytes 3932168 | tf_op jit(solution)/shard_map/ppermute | solution.py:259
  9.9 17.9 %collective-permute-start.1 = (bf16[20,256,128]{2,1,0:T(8,128)(2,1)}, bf16[20,256,128]{2,1,0:T(8,128)(2,1)}, u32[]{:S(2)}, u32[]{:S(2)}) collective-permute-start(bf16[20,256,128]{2,1,0:T(8,128)(2,1)} %get-tuple-element.76), channel_id=1, source_target_pairs={{0,1},{1,0},{2,3},{3,2},{4,5},{5,4},{6,7},{7,6},{8,9},{9,8},{10,11... | collective-permute-start | bytes 3932168 | tf_op jit(solution)/shard_map/ppermute | solution.py:259
  10.0 6.4 %copy-start.10 = (bf16[20,256,128]{2,1,0:T(8,128)(2,1)S(1)}, bf16[20,256,128]{2,1,0:T(8,128)(2,1)}, u32[]{:S(2)}) copy-start(bf16[20,256,128]{2,1,0:T(8,128)(2,1)} %get-tuple-element.56) | copy-start | bytes 3932164
  17.8 10.0 %copy-start.9 = (bf16[20,256,128]{2,1,0:T(8,128)(2,1)S(1)}, bf16[20,256,128]{2,1,0:T(8,128)(2,1)}, u32[]{:S(2)}) copy-start(bf16[20,256,128]{2,1,0:T(8,128)(2,1)} %get-tuple-element.75) | copy-start | bytes 3932164
  17.8 21.8 %all-to-all-start = ((bf16[20,256,128]{2,1,0:T(8,128)(2,1)}), bf16[20,256,128]{2,1,0:T(8,128)(2,1)S(1)}, u32[]{:S(2)}, u32[]{:S(2)}) async-start(bf16[20,256,128]{2,1,0:T(8,128)(2,1)} %add_convert_fusion.1), calls=%async_computation | async-start | bytes 2621440 | tf_op jit(solution)/shard_map/all_to_all | solution.py:271
  22.2 21.3 %collective-permute-start.3 = (bf16[10,128,128]{2,1,0:T(8,128)(2,1)}, bf16[10,128,128]{2,1,0:T(8,128)(2,1)}, u32[]{:S(2)}, u32[]{:S(2)}) collective-permute-start(bf16[10,128,128]{2,1,0:T(8,128)(2,1)} %get-tuple-element.82), channel_id=1, source_target_pairs={{0,32},{32,64},{64,96},{96,0},{1,33},{33,65},{65,97},{97,1},{2,34}... | collective-permute-start | bytes 983048 | tf_op jit(solution)/shard_map/ppermute | solution.py:259
  23.8 19.7 %collective-permute-start.4 = (bf16[10,128,128]{2,1,0:T(8,128)(2,1)}, bf16[10,128,128]{2,1,0:T(8,128)(2,1)}, u32[]{:S(2)}, u32[]{:S(2)}) collective-permute-start(bf16[10,128,128]{2,1,0:T(8,128)(2,1)} %get-tuple-element.83), channel_id=1, source_target_pairs={{0,64},{32,96},{64,0},{96,32},{1,65},{33,97},{65,1},{97,33},{2,66}... | collective-permute-start | bytes 983048 | tf_op jit(solution)/shard_map/ppermute | solution.py:259
  27.1 16.4 %collective-permute-start.5 = (bf16[10,128,128]{2,1,0:T(8,128)(2,1)}, bf16[10,128,128]{2,1,0:T(8,128)(2,1)}, u32[]{:S(2)}, u32[]{:S(2)}) collective-permute-start(bf16[10,128,128]{2,1,0:T(8,128)(2,1)} %get-tuple-element.84), channel_id=1, source_target_pairs={{0,96},{32,0},{64,32},{96,64},{1,97},{33,1},{65,33},{97,65},{2,98}... | collective-permute-start | bytes 983048 | tf_op jit(solution)/shard_map/ppermute | solution.py:259
  39.8 3.7 %copy-start.12 = (bf16[10,128,128]{2,1,0:T(8,128)(2,1)S(1)}, bf16[10,128,128]{2,1,0:T(8,128)(2,1)}, u32[]{:S(2)}) copy-start(bf16[10,128,128]{2,1,0:T(8,128)(2,1)} %get-tuple-element.81) | copy-start | bytes 983044
  39.8 22.2 %all-to-all-start.1 = ((bf16[20,256,128]{2,1,0:T(8,128)(2,1)}), bf16[20,256,128]{2,1,0:T(8,128)(2,1)S(1)}, u32[]{:S(2)}, u32[]{:S(2)}) async-start(bf16[20,256,128]{2,1,0:T(8,128)(2,1)} %add_convert_fusion), calls=%async_computation.1 | async-start | bytes 2621440 | tf_op jit(solution)/shard_map/all_to_all | solution.py:271
  44.9 7.8 %collective-permute-start.6 = (bf16[10,128,128]{2,1,0:T(8,128)(2,1)S(1)}, bf16[10,128,128]{2,1,0:T(8,128)(2,1)S(1)}, u32[]{:S(2)}, u32[]{:S(2)}) collective-permute-start(bf16[10,128,128]{2,1,0:T(8,128)(2,1)S(1)} %add_convert_fusion.7), channel_id=1, source_target_pairs={{0,16},{16,0},{1,17},{17,1},{2,18},{18,2},{3,19},{19,3},{4,20},{20... | collective-permute-start | bytes 983048 | tf_op jit(solution)/shard_map/ppermute | solution.py:259
  46.2 15.7 %collective-permute-start.2 = (bf16[5,256,128]{2,1,0:T(8,128)(2,1)S(1)}, bf16[5,256,128]{2,1,0:T(8,128)(2,1)S(1)}, u32[]{:S(2)}, u32[]{:S(2)}) collective-permute-start(bf16[5,256,128]{2,1,0:T(8,128)(2,1)S(1)} %add_convert_fusion.9), channel_id=1, source_target_pairs={{0,2},{2,0},{1,3},{3,1},{4,6},{6,4},{5,7},{7,5},{8,10},{10,8},{9,1... | collective-permute-start | bytes 983048 | tf_op jit(solution)/shard_map/ppermute | solution.py:259
  52.8 14.8 %collective-permute-start.11 = (bf16[10,128,128]{2,1,0:T(8,128)(2,1)}, bf16[10,128,128]{2,1,0:T(8,128)(2,1)S(1)}, u32[]{:S(2)}, u32[]{:S(2)}) collective-permute-start(bf16[10,128,128]{2,1,0:T(8,128)(2,1)} %get-tuple-element.91), channel_id=1, source_target_pairs={{0,32},{32,64},{64,96},{96,0},{1,33},{33,65},{65,97},{97,1},{2,34}... | collective-permute-start | bytes 983048 | tf_op jit(solution)/shard_map/ppermute | solution.py:259
  54.2 13.4 %collective-permute-start.12 = (bf16[10,128,128]{2,1,0:T(8,128)(2,1)}, bf16[10,128,128]{2,1,0:T(8,128)(2,1)S(1)}, u32[]{:S(2)}, u32[]{:S(2)}) collective-permute-start(bf16[10,128,128]{2,1,0:T(8,128)(2,1)} %get-tuple-element.92), channel_id=1, source_target_pairs={{0,64},{32,96},{64,0},{96,32},{1,65},{33,97},{65,1},{97,33},{2,66}... | collective-permute-start | bytes 983048 | tf_op jit(solution)/shard_map/ppermute | solution.py:259
  57.5 11.2 %collective-permute-start.13 = (bf16[10,128,128]{2,1,0:T(8,128)(2,1)}, bf16[10,128,128]{2,1,0:T(8,128)(2,1)}, u32[]{:S(2)}, u32[]{:S(2)}) collective-permute-start(bf16[10,128,128]{2,1,0:T(8,128)(2,1)} %get-tuple-element.93), channel_id=1, source_target_pairs={{0,96},{32,0},{64,32},{96,64},{1,97},{33,1},{65,33},{97,65},{2,98}... | collective-permute-start | bytes 983048 | tf_op jit(solution)/shard_map/ppermute | solution.py:259
  63.6 5.2 %copy-start.11 = (bf16[10,128,128]{2,1,0:T(8,128)(2,1)S(1)}, bf16[10,128,128]{2,1,0:T(8,128)(2,1)}, u32[]{:S(2)}) copy-start(bf16[10,128,128]{2,1,0:T(8,128)(2,1)} %get-tuple-element.90) | copy-start | bytes 983044
  63.6 30.5 %all-to-all-start.2 = ((bf16[20,256,128]{2,1,0:T(8,128)(2,1)}), bf16[20,256,128]{2,1,0:T(8,128)(2,1)S(1)}, u32[]{:S(2)}, u32[]{:S(2)}) async-start(bf16[20,256,128]{2,1,0:T(8,128)(2,1)} %bitcast.4), calls=%async_computation.2 | async-start | bytes 2621440 | tf_op jit(solution)/shard_map/all_to_all | solution.py:271
  69.9 8.9 %collective-permute-start.14 = (bf16[10,128,128]{2,1,0:T(8,128)(2,1)S(1)}, bf16[10,128,128]{2,1,0:T(8,128)(2,1)S(1)}, u32[]{:S(2)}, u32[]{:S(2)}) collective-permute-start(bf16[10,128,128]{2,1,0:T(8,128)(2,1)S(1)} %add_convert_fusion.3), channel_id=1, source_target_pairs={{0,16},{16,0},{1,17},{17,1},{2,18},{18,2},{3,19},{19,3},{4,20},{20... | collective-permute-start | bytes 983048 | tf_op jit(solution)/shard_map/ppermute | solution.py:259
  71.2 12.6 %collective-permute-start.10 = (bf16[5,256,128]{2,1,0:T(8,128)(2,1)S(1)}, bf16[5,256,128]{2,1,0:T(8,128)(2,1)S(1)}, u32[]{:S(2)}, u32[]{:S(2)}) collective-permute-start(bf16[5,256,128]{2,1,0:T(8,128)(2,1)S(1)} %add_convert_fusion.5), channel_id=1, source_target_pairs={{0,2},{2,0},{1,3},{3,1},{4,6},{6,4},{5,7},{7,5},{8,10},{10,8},{9,1... | collective-permute-start | bytes 983048 | tf_op jit(solution)/shard_map/ppermute | solution.py:259
  73.6 10.9 %collective-permute-start.9 = (bf16[10,128,128]{2,1,0:T(8,128)(2,1)S(1)}, bf16[10,128,128]{2,1,0:T(8,128)(2,1)S(1)}, u32[]{:S(2)}, u32[]{:S(2)}) collective-permute-start(bf16[10,128,128]{2,1,0:T(8,128)(2,1)S(1)} %add_convert_fusion.6.refs_4_), channel_id=1, source_target_pairs={{0,96},{32,0},{64,32},{96,64},{1,97},{33,1},{65,33},{97,65},{2,98}... | collective-permute-start | bytes 983048 | tf_op jit(solution)/shard_map/ppermute | solution.py:259
  77.2 7.8 %collective-permute-start.8 = (bf16[10,128,128]{2,1,0:T(8,128)(2,1)S(1)}, bf16[10,128,128]{2,1,0:T(8,128)(2,1)S(1)}, u32[]{:S(2)}, u32[]{:S(2)}) collective-permute-start(bf16[10,128,128]{2,1,0:T(8,128)(2,1)S(1)} %add_convert_fusion.6.refs_4_), channel_id=1, source_target_pairs={{0,64},{32,96},{64,0},{96,32},{1,65},{33,97},{65,1},{97,33},{2,66}... | collective-permute-start | bytes 983048 | tf_op jit(solution)/shard_map/ppermute | solution.py:259
  78.9 15.2 %collective-permute-start.7 = (bf16[10,128,128]{2,1,0:T(8,128)(2,1)S(1)}, bf16[10,128,128]{2,1,0:T(8,128)(2,1)S(1)}, u32[]{:S(2)}, u32[]{:S(2)}) collective-permute-start(bf16[10,128,128]{2,1,0:T(8,128)(2,1)S(1)} %add_convert_fusion.6.refs_4_), channel_id=1, source_target_pairs={{0,32},{32,64},{64,96},{96,0},{1,33},{33,65},{65,97},{97,1},{2,34}... | collective-permute-start | bytes 983048 | tf_op jit(solution)/shard_map/ppermute | solution.py:259
  84.6 13.7 %copy-start.2 = (bf16[10,128,128]{2,1,0:T(8,128)(2,1)}, bf16[10,128,128]{2,1,0:T(8,128)(2,1)S(1)}, u32[]{:S(2)}) copy-start(bf16[10,128,128]{2,1,0:T(8,128)(2,1)S(1)} %collective-permute-done.9.refs_7_) | copy-start | bytes 983044
  85.0 13.3 %copy-start.4 = (bf16[10,128,128]{2,1,0:T(8,128)(2,1)}, bf16[10,128,128]{2,1,0:T(8,128)(2,1)S(1)}, u32[]{:S(2)}) copy-start(bf16[10,128,128]{2,1,0:T(8,128)(2,1)S(1)} %collective-permute-done.8.refs_6_) | copy-start | bytes 983044
  94.1 4.2 %copy-start.6 = (bf16[10,128,128]{2,1,0:T(8,128)(2,1)}, bf16[10,128,128]{2,1,0:T(8,128)(2,1)S(1)}, u32[]{:S(2)}) copy-start(bf16[10,128,128]{2,1,0:T(8,128)(2,1)S(1)} %collective-permute-done.7.refs_5_) | copy-start | bytes 983044
  94.1 10.2 %collective-permute-start.18 = (bf16[20,256,128]{2,1,0:T(8,128)(2,1)S(1)}, bf16[20,256,128]{2,1,0:T(8,128)(2,1)}, u32[]{:S(2)}, u32[]{:S(2)}) collective-permute-start(bf16[20,256,128]{2,1,0:T(8,128)(2,1)S(1)} %all-to-all-done.2.refs_2_), channel_id=1, source_target_pairs={{0,1},{1,0},{2,3},{3,2},{4,5},{5,4},{6,7},{7,6},{8,9},{9,8},{10,11... | collective-permute-start | bytes 3932168 | tf_op jit(solution)/shard_map/ppermute | solution.py:259
  98.2 6.1 %copy-start.8 = (s32[8]{0:T(128)S(1)}, s32[8]{0:T(128)}, u32[]{:S(2)}) copy-start(s32[8]{0:T(128)} %refs_1_.7) | copy-start | bytes 100
  98.2 22.2 %all-to-all-start.3 = ((bf16[20,256,128]{2,1,0:T(8,128)(2,1)}), bf16[20,256,128]{2,1,0:T(8,128)(2,1)S(1)}, u32[]{:S(2)}, u32[]{:S(2)}) async-start(bf16[20,256,128]{2,1,0:T(8,128)(2,1)} %bitcast.6), calls=%async_computation.3 | async-start | bytes 2621440 | tf_op jit(solution)/shard_map/all_to_all | solution.py:271
  101.8 11.1 %collective-permute-start.17 = (bf16[10,128,128]{2,1,0:T(8,128)(2,1)S(1)}, bf16[10,128,128]{2,1,0:T(8,128)(2,1)}, u32[]{:S(2)}, u32[]{:S(2)}) collective-permute-start(bf16[10,128,128]{2,1,0:T(8,128)(2,1)S(1)} %add_convert_fusion.2.refs_4_), channel_id=1, source_target_pairs={{0,96},{32,0},{64,32},{96,64},{1,97},{33,1},{65,33},{97,65},{2,98}... | collective-permute-start | bytes 983048 | tf_op jit(solution)/shard_map/ppermute | solution.py:259
  102.2 10.7 %collective-permute-start.16 = (bf16[10,128,128]{2,1,0:T(8,128)(2,1)S(1)}, bf16[10,128,128]{2,1,0:T(8,128)(2,1)}, u32[]{:S(2)}, u32[]{:S(2)}) collective-permute-start(bf16[10,128,128]{2,1,0:T(8,128)(2,1)S(1)} %add_convert_fusion.2.refs_4_), channel_id=1, source_target_pairs={{0,64},{32,96},{64,0},{96,32},{1,65},{33,97},{65,1},{97,33},{2,66}... | collective-permute-start | bytes 983048 | tf_op jit(solution)/shard_map/ppermute | solution.py:259
  103.8 16.6 %collective-permute-start.15 = (bf16[10,128,128]{2,1,0:T(8,128)(2,1)S(1)}, bf16[10,128,128]{2,1,0:T(8,128)(2,1)}, u32[]{:S(2)}, u32[]{:S(2)}) collective-permute-start(bf16[10,128,128]{2,1,0:T(8,128)(2,1)S(1)} %add_convert_fusion.2.refs_4_), channel_id=1, source_target_pairs={{0,32},{32,64},{64,96},{96,0},{1,33},{33,65},{65,97},{97,1},{2,34}... | collective-permute-start | bytes 983048 | tf_op jit(solution)/shard_map/ppermute | solution.py:259
  120.5 3.2 %collective-permute-start.19 = (bf16[20,256,128]{2,1,0:T(8,128)(2,1)S(1)}, bf16[20,256,128]{2,1,0:T(8,128)(2,1)S(1)}, u32[]{:S(2)}, u32[]{:S(2)}) collective-permute-start(bf16[20,256,128]{2,1,0:T(8,128)(2,1)S(1)} %all-to-all-done.3.refs_2_), channel_id=1, source_target_pairs={{0,1},{1,0},{2,3},{3,2},{4,5},{5,4},{6,7},{7,6},{8,9},{9,8},{10,11... | collective-permute-start | bytes 3932168 | tf_op jit(solution)/shard_map/ppermute | solution.py:259
  (5 other events, 5.1 us)

commit v7 on v6

--- a/solution.py
+++ b/solution.py
@@ -319,11 +319,12 @@
     half_a = over_y(copies_a)
     one_x, two_x = swap(one_b, "xh"), swap(two_b, "xl")
     one_b, two_b = total(one_b, one_x), total(two_b, two_x)
-    half_a, rights_a, one_b, two_b = fence((half_a, rights_a, one_b, two_b))
+    copies_b = left_copies(one_b)
+    half_a, rights_a, copies_b, two_b = fence((half_a, rights_a, copies_b, two_b))
 
     rights_b = [two_b] + over_z([two_b] * Z)
     at = jnp.stack([core, z, row_first, col_first]).astype(jnp.int32)
-    half_b = over_y(left_copies(one_b))
+    half_b = over_y(copies_b)
     product_a = product(A, None, at, sizes, half_a, swap(half_a, "core"), rights_a)
     half_b, rights_b, product_a = fence((half_b, rights_b, product_a))
     return product(B, order ** (-0.5), at, sizes, half_b, swap(half_b, "core"), rights_b, product_a)

time: 132 us -> 132 us (level)
  transfers between devices with their start and end apart: 24 -> 24, of which waited for: 9 -> 9; matrix products, arithmetic and copies ran while one was open for 9% -> 7% of each run, Pallas kernels for 13% -> 13%
where the time goes in v7:
time: 132 us; the launch traced here: 131 us
  starting transfers between devices  45.7 us (35%)
  waiting for transfers between devices  36.1 us (27%)
  Pallas kernels  31.5 us (24%)
  local copies, waits for them, and re-layouts  9 us (7%)
  other arithmetic  8.2 us (6%)
    ppermute x20, waiting for transfers between devices, shift(): lax.ppermute(array, axis, [(i, (i + step) % size) for i in range(size)])  33.4 us
    ppermute x20, starting transfers between devices, shift(): lax.ppermute(array, axis, [(i, (i + step) % size) for i in range(size)])  30 us
    all_to_all x4, starting transfers between devices, over_y(): return lax.all_to_all(array, 'y', 0, 0, tiled=True)  15.7 us
    pallas_call x2, Pallas kernels, right_terms(): pl.pallas_call(lambda *refs: right_kernel(part, *refs), out_shape=[jax.Sh...  12.7 us
    pallas_call x2, Pallas kernels, product(): pl.pallas_call(lambda *refs: product_kernel(part, scale, *refs), out_shap...  10.5 us
    pallas_call x1, Pallas kernels, left_terms(): pl.pallas_call(left_kernel, out_shape=[jax.ShapeDtypeStruct((HALF, rows,...  8.36 us
    convert_element_type x10, other arithmetic, total(): sum((term.astype(jnp.float32) for term in terms)).astype(jnp.bfloat16)  8.13 us
    unnamed x26, local copies, waits for them, and re-layouts  5.15 us
  transfers between devices with their start and end apart: 24, of which 9 were waited for; matrix products, arithmetic and copies ran while one was open for 7% of the time, Pallas kernels for 13%

profile of v7, /device:TPU:1, one launch (start us, length us, event | category | flops | bytes accessed | tf_op | source)
XLA Modules:
  0.0 130.9 jit_solution(6096234500286482788)
XLA Ops:
  0.0 8.4 %left.1 = (bf16[20,256,128]{2,1,0:T(8,128)(2,1)}, bf16[20,256,128]{2,1,0:T(8,128)(2,1)}, bf16[20,256,128]{2,1,0:T(8,128)(2,1)}, bf16[20,256,128]{2,1,0:T(8,128)(2,1)}) custom-call(s32[1]{0:T(128)} %bitcast.at_ref, s32[8]{0:T(128)} %refs_1_.7, bf16[8,256,256]{2,1,0:T(8,128)(2,1)} %edge_ref.1, bf16[8,256,2048]{2,1,0:T(8,128)(2,1)} %site_ref.1), custom_call_target="tpu_custom_call" | custom-call | flops 1342177280 | bytes 12582912 | tf_op jit(solution)/shard_map/left/pallas_call | solution.py:92
  8.4 1.5 %collective-permute-start = (bf16[20,256,128]{2,1,0:T(8,128)(2,1)}, bf16[20,256,128]{2,1,0:T(8,128)(2,1)S(1)}, u32[]{:S(2)}, u32[]{:S(2)}) collective-permute-start(bf16[20,256,128]{2,1,0:T(8,128)(2,1)} %get-tuple-element.57), channel_id=1, source_target_pairs={{0,1},{1,0},{2,3},{3,2},{4,5},{5,4},{6,7},{7,6},{8,9},{9,8},{10,11... | collective-permute-start | bytes 3932168 | tf_op jit(solution)/shard_map/ppermute | solution.py:259
  10.0 6.4 %right.2 = (bf16[10,128,128]{2,1,0:T(8,128)(2,1)}, bf16[10,128,128]{2,1,0:T(8,128)(2,1)}, bf16[10,128,128]{2,1,0:T(8,128)(2,1)}, bf16[10,128,128]{2,1,0:T(8,128)(2,1)}) custom-call(s32[1]{0:T(128)} %bitcast.1.refs_0_, s32[8]{0:T(128)} %refs_1_.7, bf16[8,2048,512]{2,1,0:T(8,128)(2,1)} %refs_2_.1, bf16[8,512,128]{2,1,0:T(8,128)(2,1)} %refs_3_.1), custom_call_target="tpu_custom_call" | custom-call | flops 671088640 | bytes 10485760 | tf_op jit(solution)/shard_map/right/pallas_call | solution.py:165
  16.4 1.4 %add_convert_fusion.1 = bf16[20,256,128]{2,1,0:T(8,128)(2,1)} fusion(bf16[20,256,128]{2,1,0:T(8,128)(2,1)S(1)} %collective-permute-done, bf16[20,256,128]{2,1,0:T(8,128)(2,1)S(1)} %copy-done.10), kind=kLoop, calls=%fused_computation.1 | loop fusion | flops 2621440 | bytes 3932160 | tf_op jit(solution)/shard_map/convert_element_type | solution.py:263
  17.8 4.4 %all-to-all-start = ((bf16[20,256,128]{2,1,0:T(8,128)(2,1)}), bf16[20,256,128]{2,1,0:T(8,128)(2,1)S(1)}, u32[]{:S(2)}, u32[]{:S(2)}) async-start(bf16[20,256,128]{2,1,0:T(8,128)(2,1)} %add_convert_fusion.1), calls=%async_computation | async-start | bytes 2621440 | tf_op jit(solution)/shard_map/all_to_all | solution.py:271
  22.2 1.6 %collective-permute-start.3 = (bf16[10,128,128]{2,1,0:T(8,128)(2,1)}, bf16[10,128,128]{2,1,0:T(8,128)(2,1)}, u32[]{:S(2)}, u32[]{:S(2)}) collective-permute-start(bf16[10,128,128]{2,1,0:T(8,128)(2,1)} %get-tuple-element.82), channel_id=1, source_target_pairs={{0,32},{32,64},{64,96},{96,0},{1,33},{33,65},{65,97},{97,1},{2,34}... | collective-permute-start | bytes 983048 | tf_op jit(solution)/shard_map/ppermute | solution.py:259
  23.8 3.3 %collective-permute-start.4 = (bf16[10,128,128]{2,1,0:T(8,128)(2,1)}, bf16[10,128,128]{2,1,0:T(8,128)(2,1)}, u32[]{:S(2)}, u32[]{:S(2)}) collective-permute-start(bf16[10,128,128]{2,1,0:T(8,128)(2,1)} %get-tuple-element.83), channel_id=1, source_target_pairs={{0,64},{32,96},{64,0},{96,32},{1,65},{33,97},{65,1},{97,33},{2,66}... | collective-permute-start | bytes 983048 | tf_op jit(solution)/shard_map/ppermute | solution.py:259
  27.8 2.7 %add_convert_fusion = bf16[20,256,128]{2,1,0:T(8,128)(2,1)} fusion(bf16[20,256,128]{2,1,0:T(8,128)(2,1)} %collective-permute-done.1, bf16[20,256,128]{2,1,0:T(8,128)(2,1)S(1)} %copy-done.9), kind=kLoop, calls=%fused_computation | loop fusion | flops 2621440 | bytes 3932160 | tf_op jit(solution)/shard_map/convert_element_type | solution.py:263
  30.6 6.3 %right.3 = (bf16[10,128,128]{2,1,0:T(8,128)(2,1)}, bf16[10,128,128]{2,1,0:T(8,128)(2,1)}, bf16[10,128,128]{2,1,0:T(8,128)(2,1)}, bf16[10,128,128]{2,1,0:T(8,128)(2,1)}) custom-call(s32[1]{0:T(128)} %bitcast.1.refs_0_, s32[8]{0:T(128)} %refs_1_.7, bf16[8,2048,512]{2,1,0:T(8,128)(2,1)} %refs_2_.1, bf16[8,512,128]{2,1,0:T(8,128)(2,1)} %refs_3_.1), custom_call_target="tpu_custom_call" | custom-call | flops 671088640 | bytes 10485760 | tf_op jit(solution)/shard_map/right/pallas_call | solution.py:165
  36.9 2.7 %all-to-all-done = bf16[20,256,128]{2,1,0:T(8,128)(2,1)S(1)} async-done(((bf16[20,256,128]{2,1,0:T(8,128)(2,1)}), bf16[20,256,128]{2,1,0:T(8,128)(2,1)S(1)}, u32[]{:S(2)}, u32[]{:S(2)}) %all-to-all-start) | async-done | bytes 1310752 | tf_op jit(solution)/shard_map/all_to_all | solution.py:271
  39.8 3.7 %all-to-all-start.1 = ((bf16[20,256,128]{2,1,0:T(8,128)(2,1)}), bf16[20,256,128]{2,1,0:T(8,128)(2,1)S(1)}, u32[]{:S(2)}, u32[]{:S(2)}) async-start(bf16[20,256,128]{2,1,0:T(8,128)(2,1)} %add_convert_fusion), calls=%async_computation.1 | async-start | bytes 2621440 | tf_op jit(solution)/shard_map/all_to_all | solution.py:271
  43.5 1.4 %add_convert_fusion.7 = bf16[10,128,128]{2,1,0:T(8,128)(2,1)S(1)} fusion(bf16[10,128,128]{2,1,0:T(8,128)(2,1)} %collective-permute-done.5, bf16[10,128,128]{2,1,0:T(8,128)(2,1)} %collective-permute-done.4, bf16[10,128,128]{2,1,0:T(8,128)(2,1)} %collective-permute-done.3, bf16[10,128,128]{2,1,0:T(8,128)(2,1)S(1)} %copy-done.12), kind=kLoop, calls=%fused_computation.7 | loop fusion | flops 1310720 | bytes 1638400 | tf_op jit(solution)/shard_map/convert_element_type | solution.py:263
  46.1 2.5 %collective-permute-start.2 = (bf16[5,256,128]{2,1,0:T(8,128)(2,1)S(1)}, bf16[5,256,128]{2,1,0:T(8,128)(2,1)S(1)}, u32[]{:S(2)}, u32[]{:S(2)}) collective-permute-start(bf16[5,256,128]{2,1,0:T(8,128)(2,1)S(1)} %add_convert_fusion.9), channel_id=1, source_target_pairs={{0,2},{2,0},{1,3},{3,1},{4,6},{6,4},{5,7},{7,5},{8,10},{10,8},{9,1... | collective-permute-start | bytes 983048 | tf_op jit(solution)/shard_map/ppermute | solution.py:259
  48.6 4.1 %collective-permute-done.6 = bf16[10,128,128]{2,1,0:T(8,128)(2,1)S(1)} collective-permute-done((bf16[10,128,128]{2,1,0:T(8,128)(2,1)S(1)}, bf16[10,128,128]{2,1,0:T(8,128)(2,1)S(1)}, u32[]{:S(2)}, u32[]{:S(2)}) %collective-permute-start.6) | collective-permute-done | bytes 327712 | tf_op jit(solution)/shard_map/ppermute | solution.py:259
  52.8 1.4 %collective-permute-start.11 = (bf16[10,128,128]{2,1,0:T(8,128)(2,1)}, bf16[10,128,128]{2,1,0:T(8,128)(2,1)S(1)}, u32[]{:S(2)}, u32[]{:S(2)}) collective-permute-start(bf16[10,128,128]{2,1,0:T(8,128)(2,1)} %get-tuple-element.91), channel_id=1, source_target_pairs={{0,32},{32,64},{64,96},{96,0},{1,33},{33,65},{65,97},{97,1},{2,34}... | collective-permute-start | bytes 983048 | tf_op jit(solution)/shard_map/ppermute | solution.py:259
  54.2 3.3 %collective-permute-start.12 = (bf16[10,128,128]{2,1,0:T(8,128)(2,1)}, bf16[10,128,128]{2,1,0:T(8,128)(2,1)S(1)}, u32[]{:S(2)}, u32[]{:S(2)}) collective-permute-start(bf16[10,128,128]{2,1,0:T(8,128)(2,1)} %get-tuple-element.92), channel_id=1, source_target_pairs={{0,64},{32,96},{64,0},{96,32},{1,65},{33,97},{65,1},{97,33},{2,66}... | collective-permute-start | bytes 983048 | tf_op jit(solution)/shard_map/ppermute | solution.py:259
  58.2 3.7 %collective-permute-done.2 = bf16[5,256,128]{2,1,0:T(8,128)(2,1)S(1)} collective-permute-done((bf16[5,256,128]{2,1,0:T(8,128)(2,1)S(1)}, bf16[5,256,128]{2,1,0:T(8,128)(2,1)S(1)}, u32[]{:S(2)}, u32[]{:S(2)}) %collective-permute-start.2) | collective-permute-done | bytes 327712 | tf_op jit(solution)/shard_map/ppermute | solution.py:259
  62.2 1.4 %broadcast_in_dim.4 = bf16[4,5,256,128]{3,2,1,0:T(8,128)(2,1)} broadcast(bf16[5,256,128]{2,1,0:T(8,128)(2,1)S(1)} %add_convert_fusion.8), dimensions={1,2,3} | broadcast | bytes 1638400 | tf_op jit(solution)/shard_map/broadcast_in_dim | solution.py:291
  63.6 4.0 %all-to-all-start.2 = ((bf16[20,256,128]{2,1,0:T(8,128)(2,1)}), bf16[20,256,128]{2,1,0:T(8,128)(2,1)S(1)}, u32[]{:S(2)}, u32[]{:S(2)}) async-start(bf16[20,256,128]{2,1,0:T(8,128)(2,1)} %bitcast.4), calls=%async_computation.2 | async-start | bytes 2621440 | tf_op jit(solution)/shard_map/all_to_all | solution.py:271
  71.2 2.5 %collective-permute-start.10 = (bf16[5,256,128]{2,1,0:T(8,128)(2,1)S(1)}, bf16[5,256,128]{2,1,0:T(8,128)(2,1)S(1)}, u32[]{:S(2)}, u32[]{:S(2)}) collective-permute-start(bf16[5,256,128]{2,1,0:T(8,128)(2,1)S(1)} %add_convert_fusion.5), channel_id=1, source_target_pairs={{0,2},{2,0},{1,3},{3,1},{4,6},{6,4},{5,7},{7,5},{8,10},{10,8},{9,1... | collective-permute-start | bytes 983048 | tf_op jit(solution)/shard_map/ppermute | solution.py:259
  73.7 3.6 %collective-permute-start.9 = (bf16[10,128,128]{2,1,0:T(8,128)(2,1)S(1)}, bf16[10,128,128]{2,1,0:T(8,128)(2,1)S(1)}, u32[]{:S(2)}, u32[]{:S(2)}) collective-permute-start(bf16[10,128,128]{2,1,0:T(8,128)(2,1)S(1)} %add_convert_fusion.6.refs_4_), channel_id=1, source_target_pairs={{0,96},{32,0},{64,32},{96,64},{1,97},{33,1},{65,33},{97,65},{2,98}... | collective-permute-start | bytes 983048 | tf_op jit(solution)/shard_map/ppermute | solution.py:259
  77.2 1.6 %collective-permute-start.8 = (bf16[10,128,128]{2,1,0:T(8,128)(2,1)S(1)}, bf16[10,128,128]{2,1,0:T(8,128)(2,1)S(1)}, u32[]{:S(2)}, u32[]{:S(2)}) collective-permute-start(bf16[10,128,128]{2,1,0:T(8,128)(2,1)S(1)} %add_convert_fusion.6.refs_4_), channel_id=1, source_target_pairs={{0,64},{32,96},{64,0},{96,32},{1,65},{33,97},{65,1},{97,33},{2,66}... | collective-permute-start | bytes 983048 | tf_op jit(solution)/shard_map/ppermute | solution.py:259
  79.0 4.8 %collective-permute-done.10 = bf16[5,256,128]{2,1,0:T(8,128)(2,1)S(1)} collective-permute-done((bf16[5,256,128]{2,1,0:T(8,128)(2,1)S(1)}, bf16[5,256,128]{2,1,0:T(8,128)(2,1)S(1)}, u32[]{:S(2)}, u32[]{:S(2)}) %collective-permute-start.10) | collective-permute-done | bytes 327712 | tf_op jit(solution)/shard_map/ppermute | solution.py:259
  85.0 9.1 %collective-permute-done.7.refs_5_ = bf16[10,128,128]{2,1,0:T(8,128)(2,1)S(1)} collective-permute-done((bf16[10,128,128]{2,1,0:T(8,128)(2,1)S(1)}, bf16[10,128,128]{2,1,0:T(8,128)(2,1)S(1)}, u32[]{:S(2)}, u32[]{:S(2)}) %collective-permute-start.7) | collective-permute-done | bytes 327712 | tf_op jit(solution)/shard_map/ppermute | solution.py:259
  94.1 2.5 %broadcast_in_dim.5 = bf16[4,5,256,128]{3,2,1,0:T(8,128)(2,1)} broadcast(bf16[5,256,128]{2,1,0:T(8,128)(2,1)} %add_convert_fusion.4), dimensions={1,2,3} | broadcast | bytes 1638400 | tf_op jit(solution)/shard_map/broadcast_in_dim | solution.py:291
  96.6 1.8 %collective-permute-start.18 = (bf16[20,256,128]{2,1,0:T(8,128)(2,1)S(1)}, bf16[20,256,128]{2,1,0:T(8,128)(2,1)}, u32[]{:S(2)}, u32[]{:S(2)}) collective-permute-start(bf16[20,256,128]{2,1,0:T(8,128)(2,1)S(1)} %all-to-all-done.2.refs_2_), channel_id=1, source_target_pairs={{0,1},{1,0},{2,3},{3,2},{4,5},{5,4},{6,7},{7,6},{8,9},{9,8},{10,11... | collective-permute-start | bytes 3932168 | tf_op jit(solution)/shard_map/ppermute | solution.py:259
  98.4 3.5 %all-to-all-start.3 = ((bf16[20,256,128]{2,1,0:T(8,128)(2,1)}), bf16[20,256,128]{2,1,0:T(8,128)(2,1)S(1)}, u32[]{:S(2)}, u32[]{:S(2)}) async-start(bf16[20,256,128]{2,1,0:T(8,128)(2,1)} %bitcast.6), calls=%async_computation.3 | async-start | bytes 2621440 | tf_op jit(solution)/shard_map/all_to_all | solution.py:271
  102.4 1.6 %collective-permute-start.16 = (bf16[10,128,128]{2,1,0:T(8,128)(2,1)S(1)}, bf16[10,128,128]{2,1,0:T(8,128)(2,1)}, u32[]{:S(2)}, u32[]{:S(2)}) collective-permute-start(bf16[10,128,128]{2,1,0:T(8,128)(2,1)S(1)} %add_convert_fusion.2.refs_4_), channel_id=1, source_target_pairs={{0,64},{32,96},{64,0},{96,32},{1,65},{33,97},{65,1},{97,33},{2,66}... | collective-permute-start | bytes 983048 | tf_op jit(solution)/shard_map/ppermute | solution.py:259
  107.4 4.7 %product.1.refs_8_ = f32[8,256,128]{2,1,0:T(8,128)S(1)} custom-call(s32[4]{0:T(128)S(1)} %pad_add_fusion.refs_0_, s32[8]{0:T(128)S(1)} %copy-done.8, bf16[20,256,128]{2,1,0:T(8,128)(2,1)S(1)} %all-to-all-done.2.refs_2_, bf16[20,256,128]{2,1,0:T(8,128)(2,1)} %collective-permute-done.18.refs_3_, bf16[10,128,128]{2,1,0:T(8,128)(2,1)S(1)} %add_convert_fusion.6.refs_4_, ...), custom_call_target="tpu_custom_call" | custom-call | flops 335544320 | bytes 6291456 | tf_op jit(solution)/shard_map/product/pallas_call | solution.py:239
  113.1 7.5 %collective-permute-done.15.refs_5_ = bf16[10,128,128]{2,1,0:T(8,128)(2,1)} collective-permute-done((bf16[10,128,128]{2,1,0:T(8,128)(2,1)S(1)}, bf16[10,128,128]{2,1,0:T(8,128)(2,1)}, u32[]{:S(2)}, u32[]{:S(2)}) %collective-permute-start.15) | collective-permute-done | bytes 327712 | tf_op jit(solution)/shard_map/ppermute | solution.py:259
  121.1 2.7 %collective-permute-done.19.refs_3_ = bf16[20,256,128]{2,1,0:T(8,128)(2,1)S(1)} collective-permute-done((bf16[20,256,128]{2,1,0:T(8,128)(2,1)S(1)}, bf16[20,256,128]{2,1,0:T(8,128)(2,1)S(1)}, u32[]{:S(2)}, u32[]{:S(2)}) %collective-permute-start.19) | collective-permute-done | bytes 1310752 | tf_op jit(solution)/shard_map/ppermute | solution.py:259
  125.0 5.7 %product_end.1 = bf16[8,256,128]{2,1,0:T(8,128)(2,1)} custom-call(s32[4]{0:T(128)S(1)} %pad_add_fusion.refs_0_, s32[8]{0:T(128)S(1)} %copy-done.8, bf16[20,256,128]{2,1,0:T(8,128)(2,1)S(1)} %all-to-all-done.3.refs_2_, bf16[20,256,128]{2,1,0:T(8,128)(2,1)S(1)} %collective-permute-done.19.refs_3_, bf16[10,128,128]{2,1,0:T(8,128)(2,1)S(1)} %add_convert_fusion.2.refs_4_, ...), custom_call_target="tpu_custom_call" | custom-call | flops 335544320 | bytes 6291456 | tf_op jit(solution)/shard_map/product_end/pallas_call | solution.py:239
  (60 shorter events, 14.7 us)
Async XLA Ops:
  8.4 8.0 %collective-permute-start = (bf16[20,256,128]{2,1,0:T(8,128)(2,1)}, bf16[20,256,128]{2,1,0:T(8,128)(2,1)S(1)}, u32[]{:S(2)}, u32[]{:S(2)}) collective-permute-start(bf16[20,256,128]{2,1,0:T(8,128)(2,1)} %get-tuple-element.57), channel_id=1, source_target_pairs={{0,1},{1,0},{2,3},{3,2},{4,5},{5,4},{6,7},{7,6},{8,9},{9,8},{10,11... | collective-permute-start | bytes 3932168 | tf_op jit(solution)/shard_map/ppermute | solution.py:259
  9.9 17.9 %collective-permute-start.1 = (bf16[20,256,128]{2,1,0:T(8,128)(2,1)}, bf16[20,256,128]{2,1,0:T(8,128)(2,1)}, u32[]{:S(2)}, u32[]{:S(2)}) collective-permute-start(bf16[20,256,128]{2,1,0:T(8,128)(2,1)} %get-tuple-element.76), channel_id=1, source_target_pairs={{0,1},{1,0},{2,3},{3,2},{4,5},{5,4},{6,7},{7,6},{8,9},{9,8},{10,11... | collective-permute-start | bytes 3932168 | tf_op jit(solution)/shard_map/ppermute | solution.py:259
  10.0 6.4 %copy-start.10 = (bf16[20,256,128]{2,1,0:T(8,128)(2,1)S(1)}, bf16[20,256,128]{2,1,0:T(8,128)(2,1)}, u32[]{:S(2)}) copy-start(bf16[20,256,128]{2,1,0:T(8,128)(2,1)} %get-tuple-element.56) | copy-start | bytes 3932164
  17.8 10.0 %copy-start.9 = (bf16[20,256,128]{2,1,0:T(8,128)(2,1)S(1)}, bf16[20,256,128]{2,1,0:T(8,128)(2,1)}, u32[]{:S(2)}) copy-start(bf16[20,256,128]{2,1,0:T(8,128)(2,1)} %get-tuple-element.75) | copy-start | bytes 3932164
  17.8 21.8 %all-to-all-start = ((bf16[20,256,128]{2,1,0:T(8,128)(2,1)}), bf16[20,256,128]{2,1,0:T(8,128)(2,1)S(1)}, u32[]{:S(2)}, u32[]{:S(2)}) async-start(bf16[20,256,128]{2,1,0:T(8,128)(2,1)} %add_convert_fusion.1), calls=%async_computation | async-start | bytes 2621440 | tf_op jit(solution)/shard_map/all_to_all | solution.py:271
  22.2 21.3 %collective-permute-start.3 = (bf16[10,128,128]{2,1,0:T(8,128)(2,1)}, bf16[10,128,128]{2,1,0:T(8,128)(2,1)}, u32[]{:S(2)}, u32[]{:S(2)}) collective-permute-start(bf16[10,128,128]{2,1,0:T(8,128)(2,1)} %get-tuple-element.82), channel_id=1, source_target_pairs={{0,32},{32,64},{64,96},{96,0},{1,33},{33,65},{65,97},{97,1},{2,34}... | collective-permute-start | bytes 983048 | tf_op jit(solution)/shard_map/ppermute | solution.py:259
  23.8 19.7 %collective-permute-start.4 = (bf16[10,128,128]{2,1,0:T(8,128)(2,1)}, bf16[10,128,128]{2,1,0:T(8,128)(2,1)}, u32[]{:S(2)}, u32[]{:S(2)}) collective-permute-start(bf16[10,128,128]{2,1,0:T(8,128)(2,1)} %get-tuple-element.83), channel_id=1, source_target_pairs={{0,64},{32,96},{64,0},{96,32},{1,65},{33,97},{65,1},{97,33},{2,66}... | collective-permute-start | bytes 983048 | tf_op jit(solution)/shard_map/ppermute | solution.py:259
  27.1 16.4 %collective-permute-start.5 = (bf16[10,128,128]{2,1,0:T(8,128)(2,1)}, bf16[10,128,128]{2,1,0:T(8,128)(2,1)}, u32[]{:S(2)}, u32[]{:S(2)}) collective-permute-start(bf16[10,128,128]{2,1,0:T(8,128)(2,1)} %get-tuple-element.84), channel_id=1, source_target_pairs={{0,96},{32,0},{64,32},{96,64},{1,97},{33,1},{65,33},{97,65},{2,98}... | collective-permute-start | bytes 983048 | tf_op jit(solution)/shard_map/ppermute | solution.py:259
  39.8 3.7 %copy-start.12 = (bf16[10,128,128]{2,1,0:T(8,128)(2,1)S(1)}, bf16[10,128,128]{2,1,0:T(8,128)(2,1)}, u32[]{:S(2)}) copy-start(bf16[10,128,128]{2,1,0:T(8,128)(2,1)} %get-tuple-element.81) | copy-start | bytes 983044
  39.8 22.2 %all-to-all-start.1 = ((bf16[20,256,128]{2,1,0:T(8,128)(2,1)}), bf16[20,256,128]{2,1,0:T(8,128)(2,1)S(1)}, u32[]{:S(2)}, u32[]{:S(2)}) async-start(bf16[20,256,128]{2,1,0:T(8,128)(2,1)} %add_convert_fusion), calls=%async_computation.1 | async-start | bytes 2621440 | tf_op jit(solution)/shard_map/all_to_all | solution.py:271
  44.9 7.8 %collective-permute-start.6 = (bf16[10,128,128]{2,1,0:T(8,128)(2,1)S(1)}, bf16[10,128,128]{2,1,0:T(8,128)(2,1)S(1)}, u32[]{:S(2)}, u32[]{:S(2)}) collective-permute-start(bf16[10,128,128]{2,1,0:T(8,128)(2,1)S(1)} %add_convert_fusion.7), channel_id=1, source_target_pairs={{0,16},{16,0},{1,17},{17,1},{2,18},{18,2},{3,19},{19,3},{4,20},{20... | collective-permute-start | bytes 983048 | tf_op jit(solution)/shard_map/ppermute | solution.py:259
  46.1 15.7 %collective-permute-start.2 = (bf16[5,256,128]{2,1,0:T(8,128)(2,1)S(1)}, bf16[5,256,128]{2,1,0:T(8,128)(2,1)S(1)}, u32[]{:S(2)}, u32[]{:S(2)}) collective-permute-start(bf16[5,256,128]{2,1,0:T(8,128)(2,1)S(1)} %add_convert_fusion.9), channel_id=1, source_target_pairs={{0,2},{2,0},{1,3},{3,1},{4,6},{6,4},{5,7},{7,5},{8,10},{10,8},{9,1... | collective-permute-start | bytes 983048 | tf_op jit(solution)/shard_map/ppermute | solution.py:259
  52.8 14.8 %collective-permute-start.11 = (bf16[10,128,128]{2,1,0:T(8,128)(2,1)}, bf16[10,128,128]{2,1,0:T(8,128)(2,1)S(1)}, u32[]{:S(2)}, u32[]{:S(2)}) collective-permute-start(bf16[10,128,128]{2,1,0:T(8,128)(2,1)} %get-tuple-element.91), channel_id=1, source_target_pairs={{0,32},{32,64},{64,96},{96,0},{1,33},{33,65},{65,97},{97,1},{2,34}... | collective-permute-start | bytes 983048 | tf_op jit(solution)/shard_map/ppermute | solution.py:259
  54.2 13.4 %collective-permute-start.12 = (bf16[10,128,128]{2,1,0:T(8,128)(2,1)}, bf16[10,128,128]{2,1,0:T(8,128)(2,1)S(1)}, u32[]{:S(2)}, u32[]{:S(2)}) collective-permute-start(bf16[10,128,128]{2,1,0:T(8,128)(2,1)} %get-tuple-element.92), channel_id=1, source_target_pairs={{0,64},{32,96},{64,0},{96,32},{1,65},{33,97},{65,1},{97,33},{2,66}... | collective-permute-start | bytes 983048 | tf_op jit(solution)/shard_map/ppermute | solution.py:259
  57.5 11.2 %collective-permute-start.13 = (bf16[10,128,128]{2,1,0:T(8,128)(2,1)}, bf16[10,128,128]{2,1,0:T(8,128)(2,1)}, u32[]{:S(2)}, u32[]{:S(2)}) collective-permute-start(bf16[10,128,128]{2,1,0:T(8,128)(2,1)} %get-tuple-element.93), channel_id=1, source_target_pairs={{0,96},{32,0},{64,32},{96,64},{1,97},{33,1},{65,33},{97,65},{2,98}... | collective-permute-start | bytes 983048 | tf_op jit(solution)/shard_map/ppermute | solution.py:259
  63.6 5.2 %copy-start.11 = (bf16[10,128,128]{2,1,0:T(8,128)(2,1)S(1)}, bf16[10,128,128]{2,1,0:T(8,128)(2,1)}, u32[]{:S(2)}) copy-start(bf16[10,128,128]{2,1,0:T(8,128)(2,1)} %get-tuple-element.90) | copy-start | bytes 983044
  63.6 30.6 %all-to-all-start.2 = ((bf16[20,256,128]{2,1,0:T(8,128)(2,1)}), bf16[20,256,128]{2,1,0:T(8,128)(2,1)S(1)}, u32[]{:S(2)}, u32[]{:S(2)}) async-start(bf16[20,256,128]{2,1,0:T(8,128)(2,1)} %bitcast.4), calls=%async_computation.2 | async-start | bytes 2621440 | tf_op jit(solution)/shard_map/all_to_all | solution.py:271
  69.9 9.0 %collective-permute-start.14 = (bf16[10,128,128]{2,1,0:T(8,128)(2,1)S(1)}, bf16[10,128,128]{2,1,0:T(8,128)(2,1)S(1)}, u32[]{:S(2)}, u32[]{:S(2)}) collective-permute-start(bf16[10,128,128]{2,1,0:T(8,128)(2,1)S(1)} %add_convert_fusion.3), channel_id=1, source_target_pairs={{0,16},{16,0},{1,17},{17,1},{2,18},{18,2},{3,19},{19,3},{4,20},{20... | collective-permute-start | bytes 983048 | tf_op jit(solution)/shard_map/ppermute | solution.py:259
  71.2 12.6 %collective-permute-start.10 = (bf16[5,256,128]{2,1,0:T(8,128)(2,1)S(1)}, bf16[5,256,128]{2,1,0:T(8,128)(2,1)S(1)}, u32[]{:S(2)}, u32[]{:S(2)}) collective-permute-start(bf16[5,256,128]{2,1,0:T(8,128)(2,1)S(1)} %add_convert_fusion.5), channel_id=1, source_target_pairs={{0,2},{2,0},{1,3},{3,1},{4,6},{6,4},{5,7},{7,5},{8,10},{10,8},{9,1... | collective-permute-start | bytes 983048 | tf_op jit(solution)/shard_map/ppermute | solution.py:259
  73.7 10.9 %collective-permute-start.9 = (bf16[10,128,128]{2,1,0:T(8,128)(2,1)S(1)}, bf16[10,128,128]{2,1,0:T(8,128)(2,1)S(1)}, u32[]{:S(2)}, u32[]{:S(2)}) collective-permute-start(bf16[10,128,128]{2,1,0:T(8,128)(2,1)S(1)} %add_convert_fusion.6.refs_4_), channel_id=1, source_target_pairs={{0,96},{32,0},{64,32},{96,64},{1,97},{33,1},{65,33},{97,65},{2,98}... | collective-permute-start | bytes 983048 | tf_op jit(solution)/shard_map/ppermute | solution.py:259
  77.2 7.8 %collective-permute-start.8 = (bf16[10,128,128]{2,1,0:T(8,128)(2,1)S(1)}, bf16[10,128,128]{2,1,0:T(8,128)(2,1)S(1)}, u32[]{:S(2)}, u32[]{:S(2)}) collective-permute-start(bf16[10,128,128]{2,1,0:T(8,128)(2,1)S(1)} %add_convert_fusion.6.refs_4_), channel_id=1, source_target_pairs={{0,64},{32,96},{64,0},{96,32},{1,65},{33,97},{65,1},{97,33},{2,66}... | collective-permute-start | bytes 983048 | tf_op jit(solution)/shard_map/ppermute | solution.py:259
  78.9 15.2 %collective-permute-start.7 = (bf16[10,128,128]{2,1,0:T(8,128)(2,1)S(1)}, bf16[10,128,128]{2,1,0:T(8,128)(2,1)S(1)}, u32[]{:S(2)}, u32[]{:S(2)}) collective-permute-start(bf16[10,128,128]{2,1,0:T(8,128)(2,1)S(1)} %add_convert_fusion.6.refs_4_), channel_id=1, source_target_pairs={{0,32},{32,64},{64,96},{96,0},{1,33},{33,65},{65,97},{97,1},{2,34}... | collective-permute-start | bytes 983048 | tf_op jit(solution)/shard_map/ppermute | solution.py:259
  84.6 13.8 %copy-start.2 = (bf16[10,128,128]{2,1,0:T(8,128)(2,1)}, bf16[10,128,128]{2,1,0:T(8,128)(2,1)S(1)}, u32[]{:S(2)}) copy-start(bf16[10,128,128]{2,1,0:T(8,128)(2,1)S(1)} %collective-permute-done.9.refs_7_) | copy-start | bytes 983044
  85.0 13.4 %copy-start.4 = (bf16[10,128,128]{2,1,0:T(8,128)(2,1)}, bf16[10,128,128]{2,1,0:T(8,128)(2,1)S(1)}, u32[]{:S(2)}) copy-start(bf16[10,128,128]{2,1,0:T(8,128)(2,1)S(1)} %collective-permute-done.8.refs_6_) | copy-start | bytes 983044
  94.1 4.3 %copy-start.6 = (bf16[10,128,128]{2,1,0:T(8,128)(2,1)}, bf16[10,128,128]{2,1,0:T(8,128)(2,1)S(1)}, u32[]{:S(2)}) copy-start(bf16[10,128,128]{2,1,0:T(8,128)(2,1)S(1)} %collective-permute-done.7.refs_5_) | copy-start | bytes 983044
  96.6 7.8 %copy-start.8 = (s32[8]{0:T(128)S(1)}, s32[8]{0:T(128)}, u32[]{:S(2)}) copy-start(s32[8]{0:T(128)} %refs_1_.7) | copy-start | bytes 100
  96.6 7.8 %collective-permute-start.18 = (bf16[20,256,128]{2,1,0:T(8,128)(2,1)S(1)}, bf16[20,256,128]{2,1,0:T(8,128)(2,1)}, u32[]{:S(2)}, u32[]{:S(2)}) collective-permute-start(bf16[20,256,128]{2,1,0:T(8,128)(2,1)S(1)} %all-to-all-done.2.refs_2_), channel_id=1, source_target_pairs={{0,1},{1,0},{2,3},{3,2},{4,5},{5,4},{6,7},{7,6},{8,9},{9,8},{10,11... | collective-permute-start | bytes 3932168 | tf_op jit(solution)/shard_map/ppermute | solution.py:259
  98.4 22.2 %all-to-all-start.3 = ((bf16[20,256,128]{2,1,0:T(8,128)(2,1)}), bf16[20,256,128]{2,1,0:T(8,128)(2,1)S(1)}, u32[]{:S(2)}, u32[]{:S(2)}) async-start(bf16[20,256,128]{2,1,0:T(8,128)(2,1)} %bitcast.6), calls=%async_computation.3 | async-start | bytes 2621440 | tf_op jit(solution)/shard_map/all_to_all | solution.py:271
  101.9 11.1 %collective-permute-start.17 = (bf16[10,128,128]{2,1,0:T(8,128)(2,1)S(1)}, bf16[10,128,128]{2,1,0:T(8,128)(2,1)}, u32[]{:S(2)}, u32[]{:S(2)}) collective-permute-start(bf16[10,128,128]{2,1,0:T(8,128)(2,1)S(1)} %add_convert_fusion.2.refs_4_), channel_id=1, source_target_pairs={{0,96},{32,0},{64,32},{96,64},{1,97},{33,1},{65,33},{97,65},{2,98}... | collective-permute-start | bytes 983048 | tf_op jit(solution)/shard_map/ppermute | solution.py:259
  102.4 10.7 %collective-permute-start.16 = (bf16[10,128,128]{2,1,0:T(8,128)(2,1)S(1)}, bf16[10,128,128]{2,1,0:T(8,128)(2,1)}, u32[]{:S(2)}, u32[]{:S(2)}) collective-permute-start(bf16[10,128,128]{2,1,0:T(8,128)(2,1)S(1)} %add_convert_fusion.2.refs_4_), channel_id=1, source_target_pairs={{0,64},{32,96},{64,0},{96,32},{1,65},{33,97},{65,1},{97,33},{2,66}... | collective-permute-start | bytes 983048 | tf_op jit(solution)/shard_map/ppermute | solution.py:259
  104.0 16.6 %collective-permute-start.15 = (bf16[10,128,128]{2,1,0:T(8,128)(2,1)S(1)}, bf16[10,128,128]{2,1,0:T(8,128)(2,1)}, u32[]{:S(2)}, u32[]{:S(2)}) collective-permute-start(bf16[10,128,128]{2,1,0:T(8,128)(2,1)S(1)} %add_convert_fusion.2.refs_4_), channel_id=1, source_target_pairs={{0,32},{32,64},{64,96},{96,0},{1,33},{33,65},{65,97},{97,1},{2,34}... | collective-permute-start | bytes 983048 | tf_op jit(solution)/shard_map/ppermute | solution.py:259
  120.6 3.2 %collective-permute-start.19 = (bf16[20,256,128]{2,1,0:T(8,128)(2,1)S(1)}, bf16[20,256,128]{2,1,0:T(8,128)(2,1)S(1)}, u32[]{:S(2)}, u32[]{:S(2)}) collective-permute-start(bf16[20,256,128]{2,1,0:T(8,128)(2,1)S(1)} %all-to-all-done.3.refs_2_), channel_id=1, source_target_pairs={{0,1},{1,0},{2,3},{3,2},{4,5},{5,4},{6,7},{7,6},{8,9},{9,8},{10,11... | collective-permute-start | bytes 3932168 | tf_op jit(solution)/shard_map/ppermute | solution.py:259
  (5 other events, 5.1 us)

commit v8 on v5

--- a/solution.py
+++ b/solution.py
@@ -9,6 +9,7 @@
 WIDTH = 128
 PART = 40
 CHUNK = 4
+DEEP = 8
 Z, XL, Y, XH, CORE = 4, 2, 4, 2, 2
 HALF = PART // CORE
 ONE = HALF // Y
@@ -191,24 +192,25 @@
         copies.append(pltpu.make_async_copy(before_ref, before_buf, sems.at[2 + Z]))
     for copy in copies:
         copy.start()
-    for k in range(CHUNK):
+    for k in range(DEEP):
         one_buf[PART + k] = jnp.zeros(one_buf.shape[1:], one_buf.dtype)
     for copy in copies:
         copy.wait()
     rows, cols = out_ref.shape[1:]
-    deep = lax.broadcasted_iota(jnp.int32, (CHUNK * WIDTH, cols), 0)
+    deep = lax.broadcasted_iota(jnp.int32, (DEEP * WIDTH, cols), 0)
     row = lax.broadcasted_iota(jnp.int32, (rows, cols), 0) + row_first
     col = lax.broadcasted_iota(jnp.int32, (rows, cols), 1) + col_first
     for s in range(len(plan)):
-        first, begin, end, _, chunks = plan[s]
+        first, begin, end, _, _ = plan[s]
+        chunks = lax.shift_right_logical(end - begin + (DEEP - 1), 3)
         size = size_ref[s]
         deep_end = jnp.minimum(size, end * WIDTH)
 
         def add(c, total):
-            block = begin + c * CHUNK
+            block = begin + c * DEEP
             q = first + block - lo
-            left = jnp.concatenate([one_buf[q + k] for k in range(CHUNK)], axis=1)
-            right = two_buf[pl.ds(q, CHUNK)].reshape(CHUNK * WIDTH, cols)
+            left = jnp.concatenate([one_buf[q + k] for k in range(DEEP)], axis=1)
+            right = two_buf[pl.ds(q, DEEP)].reshape(DEEP * WIDTH, cols)
             right = jnp.where(deep < deep_end - block * WIDTH, right, jnp.bfloat16(0.0))
             return total + jnp.dot(left, right, preferred_element_type=jnp.float32)
 
@@ -231,8 +233,8 @@
         in_specs=[SMEM, SMEM] + [ANY] * (2 + Z + end),
         out_specs=VMEM,
         scratch_shapes=[
-            pltpu.VMEM((PART + CHUNK, rows, WIDTH), jnp.bfloat16),
-            pltpu.VMEM((PART + CHUNK, WIDTH, cols), jnp.bfloat16),
+            pltpu.VMEM((PART + DEEP, rows, WIDTH), jnp.bfloat16),
+            pltpu.VMEM((PART + DEEP, WIDTH, cols), jnp.bfloat16),
             pltpu.SemaphoreType.DMA((2 + Z + end,)),
         ]
         + [pltpu.VMEM(shape, jnp.float32)] * end,

time: 132 us -> 131 us (level)
  Pallas kernels: 32.5 us -> 30.8 us
    pallas_call x2, Pallas kernels: 10.7 us -> 9.35 us  [product(): pl.pallas_call(lambda *refs: product_kernel(part, scale, *refs), out_shap...]
  transfers between devices with their start and end apart: 24 -> 24, of which waited for: 10 -> 11; matrix products, arithmetic and copies ran while one was open for 9% -> 9% of each run, Pallas kernels for 14% -> 13%
where the time goes in v8:
time: 131 us
  starting transfers between devices  45.9 us (35%)
  waiting for transfers between devices  36.6 us (28%)
  Pallas kernels  30.8 us (24%)
  local copies, waits for them, and re-layouts  8.88 us (7%)
  other arithmetic  8.2 us (6%)
    ppermute x20, waiting for transfers between devices, shift(): lax.ppermute(array, axis, [(i, (i + step) % size) for i in range(size)])  34.1 us
    ppermute x20, starting transfers between devices, shift(): lax.ppermute(array, axis, [(i, (i + step) % size) for i in range(size)])  30.2 us
    all_to_all x4, starting transfers between devices, over_y(): return lax.all_to_all(array, 'y', 0, 0, tiled=True)  15.7 us
    pallas_call x2, Pallas kernels, right_terms(): pl.pallas_call(lambda *refs: right_kernel(part, *refs), out_shape=[jax.Sh...  13.1 us
    pallas_call x2, Pallas kernels, product(): pl.pallas_call(lambda *refs: product_kernel(part, scale, *refs), out_shap...  9.35 us
    pallas_call x1, Pallas kernels, left_terms(): pl.pallas_call(left_kernel, out_shape=[jax.ShapeDtypeStruct((HALF, rows,...  8.37 us
    convert_element_type x10, other arithmetic, total(): sum((term.astype(jnp.float32) for term in terms)).astype(jnp.bfloat16)  8.13 us
    unnamed x26, local copies, waits for them, and re-layouts  5.15 us
  transfers between devices with their start and end apart: 24, of which 11 were waited for; matrix products, arithmetic and copies ran while one was open for 9% of the time, Pallas kernels for 13%

profile of v8, /device:TPU:1, one launch (start us, length us, event | category | flops | bytes accessed | tf_op | source)
XLA Modules:
  0.0 130.7 jit_solution(1469836975076164755)
XLA Ops:
  0.0 8.4 %left.1 = (bf16[20,256,128]{2,1,0:T(8,128)(2,1)}, bf16[20,256,128]{2,1,0:T(8,128)(2,1)}, bf16[20,256,128]{2,1,0:T(8,128)(2,1)}, bf16[20,256,128]{2,1,0:T(8,128)(2,1)}) custom-call(s32[1]{0:T(128)} %bitcast.at_ref, s32[8]{0:T(128)} %refs_1_.7, bf16[8,256,256]{2,1,0:T(8,128)(2,1)} %edge_ref.1, bf16[8,256,2048]{2,1,0:T(8,128)(2,1)} %site_ref.1), custom_call_target="tpu_custom_call" | custom-call | flops 1342177280 | bytes 12582912 | tf_op jit(solution)/shard_map/left/pallas_call | solution.py:93
  8.4 1.5 %collective-permute-start = (bf16[20,256,128]{2,1,0:T(8,128)(2,1)}, bf16[20,256,128]{2,1,0:T(8,128)(2,1)S(1)}, u32[]{:S(2)}, u32[]{:S(2)}) collective-permute-start(bf16[20,256,128]{2,1,0:T(8,128)(2,1)} %get-tuple-element.57), channel_id=1, source_target_pairs={{0,1},{1,0},{2,3},{3,2},{4,5},{5,4},{6,7},{7,6},{8,9},{9,8},{10,11... | collective-permute-start | bytes 3932168 | tf_op jit(solution)/shard_map/ppermute | solution.py:250
  10.0 6.6 %right.2 = (bf16[10,128,128]{2,1,0:T(8,128)(2,1)}, bf16[10,128,128]{2,1,0:T(8,128)(2,1)}, bf16[10,128,128]{2,1,0:T(8,128)(2,1)}, bf16[10,128,128]{2,1,0:T(8,128)(2,1)}) custom-call(s32[1]{0:T(128)} %bitcast.1.refs_0_, s32[8]{0:T(128)} %refs_1_.7, bf16[8,2048,512]{2,1,0:T(8,128)(2,1)} %refs_2_.1, bf16[8,512,128]{2,1,0:T(8,128)(2,1)} %refs_3_.1), custom_call_target="tpu_custom_call" | custom-call | flops 671088640 | bytes 10485760 | tf_op jit(solution)/shard_map/right/pallas_call | solution.py:156
  16.6 1.4 %add_convert_fusion.1 = bf16[20,256,128]{2,1,0:T(8,128)(2,1)} fusion(bf16[20,256,128]{2,1,0:T(8,128)(2,1)S(1)} %collective-permute-done, bf16[20,256,128]{2,1,0:T(8,128)(2,1)S(1)} %copy-done.10), kind=kLoop, calls=%fused_computation.1 | loop fusion | flops 2621440 | bytes 3932160 | tf_op jit(solution)/shard_map/convert_element_type | solution.py:254
  18.1 4.4 %all-to-all-start = ((bf16[20,256,128]{2,1,0:T(8,128)(2,1)}), bf16[20,256,128]{2,1,0:T(8,128)(2,1)S(1)}, u32[]{:S(2)}, u32[]{:S(2)}) async-start(bf16[20,256,128]{2,1,0:T(8,128)(2,1)} %add_convert_fusion.1), calls=%async_computation | async-start | bytes 2621440 | tf_op jit(solution)/shard_map/all_to_all | solution.py:262
  22.5 1.6 %collective-permute-start.3 = (bf16[10,128,128]{2,1,0:T(8,128)(2,1)}, bf16[10,128,128]{2,1,0:T(8,128)(2,1)}, u32[]{:S(2)}, u32[]{:S(2)}) collective-permute-start(bf16[10,128,128]{2,1,0:T(8,128)(2,1)} %get-tuple-element.82), channel_id=1, source_target_pairs={{0,32},{32,64},{64,96},{96,0},{1,33},{33,65},{65,97},{97,1},{2,34}... | collective-permute-start | bytes 983048 | tf_op jit(solution)/shard_map/ppermute | solution.py:250
  24.1 3.3 %collective-permute-start.4 = (bf16[10,128,128]{2,1,0:T(8,128)(2,1)}, bf16[10,128,128]{2,1,0:T(8,128)(2,1)}, u32[]{:S(2)}, u32[]{:S(2)}) collective-permute-start(bf16[10,128,128]{2,1,0:T(8,128)(2,1)} %get-tuple-element.83), channel_id=1, source_target_pairs={{0,64},{32,96},{64,0},{96,32},{1,65},{33,97},{65,1},{97,33},{2,66}... | collective-permute-start | bytes 983048 | tf_op jit(solution)/shard_map/ppermute | solution.py:250
  28.2 2.7 %add_convert_fusion = bf16[20,256,128]{2,1,0:T(8,128)(2,1)} fusion(bf16[20,256,128]{2,1,0:T(8,128)(2,1)} %collective-permute-done.1, bf16[20,256,128]{2,1,0:T(8,128)(2,1)S(1)} %copy-done.9), kind=kLoop, calls=%fused_computation | loop fusion | flops 2621440 | bytes 3932160 | tf_op jit(solution)/shard_map/convert_element_type | solution.py:254
  30.9 6.5 %right.3 = (bf16[10,128,128]{2,1,0:T(8,128)(2,1)}, bf16[10,128,128]{2,1,0:T(8,128)(2,1)}, bf16[10,128,128]{2,1,0:T(8,128)(2,1)}, bf16[10,128,128]{2,1,0:T(8,128)(2,1)}) custom-call(s32[1]{0:T(128)} %bitcast.1.refs_0_, s32[8]{0:T(128)} %refs_1_.7, bf16[8,2048,512]{2,1,0:T(8,128)(2,1)} %refs_2_.1, bf16[8,512,128]{2,1,0:T(8,128)(2,1)} %refs_3_.1), custom_call_target="tpu_custom_call" | custom-call | flops 671088640 | bytes 10485760 | tf_op jit(solution)/shard_map/right/pallas_call | solution.py:156
  37.4 2.5 %all-to-all-done = bf16[20,256,128]{2,1,0:T(8,128)(2,1)S(1)} async-done(((bf16[20,256,128]{2,1,0:T(8,128)(2,1)}), bf16[20,256,128]{2,1,0:T(8,128)(2,1)S(1)}, u32[]{:S(2)}, u32[]{:S(2)}) %all-to-all-start) | async-done | bytes 1310752 | tf_op jit(solution)/shard_map/all_to_all | solution.py:262
  40.1 3.7 %all-to-all-start.1 = ((bf16[20,256,128]{2,1,0:T(8,128)(2,1)}), bf16[20,256,128]{2,1,0:T(8,128)(2,1)S(1)}, u32[]{:S(2)}, u32[]{:S(2)}) async-start(bf16[20,256,128]{2,1,0:T(8,128)(2,1)} %add_convert_fusion), calls=%async_computation.1 | async-start | bytes 2621440 | tf_op jit(solution)/shard_map/all_to_all | solution.py:262
  43.8 1.4 %add_convert_fusion.7 = bf16[10,128,128]{2,1,0:T(8,128)(2,1)S(1)} fusion(bf16[10,128,128]{2,1,0:T(8,128)(2,1)} %collective-permute-done.5, bf16[10,128,128]{2,1,0:T(8,128)(2,1)} %collective-permute-done.4, bf16[10,128,128]{2,1,0:T(8,128)(2,1)} %collective-permute-done.3, bf16[10,128,128]{2,1,0:T(8,128)(2,1)S(1)} %copy-done.12), kind=kLoop, calls=%fused_computation.7 | loop fusion | flops 1310720 | bytes 1638400 | tf_op jit(solution)/shard_map/convert_element_type | solution.py:254
  46.5 2.5 %collective-permute-start.2 = (bf16[5,256,128]{2,1,0:T(8,128)(2,1)S(1)}, bf16[5,256,128]{2,1,0:T(8,128)(2,1)S(1)}, u32[]{:S(2)}, u32[]{:S(2)}) collective-permute-start(bf16[5,256,128]{2,1,0:T(8,128)(2,1)S(1)} %add_convert_fusion.9), channel_id=1, source_target_pairs={{0,2},{2,0},{1,3},{3,1},{4,6},{6,4},{5,7},{7,5},{8,10},{10,8},{9,1... | collective-permute-start | bytes 983048 | tf_op jit(solution)/shard_map/ppermute | solution.py:250
  48.9 4.1 %collective-permute-done.6 = bf16[10,128,128]{2,1,0:T(8,128)(2,1)S(1)} collective-permute-done((bf16[10,128,128]{2,1,0:T(8,128)(2,1)S(1)}, bf16[10,128,128]{2,1,0:T(8,128)(2,1)S(1)}, u32[]{:S(2)}, u32[]{:S(2)}) %collective-permute-start.6) | collective-permute-done | bytes 327712 | tf_op jit(solution)/shard_map/ppermute | solution.py:250
  53.1 1.5 %collective-permute-start.11 = (bf16[10,128,128]{2,1,0:T(8,128)(2,1)}, bf16[10,128,128]{2,1,0:T(8,128)(2,1)S(1)}, u32[]{:S(2)}, u32[]{:S(2)}) collective-permute-start(bf16[10,128,128]{2,1,0:T(8,128)(2,1)} %get-tuple-element.91), channel_id=1, source_target_pairs={{0,32},{32,64},{64,96},{96,0},{1,33},{33,65},{65,97},{97,1},{2,34}... | collective-permute-start | bytes 983048 | tf_op jit(solution)/shard_map/ppermute | solution.py:250
  54.6 3.3 %collective-permute-start.12 = (bf16[10,128,128]{2,1,0:T(8,128)(2,1)}, bf16[10,128,128]{2,1,0:T(8,128)(2,1)S(1)}, u32[]{:S(2)}, u32[]{:S(2)}) collective-permute-start(bf16[10,128,128]{2,1,0:T(8,128)(2,1)} %get-tuple-element.92), channel_id=1, source_target_pairs={{0,64},{32,96},{64,0},{96,32},{1,65},{33,97},{65,1},{97,33},{2,66}... | collective-permute-start | bytes 983048 | tf_op jit(solution)/shard_map/ppermute | solution.py:250
  58.7 3.6 %collective-permute-done.2 = bf16[5,256,128]{2,1,0:T(8,128)(2,1)S(1)} collective-permute-done((bf16[5,256,128]{2,1,0:T(8,128)(2,1)S(1)}, bf16[5,256,128]{2,1,0:T(8,128)(2,1)S(1)}, u32[]{:S(2)}, u32[]{:S(2)}) %collective-permute-start.2) | collective-permute-done | bytes 327712 | tf_op jit(solution)/shard_map/ppermute | solution.py:250
  62.5 1.4 %broadcast_in_dim.4 = bf16[4,5,256,128]{3,2,1,0:T(8,128)(2,1)} broadcast(bf16[5,256,128]{2,1,0:T(8,128)(2,1)S(1)} %add_convert_fusion.8), dimensions={1,2,3} | broadcast | bytes 1638400 | tf_op jit(solution)/shard_map/broadcast_in_dim | solution.py:282
  63.9 4.0 %all-to-all-start.2 = ((bf16[20,256,128]{2,1,0:T(8,128)(2,1)}), bf16[20,256,128]{2,1,0:T(8,128)(2,1)S(1)}, u32[]{:S(2)}, u32[]{:S(2)}) async-start(bf16[20,256,128]{2,1,0:T(8,128)(2,1)} %bitcast.4), calls=%async_computation.2 | async-start | bytes 2621440 | tf_op jit(solution)/shard_map/all_to_all | solution.py:262
  71.5 2.5 %collective-permute-start.10 = (bf16[5,256,128]{2,1,0:T(8,128)(2,1)S(1)}, bf16[5,256,128]{2,1,0:T(8,128)(2,1)S(1)}, u32[]{:S(2)}, u32[]{:S(2)}) collective-permute-start(bf16[5,256,128]{2,1,0:T(8,128)(2,1)S(1)} %add_convert_fusion.5), channel_id=1, source_target_pairs={{0,2},{2,0},{1,3},{3,1},{4,6},{6,4},{5,7},{7,5},{8,10},{10,8},{9,1... | collective-permute-start | bytes 983048 | tf_op jit(solution)/shard_map/ppermute | solution.py:250
  74.0 3.6 %collective-permute-start.9 = (bf16[10,128,128]{2,1,0:T(8,128)(2,1)S(1)}, bf16[10,128,128]{2,1,0:T(8,128)(2,1)S(1)}, u32[]{:S(2)}, u32[]{:S(2)}) collective-permute-start(bf16[10,128,128]{2,1,0:T(8,128)(2,1)S(1)} %add_convert_fusion.6.refs_4_), channel_id=1, source_target_pairs={{0,96},{32,0},{64,32},{96,64},{1,97},{33,1},{65,33},{97,65},{2,98}... | collective-permute-start | bytes 983048 | tf_op jit(solution)/shard_map/ppermute | solution.py:250
  77.6 1.7 %collective-permute-start.8 = (bf16[10,128,128]{2,1,0:T(8,128)(2,1)S(1)}, bf16[10,128,128]{2,1,0:T(8,128)(2,1)S(1)}, u32[]{:S(2)}, u32[]{:S(2)}) collective-permute-start(bf16[10,128,128]{2,1,0:T(8,128)(2,1)S(1)} %add_convert_fusion.6.refs_4_), channel_id=1, source_target_pairs={{0,64},{32,96},{64,0},{96,32},{1,65},{33,97},{65,1},{97,33},{2,66}... | collective-permute-start | bytes 983048 | tf_op jit(solution)/shard_map/ppermute | solution.py:250
  79.4 4.8 %collective-permute-done.10 = bf16[5,256,128]{2,1,0:T(8,128)(2,1)S(1)} collective-permute-done((bf16[5,256,128]{2,1,0:T(8,128)(2,1)S(1)}, bf16[5,256,128]{2,1,0:T(8,128)(2,1)S(1)}, u32[]{:S(2)}, u32[]{:S(2)}) %collective-permute-start.10) | collective-permute-done | bytes 327712 | tf_op jit(solution)/shard_map/ppermute | solution.py:250
  85.4 9.1 %collective-permute-done.7.refs_5_ = bf16[10,128,128]{2,1,0:T(8,128)(2,1)S(1)} collective-permute-done((bf16[10,128,128]{2,1,0:T(8,128)(2,1)S(1)}, bf16[10,128,128]{2,1,0:T(8,128)(2,1)S(1)}, u32[]{:S(2)}, u32[]{:S(2)}) %collective-permute-start.7) | collective-permute-done | bytes 327712 | tf_op jit(solution)/shard_map/ppermute | solution.py:250
  94.5 1.8 %collective-permute-start.18 = (bf16[20,256,128]{2,1,0:T(8,128)(2,1)S(1)}, bf16[20,256,128]{2,1,0:T(8,128)(2,1)}, u32[]{:S(2)}, u32[]{:S(2)}) collective-permute-start(bf16[20,256,128]{2,1,0:T(8,128)(2,1)S(1)} %all-to-all-done.2.refs_2_), channel_id=1, source_target_pairs={{0,1},{1,0},{2,3},{3,2},{4,5},{5,4},{6,7},{7,6},{8,9},{9,8},{10,11... | collective-permute-start | bytes 3932168 | tf_op jit(solution)/shard_map/ppermute | solution.py:250
  96.3 2.4 %broadcast_in_dim.5 = bf16[4,5,256,128]{3,2,1,0:T(8,128)(2,1)} broadcast(bf16[5,256,128]{2,1,0:T(8,128)(2,1)} %add_convert_fusion.4), dimensions={1,2,3} | broadcast | bytes 1638400 | tf_op jit(solution)/shard_map/broadcast_in_dim | solution.py:282
  98.6 3.6 %all-to-all-start.3 = ((bf16[20,256,128]{2,1,0:T(8,128)(2,1)}), bf16[20,256,128]{2,1,0:T(8,128)(2,1)S(1)}, u32[]{:S(2)}, u32[]{:S(2)}) async-start(bf16[20,256,128]{2,1,0:T(8,128)(2,1)} %bitcast.6), calls=%async_computation.3 | async-start | bytes 2621440 | tf_op jit(solution)/shard_map/all_to_all | solution.py:262
  102.6 1.7 %collective-permute-start.16 = (bf16[10,128,128]{2,1,0:T(8,128)(2,1)S(1)}, bf16[10,128,128]{2,1,0:T(8,128)(2,1)}, u32[]{:S(2)}, u32[]{:S(2)}) collective-permute-start(bf16[10,128,128]{2,1,0:T(8,128)(2,1)S(1)} %add_convert_fusion.2.refs_4_), channel_id=1, source_target_pairs={{0,64},{32,96},{64,0},{96,32},{1,65},{33,97},{65,1},{97,33},{2,66}... | collective-permute-start | bytes 983048 | tf_op jit(solution)/shard_map/ppermute | solution.py:250
  107.6 4.0 %product.1.refs_8_ = f32[8,256,128]{2,1,0:T(8,128)S(1)} custom-call(s32[4]{0:T(128)S(1)} %pad_add_fusion.refs_0_, s32[8]{0:T(128)S(1)} %copy-done.8, bf16[20,256,128]{2,1,0:T(8,128)(2,1)S(1)} %all-to-all-done.2.refs_2_, bf16[20,256,128]{2,1,0:T(8,128)(2,1)} %collective-permute-done.18.refs_3_, bf16[10,128,128]{2,1,0:T(8,128)(2,1)S(1)} %add_convert_fusion.6.refs_4_, ...), custom_call_target="tpu_custom_call" | custom-call | flops 335544320 | bytes 6291456 | tf_op jit(solution)/shard_map/product/pallas_call | solution.py:230
  113.0 7.8 %collective-permute-done.15.refs_5_ = bf16[10,128,128]{2,1,0:T(8,128)(2,1)} collective-permute-done((bf16[10,128,128]{2,1,0:T(8,128)(2,1)S(1)}, bf16[10,128,128]{2,1,0:T(8,128)(2,1)}, u32[]{:S(2)}, u32[]{:S(2)}) %collective-permute-start.15) | collective-permute-done | bytes 327712 | tf_op jit(solution)/shard_map/ppermute | solution.py:250
  121.3 2.7 %collective-permute-done.19.refs_3_ = bf16[20,256,128]{2,1,0:T(8,128)(2,1)S(1)} collective-permute-done((bf16[20,256,128]{2,1,0:T(8,128)(2,1)S(1)}, bf16[20,256,128]{2,1,0:T(8,128)(2,1)S(1)}, u32[]{:S(2)}, u32[]{:S(2)}) %collective-permute-start.19) | collective-permute-done | bytes 1310752 | tf_op jit(solution)/shard_map/ppermute | solution.py:250
  125.2 5.3 %product_end.1 = bf16[8,256,128]{2,1,0:T(8,128)(2,1)} custom-call(s32[4]{0:T(128)S(1)} %pad_add_fusion.refs_0_, s32[8]{0:T(128)S(1)} %copy-done.8, bf16[20,256,128]{2,1,0:T(8,128)(2,1)S(1)} %all-to-all-done.3.refs_2_, bf16[20,256,128]{2,1,0:T(8,128)(2,1)S(1)} %collective-permute-done.19.refs_3_, bf16[10,128,128]{2,1,0:T(8,128)(2,1)S(1)} %add_convert_fusion.2.refs_4_, ...), custom_call_target="tpu_custom_call" | custom-call | flops 335544320 | bytes 6291456 | tf_op jit(solution)/shard_map/product_end/pallas_call | solution.py:230
  (60 shorter events, 15.2 us)
Async XLA Ops:
  8.4 8.3 %collective-permute-start = (bf16[20,256,128]{2,1,0:T(8,128)(2,1)}, bf16[20,256,128]{2,1,0:T(8,128)(2,1)S(1)}, u32[]{:S(2)}, u32[]{:S(2)}) collective-permute-start(bf16[20,256,128]{2,1,0:T(8,128)(2,1)} %get-tuple-element.57), channel_id=1, source_target_pairs={{0,1},{1,0},{2,3},{3,2},{4,5},{5,4},{6,7},{7,6},{8,9},{9,8},{10,11... | collective-permute-start | bytes 3932168 | tf_op jit(solution)/shard_map/ppermute | solution.py:250
  9.9 18.3 %collective-permute-start.1 = (bf16[20,256,128]{2,1,0:T(8,128)(2,1)}, bf16[20,256,128]{2,1,0:T(8,128)(2,1)}, u32[]{:S(2)}, u32[]{:S(2)}) collective-permute-start(bf16[20,256,128]{2,1,0:T(8,128)(2,1)} %get-tuple-element.76), channel_id=1, source_target_pairs={{0,1},{1,0},{2,3},{3,2},{4,5},{5,4},{6,7},{7,6},{8,9},{9,8},{10,11... | collective-permute-start | bytes 3932168 | tf_op jit(solution)/shard_map/ppermute | solution.py:250
  10.0 6.7 %copy-start.10 = (bf16[20,256,128]{2,1,0:T(8,128)(2,1)S(1)}, bf16[20,256,128]{2,1,0:T(8,128)(2,1)}, u32[]{:S(2)}) copy-start(bf16[20,256,128]{2,1,0:T(8,128)(2,1)} %get-tuple-element.56) | copy-start | bytes 3932164
  18.1 10.1 %copy-start.9 = (bf16[20,256,128]{2,1,0:T(8,128)(2,1)S(1)}, bf16[20,256,128]{2,1,0:T(8,128)(2,1)}, u32[]{:S(2)}) copy-start(bf16[20,256,128]{2,1,0:T(8,128)(2,1)} %get-tuple-element.75) | copy-start | bytes 3932164
  18.1 21.8 %all-to-all-start = ((bf16[20,256,128]{2,1,0:T(8,128)(2,1)}), bf16[20,256,128]{2,1,0:T(8,128)(2,1)S(1)}, u32[]{:S(2)}, u32[]{:S(2)}) async-start(bf16[20,256,128]{2,1,0:T(8,128)(2,1)} %add_convert_fusion.1), calls=%async_computation | async-start | bytes 2621440 | tf_op jit(solution)/shard_map/all_to_all | solution.py:262
  22.5 21.3 %collective-permute-start.3 = (bf16[10,128,128]{2,1,0:T(8,128)(2,1)}, bf16[10,128,128]{2,1,0:T(8,128)(2,1)}, u32[]{:S(2)}, u32[]{:S(2)}) collective-permute-start(bf16[10,128,128]{2,1,0:T(8,128)(2,1)} %get-tuple-element.82), channel_id=1, source_target_pairs={{0,32},{32,64},{64,96},{96,0},{1,33},{33,65},{65,97},{97,1},{2,34}... | collective-permute-start | bytes 983048 | tf_op jit(solution)/shard_map/ppermute | solution.py:250
  24.1 19.7 %collective-permute-start.4 = (bf16[10,128,128]{2,1,0:T(8,128)(2,1)}, bf16[10,128,128]{2,1,0:T(8,128)(2,1)}, u32[]{:S(2)}, u32[]{:S(2)}) collective-permute-start(bf16[10,128,128]{2,1,0:T(8,128)(2,1)} %get-tuple-element.83), channel_id=1, source_target_pairs={{0,64},{32,96},{64,0},{96,32},{1,65},{33,97},{65,1},{97,33},{2,66}... | collective-permute-start | bytes 983048 | tf_op jit(solution)/shard_map/ppermute | solution.py:250
  27.4 16.4 %collective-permute-start.5 = (bf16[10,128,128]{2,1,0:T(8,128)(2,1)}, bf16[10,128,128]{2,1,0:T(8,128)(2,1)}, u32[]{:S(2)}, u32[]{:S(2)}) collective-permute-start(bf16[10,128,128]{2,1,0:T(8,128)(2,1)} %get-tuple-element.84), channel_id=1, source_target_pairs={{0,96},{32,0},{64,32},{96,64},{1,97},{33,1},{65,33},{97,65},{2,98}... | collective-permute-start | bytes 983048 | tf_op jit(solution)/shard_map/ppermute | solution.py:250
  40.1 3.7 %copy-start.12 = (bf16[10,128,128]{2,1,0:T(8,128)(2,1)S(1)}, bf16[10,128,128]{2,1,0:T(8,128)(2,1)}, u32[]{:S(2)}) copy-start(bf16[10,128,128]{2,1,0:T(8,128)(2,1)} %get-tuple-element.81) | copy-start | bytes 983044
  40.1 22.2 %all-to-all-start.1 = ((bf16[20,256,128]{2,1,0:T(8,128)(2,1)}), bf16[20,256,128]{2,1,0:T(8,128)(2,1)S(1)}, u32[]{:S(2)}, u32[]{:S(2)}) async-start(bf16[20,256,128]{2,1,0:T(8,128)(2,1)} %add_convert_fusion), calls=%async_computation.1 | async-start | bytes 2621440 | tf_op jit(solution)/shard_map/all_to_all | solution.py:262
  45.2 7.8 %collective-permute-start.6 = (bf16[10,128,128]{2,1,0:T(8,128)(2,1)S(1)}, bf16[10,128,128]{2,1,0:T(8,128)(2,1)S(1)}, u32[]{:S(2)}, u32[]{:S(2)}) collective-permute-start(bf16[10,128,128]{2,1,0:T(8,128)(2,1)S(1)} %add_convert_fusion.7), channel_id=1, source_target_pairs={{0,16},{16,0},{1,17},{17,1},{2,18},{18,2},{3,19},{19,3},{4,20},{20... | collective-permute-start | bytes 983048 | tf_op jit(solution)/shard_map/ppermute | solution.py:250
  46.5 15.8 %collective-permute-start.2 = (bf16[5,256,128]{2,1,0:T(8,128)(2,1)S(1)}, bf16[5,256,128]{2,1,0:T(8,128)(2,1)S(1)}, u32[]{:S(2)}, u32[]{:S(2)}) collective-permute-start(bf16[5,256,128]{2,1,0:T(8,128)(2,1)S(1)} %add_convert_fusion.9), channel_id=1, source_target_pairs={{0,2},{2,0},{1,3},{3,1},{4,6},{6,4},{5,7},{7,5},{8,10},{10,8},{9,1... | collective-permute-start | bytes 983048 | tf_op jit(solution)/shard_map/ppermute | solution.py:250
  53.1 14.8 %collective-permute-start.11 = (bf16[10,128,128]{2,1,0:T(8,128)(2,1)}, bf16[10,128,128]{2,1,0:T(8,128)(2,1)S(1)}, u32[]{:S(2)}, u32[]{:S(2)}) collective-permute-start(bf16[10,128,128]{2,1,0:T(8,128)(2,1)} %get-tuple-element.91), channel_id=1, source_target_pairs={{0,32},{32,64},{64,96},{96,0},{1,33},{33,65},{65,97},{97,1},{2,34}... | collective-permute-start | bytes 983048 | tf_op jit(solution)/shard_map/ppermute | solution.py:250
  54.6 13.4 %collective-permute-start.12 = (bf16[10,128,128]{2,1,0:T(8,128)(2,1)}, bf16[10,128,128]{2,1,0:T(8,128)(2,1)S(1)}, u32[]{:S(2)}, u32[]{:S(2)}) collective-permute-start(bf16[10,128,128]{2,1,0:T(8,128)(2,1)} %get-tuple-element.92), channel_id=1, source_target_pairs={{0,64},{32,96},{64,0},{96,32},{1,65},{33,97},{65,1},{97,33},{2,66}... | collective-permute-start | bytes 983048 | tf_op jit(solution)/shard_map/ppermute | solution.py:250
  57.9 11.3 %collective-permute-start.13 = (bf16[10,128,128]{2,1,0:T(8,128)(2,1)}, bf16[10,128,128]{2,1,0:T(8,128)(2,1)}, u32[]{:S(2)}, u32[]{:S(2)}) collective-permute-start(bf16[10,128,128]{2,1,0:T(8,128)(2,1)} %get-tuple-element.93), channel_id=1, source_target_pairs={{0,96},{32,0},{64,32},{96,64},{1,97},{33,1},{65,33},{97,65},{2,98}... | collective-permute-start | bytes 983048 | tf_op jit(solution)/shard_map/ppermute | solution.py:250
  63.9 5.3 %copy-start.11 = (bf16[10,128,128]{2,1,0:T(8,128)(2,1)S(1)}, bf16[10,128,128]{2,1,0:T(8,128)(2,1)}, u32[]{:S(2)}) copy-start(bf16[10,128,128]{2,1,0:T(8,128)(2,1)} %get-tuple-element.90) | copy-start | bytes 983044
  63.9 30.6 %all-to-all-start.2 = ((bf16[20,256,128]{2,1,0:T(8,128)(2,1)}), bf16[20,256,128]{2,1,0:T(8,128)(2,1)S(1)}, u32[]{:S(2)}, u32[]{:S(2)}) async-start(bf16[20,256,128]{2,1,0:T(8,128)(2,1)} %bitcast.4), calls=%async_computation.2 | async-start | bytes 2621440 | tf_op jit(solution)/shard_map/all_to_all | solution.py:262
  70.3 9.0 %collective-permute-start.14 = (bf16[10,128,128]{2,1,0:T(8,128)(2,1)S(1)}, bf16[10,128,128]{2,1,0:T(8,128)(2,1)S(1)}, u32[]{:S(2)}, u32[]{:S(2)}) collective-permute-start(bf16[10,128,128]{2,1,0:T(8,128)(2,1)S(1)} %add_convert_fusion.3), channel_id=1, source_target_pairs={{0,16},{16,0},{1,17},{17,1},{2,18},{18,2},{3,19},{19,3},{4,20},{20... | collective-permute-start | bytes 983048 | tf_op jit(solution)/shard_map/ppermute | solution.py:250
  71.5 12.6 %collective-permute-start.10 = (bf16[5,256,128]{2,1,0:T(8,128)(2,1)S(1)}, bf16[5,256,128]{2,1,0:T(8,128)(2,1)S(1)}, u32[]{:S(2)}, u32[]{:S(2)}) collective-permute-start(bf16[5,256,128]{2,1,0:T(8,128)(2,1)S(1)} %add_convert_fusion.5), channel_id=1, source_target_pairs={{0,2},{2,0},{1,3},{3,1},{4,6},{6,4},{5,7},{7,5},{8,10},{10,8},{9,1... | collective-permute-start | bytes 983048 | tf_op jit(solution)/shard_map/ppermute | solution.py:250
  74.0 10.9 %collective-permute-start.9 = (bf16[10,128,128]{2,1,0:T(8,128)(2,1)S(1)}, bf16[10,128,128]{2,1,0:T(8,128)(2,1)S(1)}, u32[]{:S(2)}, u32[]{:S(2)}) collective-permute-start(bf16[10,128,128]{2,1,0:T(8,128)(2,1)S(1)} %add_convert_fusion.6.refs_4_), channel_id=1, source_target_pairs={{0,96},{32,0},{64,32},{96,64},{1,97},{33,1},{65,33},{97,65},{2,98}... | collective-permute-start | bytes 983048 | tf_op jit(solution)/shard_map/ppermute | solution.py:250
  77.6 7.8 %collective-permute-start.8 = (bf16[10,128,128]{2,1,0:T(8,128)(2,1)S(1)}, bf16[10,128,128]{2,1,0:T(8,128)(2,1)S(1)}, u32[]{:S(2)}, u32[]{:S(2)}) collective-permute-start(bf16[10,128,128]{2,1,0:T(8,128)(2,1)S(1)} %add_convert_fusion.6.refs_4_), channel_id=1, source_target_pairs={{0,64},{32,96},{64,0},{96,32},{1,65},{33,97},{65,1},{97,33},{2,66}... | collective-permute-start | bytes 983048 | tf_op jit(solution)/shard_map/ppermute | solution.py:250
  79.3 15.2 %collective-permute-start.7 = (bf16[10,128,128]{2,1,0:T(8,128)(2,1)S(1)}, bf16[10,128,128]{2,1,0:T(8,128)(2,1)S(1)}, u32[]{:S(2)}, u32[]{:S(2)}) collective-permute-start(bf16[10,128,128]{2,1,0:T(8,128)(2,1)S(1)} %add_convert_fusion.6.refs_4_), channel_id=1, source_target_pairs={{0,32},{32,64},{64,96},{96,0},{1,33},{33,65},{65,97},{97,1},{2,34}... | collective-permute-start | bytes 983048 | tf_op jit(solution)/shard_map/ppermute | solution.py:250
  85.0 13.6 %copy-start.2 = (bf16[10,128,128]{2,1,0:T(8,128)(2,1)}, bf16[10,128,128]{2,1,0:T(8,128)(2,1)S(1)}, u32[]{:S(2)}) copy-start(bf16[10,128,128]{2,1,0:T(8,128)(2,1)S(1)} %collective-permute-done.9.refs_7_) | copy-start | bytes 983044
  85.4 13.3 %copy-start.4 = (bf16[10,128,128]{2,1,0:T(8,128)(2,1)}, bf16[10,128,128]{2,1,0:T(8,128)(2,1)S(1)}, u32[]{:S(2)}) copy-start(bf16[10,128,128]{2,1,0:T(8,128)(2,1)S(1)} %collective-permute-done.8.refs_6_) | copy-start | bytes 983044
  94.5 4.2 %copy-start.6 = (bf16[10,128,128]{2,1,0:T(8,128)(2,1)}, bf16[10,128,128]{2,1,0:T(8,128)(2,1)S(1)}, u32[]{:S(2)}) copy-start(bf16[10,128,128]{2,1,0:T(8,128)(2,1)S(1)} %collective-permute-done.7.refs_5_) | copy-start | bytes 983044
  94.5 10.2 %collective-permute-start.18 = (bf16[20,256,128]{2,1,0:T(8,128)(2,1)S(1)}, bf16[20,256,128]{2,1,0:T(8,128)(2,1)}, u32[]{:S(2)}, u32[]{:S(2)}) collective-permute-start(bf16[20,256,128]{2,1,0:T(8,128)(2,1)S(1)} %all-to-all-done.2.refs_2_), channel_id=1, source_target_pairs={{0,1},{1,0},{2,3},{3,2},{4,5},{5,4},{6,7},{7,6},{8,9},{9,8},{10,11... | collective-permute-start | bytes 3932168 | tf_op jit(solution)/shard_map/ppermute | solution.py:250
  98.6 6.1 %copy-start.8 = (s32[8]{0:T(128)S(1)}, s32[8]{0:T(128)}, u32[]{:S(2)}) copy-start(s32[8]{0:T(128)} %refs_1_.7) | copy-start | bytes 100
  98.6 22.2 %all-to-all-start.3 = ((bf16[20,256,128]{2,1,0:T(8,128)(2,1)}), bf16[20,256,128]{2,1,0:T(8,128)(2,1)S(1)}, u32[]{:S(2)}, u32[]{:S(2)}) async-start(bf16[20,256,128]{2,1,0:T(8,128)(2,1)} %bitcast.6), calls=%async_computation.3 | async-start | bytes 2621440 | tf_op jit(solution)/shard_map/all_to_all | solution.py:262
  102.2 10.4 %collective-permute-start.17 = (bf16[10,128,128]{2,1,0:T(8,128)(2,1)S(1)}, bf16[10,128,128]{2,1,0:T(8,128)(2,1)}, u32[]{:S(2)}, u32[]{:S(2)}) collective-permute-start(bf16[10,128,128]{2,1,0:T(8,128)(2,1)S(1)} %add_convert_fusion.2.refs_4_), channel_id=1, source_target_pairs={{0,96},{32,0},{64,32},{96,64},{1,97},{33,1},{65,33},{97,65},{2,98}... | collective-permute-start | bytes 983048 | tf_op jit(solution)/shard_map/ppermute | solution.py:250
  102.6 10.5 %collective-permute-start.16 = (bf16[10,128,128]{2,1,0:T(8,128)(2,1)S(1)}, bf16[10,128,128]{2,1,0:T(8,128)(2,1)}, u32[]{:S(2)}, u32[]{:S(2)}) collective-permute-start(bf16[10,128,128]{2,1,0:T(8,128)(2,1)S(1)} %add_convert_fusion.2.refs_4_), channel_id=1, source_target_pairs={{0,64},{32,96},{64,0},{96,32},{1,65},{33,97},{65,1},{97,33},{2,66}... | collective-permute-start | bytes 983048 | tf_op jit(solution)/shard_map/ppermute | solution.py:250
  104.2 16.6 %collective-permute-start.15 = (bf16[10,128,128]{2,1,0:T(8,128)(2,1)S(1)}, bf16[10,128,128]{2,1,0:T(8,128)(2,1)}, u32[]{:S(2)}, u32[]{:S(2)}) collective-permute-start(bf16[10,128,128]{2,1,0:T(8,128)(2,1)S(1)} %add_convert_fusion.2.refs_4_), channel_id=1, source_target_pairs={{0,32},{32,64},{64,96},{96,0},{1,33},{33,65},{65,97},{97,1},{2,34}... | collective-permute-start | bytes 983048 | tf_op jit(solution)/shard_map/ppermute | solution.py:250
  120.9 3.2 %collective-permute-start.19 = (bf16[20,256,128]{2,1,0:T(8,128)(2,1)S(1)}, bf16[20,256,128]{2,1,0:T(8,128)(2,1)S(1)}, u32[]{:S(2)}, u32[]{:S(2)}) collective-permute-start(bf16[20,256,128]{2,1,0:T(8,128)(2,1)S(1)} %all-to-all-done.3.refs_2_), channel_id=1, source_target_pairs={{0,1},{1,0},{2,3},{3,2},{4,5},{5,4},{6,7},{7,6},{8,9},{9,8},{10,11... | collective-permute-start | bytes 3932168 | tf_op jit(solution)/shard_map/ppermute | solution.py:250
  (5 other events, 5.1 us)
